TPU v7x, 32 devices: a whole 2x2x4 slice. The times are simulated.
32 devices in a mesh: groups: 2 (over y), wide: 16 (over z, x, core).
Axes of the slice: x: 2, y: 2, z: 4, core: 2. Of those that a mesh axis runs over, the one named last changes fastest.
Arguments:
- features: bfloat16 [4096, 8192], P(('groups', 'wide')), parts along dimension 0, may hold values from -6 to 6
- cotangent: bfloat16 [4096, 1024], P(('groups', 'wide')), parts along dimension 0, may hold values from -6 to 6
- frozen_key_weight: bfloat16 [8192, 1024], P('wide'), may hold values from -0.0625 to 0.0625
- adapter_down_weight: bfloat16 [32, 8192, 64], P(('groups', 'wide')), parts along dimension 0, may hold values from -0.0625 to 0.0625
- adapter_up_weight: bfloat16 [32, 64, 1024], P(('groups', 'wide')), parts along dimension 0, may hold values from -0.75 to 0.75
- row_adapter_index: int32 [4096, 1], P(('groups', 'wide')), parts along dimension 0, may hold values from 0 to 15; in each aligned block of 128 rows (0 to 127, 128 to 255, ...) at most 16 rows name the same one
- device_adapter: int32 [32], P('groups'), parts along dimension 0, may hold values from 0 to 15, each once
Outputs:
- input_grad: bfloat16 [4096, 8192], P(('groups', 'wide')), parts along dimension 0
- grad_down: float32 [32, 8192, 64], P(('groups', 'wide')), parts along dimension 0
- grad_up: float32 [32, 64, 1024], P(('groups', 'wide')), parts along dimension 0
There are 2 independent parts, one for each index of `groups`. A program takes and returns all parts, laid end to end along the dimension named above; an argument that names none is the same for every part. Nothing has to cross between parts.
Inputs may be any that keep to these rules, and one draw needn't show every extreme that they name: `row_adapter_index`: no adapter is named by more than 16 rows of one device, and on every draw some adapter is named by exactly 16 rows of some device. `device_adapter`: each adapter is held by exactly one device.
All inputs are finite; a program needn't handle non-finite values.
Results may differ from a plain program's by a relative error of at most 0.0056.
Values may be sent and summed in bfloat16 or wider, within the bound.
No kernel may reach another device: no remote copies, remote signals or barrier semaphores. Data moves between devices by JAX's collectives and lax.ppermute only.
A program may use at most 128 MiB of HBM per device.

v0:
```python
import jax
import jax.numpy as jnp
from jax import lax
from jax.sharding import PartitionSpec as P

adapter_scale = 2.0


def contract_matrices(left, right, left_dim, right_dim):
    return lax.dot_general(
        left, right, (((left_dim,), (right_dim,)), ((), ())), preferred_element_type=jnp.float32
    )


def frozen_part(cotangent, frozen_key_weight):
    return contract_matrices(
        cotangent, lax.all_gather(frozen_key_weight, "wide", axis=0, tiled=True), 1, 1
    )


def body(
    features,
    cotangent,
    frozen_key_weight,
    adapter_down_weight,
    adapter_up_weight,
    row_adapter_index,
    device_adapter,
):
    row_count = features.shape[0]
    peer_count = lax.axis_size("wide")
    device_index = lax.axis_index("wide")
    capacity = max(2, 2 * row_count // peer_count)
    slot_range = jnp.arange(peer_count, dtype=jnp.int32)
    matches = row_adapter_index[:, 0][:, None] == device_adapter[None, :]
    token_slot = jnp.sum(jnp.where(matches, slot_range[None, :], 0), axis=1)
    slot_hit = (token_slot[:, None] == slot_range[None, :]).astype(jnp.int32)
    local_counts = jnp.sum(slot_hit, axis=0)
    token_counts = lax.psum(local_counts, "wide")
    earlier = jnp.cumsum(slot_hit, axis=0) - slot_hit
    token_rank = jnp.sum(earlier * slot_hit, axis=1)
    position = token_slot * capacity + token_rank
    slot_total = peer_count * capacity
    pick = position[None, :] == jnp.arange(slot_total, dtype=jnp.int32)[:, None]
    source_row = jnp.sum(
        jnp.where(pick, jnp.arange(row_count, dtype=jnp.int32)[None, :], 0), axis=1
    )
    filled = jnp.any(pick, axis=1)
    zero_value = jnp.zeros((), jnp.bfloat16)
    send_in = jnp.where(filled[:, None], features[source_row], zero_value).reshape(
        peer_count, capacity, -1
    )
    send_cot = jnp.where(filled[:, None], cotangent[source_row], zero_value).reshape(
        peer_count, capacity, -1
    )
    recv_in, recv_cot = (
        lax.all_to_all(send_in, "wide", split_axis=0, concat_axis=0, tiled=True),
        lax.all_to_all(send_cot, "wide", split_axis=0, concat_axis=0, tiled=True),
    )
    recv_in = recv_in.reshape(slot_total, -1)
    recv_cot = recv_cot.reshape(slot_total, -1)
    down_projection = adapter_down_weight[0]
    up_projection = adapter_up_weight[0]
    low_in = jnp.dot(recv_in, down_projection, preferred_element_type=jnp.float32).astype(
        jnp.bfloat16
    )
    low_rank_output = contract_matrices(recv_cot, up_projection, 1, 1).astype(jnp.bfloat16)
    rows_per_adapter = (
        adapter_scale * contract_matrices(low_rank_output, down_projection, 1, 1)
    ).astype(jnp.bfloat16)
    inverse_permutation = adapter_scale / jnp.maximum(token_counts[device_index], 1).astype(
        jnp.float32
    )
    grad_down = inverse_permutation * contract_matrices(recv_in, low_rank_output, 0, 0)
    grad_up = inverse_permutation * contract_matrices(low_in, recv_cot, 0, 0)
    returned = lax.all_to_all(
        rows_per_adapter.reshape(peer_count, capacity, -1),
        "wide",
        split_axis=0,
        concat_axis=0,
        tiled=True,
    )
    returned = returned.reshape(slot_total, -1)
    adapter_grad = returned[position]
    base_grad = frozen_part(cotangent, frozen_key_weight)
    input_grad = (base_grad + adapter_grad.astype(jnp.float32)).astype(jnp.bfloat16)
    return (input_grad, grad_down[None], grad_up[None])


def solution(mesh):
    in_specs = (
        P(("groups", "wide"), None),
        P(("groups", "wide"), None),
        P("wide", None),
        P(("groups", "wide"), None, None),
        P(("groups", "wide"), None, None),
        P(("groups", "wide"), None),
        P("groups"),
    )
    out_specs = (
        P(("groups", "wide"), None),
        P(("groups", "wide"), None, None),
        P(("groups", "wide"), None, None),
    )
    return jax.shard_map(body, mesh=mesh, in_specs=in_specs, out_specs=out_specs, check_vma=False)
```

profile of v0, /device:TPU:11, one launch (start us, length us, event | category | flops | bytes accessed | tf_op | source)
XLA Modules:
  0.0 356.6 jit_solution(18134211121607654804)
XLA Ops:
  7.2 0.0 copy-start
  7.2 0.0 copy-start.1
  7.2 0.0 all-gather.2.cloned.1.call-start
  7.2 0.7 all-gather.2.cloned.1.call-update
  7.9 0.8 select_reduce_fusion.2
  8.8 0.1 fusion.10
  8.9 0.2 reduce_window_sum.11
  9.0 0.2 fusion.11
  9.2 0.1 fusion.9
  9.4 0.1 broadcast_in_dim.73
  9.4 0.1 select_reduce_fusion
  9.6 0.0 copy-done.1
  9.6 1.2 gather_fusion
  10.8 0.9 broadcast_select_fusion.1
  11.7 6.6 %all-to-all-start = ((bf16[16,16,1024]{2,1,0:T(8,128)(2,1)}), bf16[16,16,1024]{2,1,0:T(8,128)(2,1)S(1)}, u32[]{:S(2)}, u32[]{:S(2)}) async-start(bf16[16,16,1024]{2,1,0:T(8,128)(2,1)} %broadcast_select_fusion.1), calls=%async_computation | async-start | bytes 1048576 | tf_op jit(solution)/shard_map/all_to_all | solution.py:58
  18.2 0.0 copy-done
  18.2 5.1 %gather_fusion.2 = bf16[256,8192]{1,0:T(8,128)(2,1)} fusion(bf16[128,8192]{1,0:T(8,128)(2,1)S(1)} %copy-done, s32[1024]{0:T(1024)S(1)} %pad_clamp_fusion.1), kind=kCustom, calls=%fused_computation.2 | custom fusion | bytes 8389632 | tf_op jit(solution)/shard_map/gather | solution.py:50
  23.4 4.5 %broadcast_select_fusion = bf16[16,16,8192]{2,1,0:T(8,128)(2,1)} fusion(bf16[16,16,8192]{2,1,0:T(8,128)(2,1)} %bitcast.37, pred[16,16]{1,0:T(8,128)(4,1)S(1)} %broadcast_in_dim.73), kind=kLoop, calls=%fused_computation.9 | loop fusion | flops 2097152 | bytes 8388864 | tf_op jit(solution)/shard_map/jit(_where)/select_n | solution.py:50
  27.9 0.0 copy-start.2
  27.9 16.5 %all-to-all-done = bf16[16,16,1024]{2,1,0:T(8,128)(2,1)S(1)} async-done(((bf16[16,16,1024]{2,1,0:T(8,128)(2,1)}), bf16[16,16,1024]{2,1,0:T(8,128)(2,1)S(1)}, u32[]{:S(2)}, u32[]{:S(2)}) %all-to-all-start) | async-done | bytes 524320 | tf_op jit(solution)/shard_map/all_to_all | solution.py:58
  44.3 5.8 %all-to-all-start.2 = ((bf16[16,16,8192]{2,1,0:T(8,128)(2,1)}), bf16[16,16,8192]{2,1,0:T(8,128)(2,1)}, u32[]{:S(2)}, u32[]{:S(2)}) async-start(bf16[16,16,8192]{2,1,0:T(8,128)(2,1)} %broadcast_select_fusion), calls=%async_computation.2 | async-start | bytes 8388608 | tf_op jit(solution)/shard_map/all_to_all | solution.py:57
  50.1 0.0 copy-done.2
  50.1 0.3 convolution_convert_fusion.1
  50.4 4.5 %fusion = bf16[256,8192]{1,0:T(8,128)(2,1)} fusion(bf16[256,64]{0,1:T(8,128)(2,1)S(1)} %convolution_convert_fusion.1, bf16[1,8192,64]{1,2,0:T(8,128)(2,1)} %param.10), kind=kOutput, calls=%fused_computation.4 | convolution fusion | flops 272629760 | bytes 5275648 | tf_op jit(solution)/shard_map/dot_general | solution.py:10
  54.9 168.6 %all-to-all-done.2 = bf16[16,16,8192]{2,1,0:T(8,128)(2,1)} async-done(((bf16[16,16,8192]{2,1,0:T(8,128)(2,1)}), bf16[16,16,8192]{2,1,0:T(8,128)(2,1)}, u32[]{:S(2)}, u32[]{:S(2)}) %all-to-all-start.2) | async-done | bytes 4194336 | tf_op jit(solution)/shard_map/all_to_all | solution.py:57
  223.5 4.4 %all-to-all-start.1 = ((bf16[16,16,8192]{2,1,0:T(8,128)(2,1)}), bf16[16,16,8192]{2,1,0:T(8,128)(2,1)}, u32[]{:S(2)}, u32[]{:S(2)}) async-start(bf16[16,16,8192]{2,1,0:T(8,128)(2,1)} %bitcast.36), calls=%async_computation.1 | async-start | bytes 8388608 | tf_op jit(solution)/shard_map/all_to_all | solution.py:76
  227.9 90.1 %psum.7 = s32[16]{0:T(128)S(1)} all-reduce(s32[16]{0:T(128)S(1)} %get-tuple-element.3), channel_id=1, replica_groups=mesh['groups'=2,'wide'=16] {'wide'}, use_global_device_ids=true, to_apply=%region_6.7 | all-reduce | flops 16 | bytes 128 | tf_op jit(solution)/shard_map/psum | solution.py:39
  318.1 0.6 dynamic_slice.3
  319.4 4.4 %fusion.2 = f32[1,8192,64]{1,2,0:T(8,128)} fusion(bf16[256,64]{0,1:T(8,128)(2,1)S(1)} %convolution_convert_fusion.1, bf16[256,8192]{1,0:T(8,128)(2,1)} %bitcast.13, f32[]{:T(128)} %bitcast.11), kind=kOutput, calls=%fused_computation.8 | convolution fusion | flops 268959744 | bytes 6324228 | tf_op jit(solution)/shard_map/dot_general | solution.py:10
  323.7 4.9 %fusion.3 = f32[1,64,1024]{2,1,0:T(8,128)} fusion(bf16[256,1024]{1,0:T(8,128)(2,1)S(1)} %bitcast.39, bf16[256,8192]{1,0:T(8,128)(2,1)} %bitcast.13, bf16[1,8192,64]{1,2,0:T(8,128)(2,1)} %param.10, f32[]{:T(128)} %bitcast.11), kind=kOutput, calls=%fused_computation.11 | convolution fusion | flops 302071808 | bytes 6029316 | tf_op jit(solution)/shard_map/dot_general | solution.py:10
  328.6 0.0 all-to-all-done.1
  328.6 7.8 %gather_fusion.1 = bf16[128,8192]{1,0:T(8,128)(2,1)} fusion(bf16[256,8192]{1,0:T(8,128)(2,1)} %bitcast.8, s32[1024]{0:T(1024)S(1)} %pad_clamp_fusion), kind=kCustom, calls=%fused_computation.1 | custom fusion | bytes 4194816 | tf_op jit(solution)/shard_map/gather | solution.py:84
  336.4 0.0 all-gather.2.cloned.1.call-done
  336.4 13.3 %fusion.1 = bf16[128,8192]{1,0:T(8,128)(2,1)} fusion(bf16[128,1024]{1,0:T(8,128)(2,1)S(1)} %copy-done.1, bf16[8192,1024]{1,0:T(8,128)(2,1)} %all-gather.2.cloned.1.call-done, bf16[128,8192]{1,0:T(8,128)(2,1)} %gather_fusion.1), kind=kOutput, calls=%fused_computation.6 | convolution fusion | flops 2150629376 | bytes 21233664 | tf_op jit(solution)/shard_map/dot_general | solution.py:10
  (4 shorter events, 0.0 us)
Async XLA Ops:
  7.2 11.1 %copy-start = (bf16[128,8192]{1,0:T(8,128)(2,1)S(1)}, bf16[128,8192]{1,0:T(8,128)(2,1)}, u32[]{:S(2)}) copy-start(bf16[128,8192]{1,0:T(8,128)(2,1)} %param.7) | copy-start | bytes 6291460
  7.2 2.4 copy-start.1
  7.2 329.2 %all-gather.2.cloned.1.call-start = ((), (), s32[]{:S(2)}) async-start(), calls=%async_computation.3 | async-start | bytes 17825792 | tf_op jit(solution)/shard_map/all_gather | solution.py:17
  11.7 32.7 %all-to-all-start = ((bf16[16,16,1024]{2,1,0:T(8,128)(2,1)}), bf16[16,16,1024]{2,1,0:T(8,128)(2,1)S(1)}, u32[]{:S(2)}, u32[]{:S(2)}) async-start(bf16[16,16,1024]{2,1,0:T(8,128)(2,1)} %broadcast_select_fusion.1), calls=%async_computation | async-start | bytes 1048576 | tf_op jit(solution)/shard_map/all_to_all | solution.py:58
  27.9 22.3 %copy-start.2 = (bf16[1,64,1024]{2,1,0:T(8,128)(2,1)S(1)}, bf16[1,64,1024]{2,1,0:T(8,128)(2,1)}, u32[]{:S(2)}) copy-start(bf16[1,64,1024]{2,1,0:T(8,128)(2,1)} %param.11) | copy-start | bytes 393220
  44.3 179.1 %all-to-all-start.2 = ((bf16[16,16,8192]{2,1,0:T(8,128)(2,1)}), bf16[16,16,8192]{2,1,0:T(8,128)(2,1)}, u32[]{:S(2)}, u32[]{:S(2)}) async-start(bf16[16,16,8192]{2,1,0:T(8,128)(2,1)} %broadcast_select_fusion), calls=%async_computation.2 | async-start | bytes 8388608 | tf_op jit(solution)/shard_map/all_to_all | solution.py:57
  223.5 105.1 %all-to-all-start.1 = ((bf16[16,16,8192]{2,1,0:T(8,128)(2,1)}), bf16[16,16,8192]{2,1,0:T(8,128)(2,1)}, u32[]{:S(2)}, u32[]{:S(2)}) async-start(bf16[16,16,8192]{2,1,0:T(8,128)(2,1)} %bitcast.36), calls=%async_computation.1 | async-start | bytes 8388608 | tf_op jit(solution)/shard_map/all_to_all | solution.py:76
Sparse Core Ops, SparseCore 0:
  10.2 211.2 all-gather.1
where the time goes:
time: 362 us; the launch traced here: 357 us
  waiting for transfers between devices  186 us (51%)
  blocking collectives  90.1 us (25%)
  matrix products  27.3 us (8%)
  starting transfers between devices  16.8 us (5%)
  local copies, waits for them, and re-layouts  14.8 us (4%)
  between operations  14.8 us (4%)
  other arithmetic  6.96 us (2%)
    all_to_all x1, waiting for transfers between devices, body(): lax.all_to_all(send_in, 'wide', split_axis=0, concat_axis=0, tiled=True)  169 us
    psum x1, blocking collectives, body(): token_counts = lax.psum(local_counts, 'wide')  90.1 us
    dot_general x5, matrix products, contract_matrices(): lax.dot_general(left, right, (((left_dim,), (right_dim,)), ((), ())), pre...  27.3 us
    all_to_all x1, waiting for transfers between devices, body(): lax.all_to_all(send_cot, 'wide', split_axis=0, concat_axis=0, tiled=True)  16.5 us
    gather x1, local copies, waits for them, and re-layouts, body(): adapter_grad = returned[position]  7.81 us
  transfers between devices with their start and end apart: 4, of which 2 were waited for; matrix products, arithmetic and copies ran while one was open for 10% of the time, Pallas kernels for 0%

commit v1 on v0

--- a/solution.py
+++ b/solution.py
@@ -1,9 +1,15 @@
 import jax
 import jax.numpy as jnp
 from jax import lax
+from jax.experimental import pallas as pl
+from jax.experimental.pallas import tpu as pltpu
 from jax.sharding import PartitionSpec as P
 
 adapter_scale = 2.0
+LANES = 128
+INDEX_ROWS = 16
+STEP = 4
+VMEM_BYTES = 40 * 1024 * 1024
 
 
 def contract_matrices(left, right, left_dim, right_dim):
@@ -18,7 +24,7 @@
     )
 
 
-def body(
+def dispatch_body(
     features,
     cotangent,
     frozen_key_weight,
@@ -87,6 +93,241 @@
     return (input_grad, grad_down[None], grad_up[None])
 
 
+def params():
+    return pltpu.CompilerParams(vmem_limit_bytes=VMEM_BYTES)
+
+
+def index_columns(packed):
+    values = packed.astype(jnp.float32)
+    chunks = packed.shape[2] // LANES
+    return jnp.concatenate(
+        [
+            values[item, :, j * LANES : (j + 1) * LANES]
+            for item in range(packed.shape[0])
+            for j in range(chunks)
+        ],
+        axis=0,
+    )
+
+
+def pack_kernel(features_ref, down_ref, out_ref):
+    rows = features_ref.shape[0]
+    out_ref[0, :rows, :] = features_ref[...]
+    out_ref[0, rows:, :] = down_ref[...]
+
+
+def pack_columns(features, down, peer_count):
+    rows, width = features.shape
+    rank = down.shape[0]
+    share = width // peer_count
+    return pl.pallas_call(
+        pack_kernel,
+        grid=(peer_count,),
+        in_specs=[
+            pl.BlockSpec((rows, share), lambda d: (0, d)),
+            pl.BlockSpec((rank, share), lambda d: (0, d)),
+        ],
+        out_specs=pl.BlockSpec((1, rows + rank, share), lambda d: (d, 0, 0)),
+        out_shape=jax.ShapeDtypeStruct((peer_count, rows + rank, share), jnp.bfloat16),
+        compiler_params=params(),
+        cost_estimate=pl.CostEstimate(flops=0, bytes_accessed=6 << 20, transcendentals=0),
+    )(features, down)
+
+
+def low_out_kernel(cot_ref, up_ref, index_ref, weight_ref, ids_ref, low_ref, base_ref):
+    keys = cot_ref.shape[2]
+    cot = cot_ref[...].reshape(-1, keys)
+    up = up_ref[...].reshape(-1, keys)
+    low = contract_matrices(cot, up, 1, 1)
+    column = index_columns(index_ref[...])
+    for j in range(low.shape[1] // LANES):
+        span = slice(j * LANES, (j + 1) * LANES)
+        low_ref[:, span] = jnp.where(column == ids_ref[:, span], low[:, span], 0.0).astype(
+            jnp.bfloat16
+        )
+    base_ref[...] = contract_matrices(cot, weight_ref[...], 1, 1)
+
+
+def low_out(gathered, weight, ids, rows, rank):
+    peer_count, _, keys = gathered.shape
+    share = weight.shape[0]
+    block = STEP * rows
+    slots = peer_count * rank
+    return pl.pallas_call(
+        low_out_kernel,
+        grid=(peer_count // STEP,),
+        in_specs=[
+            pl.BlockSpec((STEP, rows, keys), lambda s: (s, 0, 0)),
+            pl.BlockSpec((peer_count, rank, keys), lambda s: (0, rows // rank, 0)),
+            pl.BlockSpec(
+                (STEP, INDEX_ROWS, keys), lambda s: (s, (rows + rank) // INDEX_ROWS, 0)
+            ),
+            pl.BlockSpec((share, keys), lambda s: (0, 0)),
+            pl.BlockSpec((1, slots), lambda s: (0, 0)),
+        ],
+        out_specs=[
+            pl.BlockSpec((block, slots), lambda s: (s, 0)),
+            pl.BlockSpec((block, share), lambda s: (s, 0)),
+        ],
+        out_shape=[
+            jax.ShapeDtypeStruct((peer_count * rows, slots), jnp.bfloat16),
+            jax.ShapeDtypeStruct((peer_count * rows, share), jnp.float32),
+        ],
+        compiler_params=params(),
+        cost_estimate=pl.CostEstimate(flops=7 << 30, bytes_accessed=16 << 20, transcendentals=0),
+    )(gathered, gathered, gathered, weight, ids)
+
+
+def share_kernel(feat_ref, down_ref, index_ref, low_ref, base_ref, ids_ref, out_ref):
+    items, rows, share = feat_ref.shape
+    down = down_ref[...].reshape(-1, share)
+    grad = base_ref[...] + adapter_scale * contract_matrices(low_ref[...], down, 1, 0)
+    out_ref[:, :rows, :] = grad.astype(jnp.bfloat16).reshape(items, rows, share)
+    partial = contract_matrices(feat_ref[...].reshape(-1, share), down, 1, 1)
+    column = index_columns(index_ref[...])
+    total = jnp.zeros_like(column)
+    for j in range(partial.shape[1] // LANES):
+        span = slice(j * LANES, (j + 1) * LANES)
+        total = total + jnp.where(column == ids_ref[:, span], partial[:, span], 0.0)
+    total = total + pltpu.roll(total, LANES // 2, 1)
+    left = lax.broadcasted_iota(jnp.int32, (INDEX_ROWS, LANES), 1) < LANES // 2
+    for item in range(items):
+        for j in range(rows // (2 * INDEX_ROWS)):
+            first = item * rows + 2 * INDEX_ROWS * j
+            middle = first + INDEX_ROWS
+            pair = jnp.where(
+                left, total[first:middle, :], total[middle : middle + INDEX_ROWS, :]
+            )
+            out_ref[item, rows:, j * LANES : (j + 1) * LANES] = pair.astype(jnp.bfloat16)
+
+
+def share_results(received, gathered, low, base, ids, rows, rank):
+    peer_count, _, share = received.shape
+    keys = gathered.shape[2]
+    block = STEP * rows
+    slots = peer_count * rank
+    return pl.pallas_call(
+        share_kernel,
+        grid=(peer_count // STEP,),
+        in_specs=[
+            pl.BlockSpec((STEP, rows, share), lambda s: (s, 0, 0)),
+            pl.BlockSpec((peer_count, rank, share), lambda s: (0, rows // rank, 0)),
+            pl.BlockSpec(
+                (STEP, INDEX_ROWS, keys), lambda s: (s, (rows + rank) // INDEX_ROWS, 0)
+            ),
+            pl.BlockSpec((block, slots), lambda s: (s, 0)),
+            pl.BlockSpec((block, share), lambda s: (s, 0)),
+            pl.BlockSpec((1, slots), lambda s: (0, 0)),
+        ],
+        out_specs=pl.BlockSpec((STEP, rows + INDEX_ROWS, share), lambda s: (s, 0, 0)),
+        out_shape=jax.ShapeDtypeStruct((peer_count, rows + INDEX_ROWS, share), jnp.bfloat16),
+        compiler_params=params(),
+        cost_estimate=pl.CostEstimate(flops=4 << 30, bytes_accessed=16 << 20, transcendentals=0),
+    )(received, received, gathered, low, base, ids)
+
+
+def finish_kernel(down_ref, low_ref, cot_ref, index_ref, own_ref, scale_ref, gd_ref, gu_ref, acc):
+    step = pl.program_id(0)
+    items, rank, share = down_ref.shape
+    keys = cot_ref.shape[2]
+    scale = scale_ref[0, 0]
+    for item in range(items):
+        gd_ref[:, item * share : (item + 1) * share] = scale * down_ref[item].astype(jnp.float32)
+    pieces = []
+    for item in range(items):
+        for j in range(share // LANES):
+            pair = low_ref[item, :, j * LANES : (j + 1) * LANES].astype(jnp.float32)
+            pieces += [pair, pltpu.roll(pair, LANES // 2, 1)]
+    low = jnp.concatenate(pieces, axis=0)
+    column = index_columns(index_ref[...])
+    low = jnp.where(column == own_ref[...], low, 0.0).astype(jnp.bfloat16)
+    term = contract_matrices(low, cot_ref[...].reshape(-1, keys), 0, 0)
+
+    @pl.when(step == 0)
+    def _():
+        acc[...] = jnp.zeros_like(acc)
+
+    acc[...] += term
+
+    @pl.when(step == pl.num_programs(0) - 1)
+    def _():
+        gu_ref[...] = scale * acc[:rank, :]
+
+
+def finish(received, gathered, own, scale, rows, rank):
+    peer_count, _, share = received.shape
+    keys = gathered.shape[2]
+    return pl.pallas_call(
+        finish_kernel,
+        grid=(peer_count // STEP,),
+        in_specs=[
+            pl.BlockSpec((STEP, rank, share), lambda s: (s, 0, 0)),
+            pl.BlockSpec((STEP, INDEX_ROWS, share), lambda s: (s, rank // INDEX_ROWS, 0)),
+            pl.BlockSpec((STEP, rows, keys), lambda s: (s, 0, 0)),
+            pl.BlockSpec(
+                (STEP, INDEX_ROWS, keys), lambda s: (s, (rows + rank) // INDEX_ROWS, 0)
+            ),
+            pl.BlockSpec((1, LANES), lambda s: (0, 0)),
+            pl.BlockSpec((1, LANES), lambda s: (0, 0)),
+        ],
+        out_specs=[
+            pl.BlockSpec((rank, STEP * share), lambda s: (0, s)),
+            pl.BlockSpec((rank, keys), lambda s: (0, 0)),
+        ],
+        out_shape=[
+            jax.ShapeDtypeStruct((rank, peer_count * share), jnp.float32),
+            jax.ShapeDtypeStruct((rank, keys), jnp.float32),
+        ],
+        scratch_shapes=[pltpu.VMEM((LANES, keys), jnp.float32)],
+        compiler_params=params(),
+        cost_estimate=pl.CostEstimate(flops=1 << 29, bytes_accessed=8 << 20, transcendentals=0),
+    )(received, received, gathered, gathered, own, scale)
+
+
+def exchange(block):
+    return lax.all_to_all(block, "wide", split_axis=0, concat_axis=0, tiled=True)
+
+
+def column_body(
+    features,
+    cotangent,
+    frozen_key_weight,
+    adapter_down_weight,
+    adapter_up_weight,
+    row_adapter_index,
+    device_adapter,
+):
+    rows, width = features.shape
+    keys = cotangent.shape[1]
+    rank = adapter_up_weight.shape[1]
+    peer_count = lax.axis_size("wide")
+    share = width // peer_count
+    down = adapter_down_weight[0].T
+    marks = jnp.broadcast_to(row_adapter_index.astype(jnp.bfloat16), (rows, LANES))
+    marks = marks.reshape(rows // INDEX_ROWS, INDEX_ROWS, LANES).transpose(1, 0, 2)
+    marks = marks.reshape(INDEX_ROWS, keys)
+    payload = jnp.concatenate([cotangent, adapter_up_weight[0], marks], axis=0)
+    gathered = lax.all_gather(payload, "wide", axis=0)
+    received = exchange(pack_columns(features, down, peer_count))
+    ids = jnp.repeat(device_adapter, rank)[None, :].astype(jnp.float32)
+    low, base = low_out(gathered, frozen_key_weight, ids, rows, rank)
+    results = exchange(share_results(received, gathered, low, base, ids, rows, rank))
+    down_blocks = contract_matrices(low, received[:, :rows].reshape(-1, share), 0, 0)
+    down_blocks = down_blocks.astype(jnp.bfloat16).reshape(peer_count, rank, share)
+    low_in = jnp.sum(results[:, rows:].astype(jnp.float32), axis=0).astype(jnp.bfloat16)
+    low_in = jnp.broadcast_to(low_in[None], (peer_count, INDEX_ROWS, share))
+    last = exchange(jnp.concatenate([down_blocks, low_in], axis=1))
+    input_grad = results[:, :rows].transpose(1, 0, 2).reshape(rows, width)
+    own = device_adapter[lax.axis_index("wide")].astype(jnp.float32)
+    hits = gathered[:, rows + rank :, :].astype(jnp.float32) == own
+    count = jnp.sum(hits.astype(jnp.float32)) / LANES
+    scale = jnp.full((1, LANES), adapter_scale, jnp.float32) / jnp.maximum(count, 1.0)
+    grad_down, grad_up = finish(
+        last, gathered, jnp.full((1, LANES), own, jnp.float32), scale, rows, rank
+    )
+    return (input_grad, grad_down.T[None], grad_up[None])
+
+
 def solution(mesh):
     in_specs = (
         P(("groups", "wide"), None),
@@ -102,4 +343,20 @@
         P(("groups", "wide"), None, None),
         P(("groups", "wide"), None, None),
     )
+
+    def body(*arrays):
+        rows, width = arrays[0].shape
+        keys = arrays[1].shape[1]
+        rank = arrays[4].shape[1]
+        peer_count = mesh.shape["wide"]
+        by_columns = (
+            peer_count % STEP == 0
+            and peer_count * rank <= keys
+            and rank * 2 == LANES
+            and rows == LANES
+            and rows // INDEX_ROWS * LANES == keys
+            and rows * rank == INDEX_ROWS * (width // peer_count)
+        )
+        return (column_body if by_columns else dispatch_body)(*arrays)
+
     return jax.shard_map(body, mesh=mesh, in_specs=in_specs, out_specs=out_specs, check_vma=False)

time: 362 us -> 264 us (0.73); the launches traced: 357 us -> 263 us
  blocking collectives: 90.1 us -> 0 us
  matrix products: 27.3 us -> 2.35 us
  Pallas kernels: 0 us -> 20 us
  waiting for transfers between devices: 186 us -> 169 us
  local copies, waits for them, and re-layouts: 14.8 us -> 29.9 us
  starting transfers between devices: 16.8 us -> 20.5 us
    all_to_all x3, waiting for transfers between devices: 185 us -> 67.1 us  [exchange(): lax.all_to_all(block, 'wide', split_axis=0, concat_axis=0, tiled=True)]
    all_gather x1, waiting for transfers between devices: 0.01 us -> 102 us  [column_body(): gathered = lax.all_gather(payload, 'wide', axis=0)]
    psum x1 -> x0, blocking collectives: 90.1 us -> none  [body(): token_counts = lax.psum(local_counts, 'wide')]
    dot_general x5 -> x1, matrix products: 27.3 us -> 2.35 us  [contract_matrices(): lax.dot_general(left, right, (((left_dim,), (right_dim,)), ((), ())), pre...]
    unnamed x6 -> x26, local copies, waits for them, and re-layouts: 0.02 us -> 24.5 us
    pallas_call x0 -> x4, Pallas kernels: none -> 20 us  [the longest x1 9.38 us: low_out(): pl.pallas_call(low_out_kernel, grid=(peer_count // STEP,), in_specs=[pl.B...]
    gather x3 -> x0, local copies, waits for them, and re-layouts: 14.1 us -> none  [the longest x1 7.81 us: body(): adapter_grad = returned[position]]
    select_n x4 -> x0, other arithmetic: 5.42 us -> none  [the longest x1 4.5 us: body(): jnp.where(filled[:, None], features[source_row], zero_value)]
  transfers between devices with their start and end apart: 4 -> 4, of which waited for: 2 -> 3; matrix products, arithmetic and copies ran while one was open for 10% -> 5% of each run, Pallas kernels for 0% -> 4%
where the time goes in v1:
time: 264 us; the launch traced here: 263 us
  waiting for transfers between devices  169 us (64%)
  local copies, waits for them, and re-layouts  29.9 us (11%)
  starting transfers between devices  20.5 us (8%)
  Pallas kernels  20 us (8%)
  between operations  15.5 us (6%)
  other arithmetic  6.59 us (2%)
    all_gather x1, waiting for transfers between devices, column_body(): gathered = lax.all_gather(payload, 'wide', axis=0)  102 us
    all_to_all x3, waiting for transfers between devices, exchange(): lax.all_to_all(block, 'wide', split_axis=0, concat_axis=0, tiled=True)  67.1 us
    unnamed x26, local copies, waits for them, and re-layouts  24.5 us
    all_to_all x3, starting transfers between devices, exchange(): lax.all_to_all(block, 'wide', split_axis=0, concat_axis=0, tiled=True)  20.4 us
    pallas_call x1, Pallas kernels, low_out(): pl.pallas_call(low_out_kernel, grid=(peer_count // STEP,), in_specs=[pl.B...  9.38 us
    pallas_call x1, Pallas kernels, share_results(): pl.pallas_call(share_kernel, grid=(peer_count // STEP,), in_specs=[pl.Blo...  6.4 us
  transfers between devices with their start and end apart: 4, of which 3 were waited for; matrix products, arithmetic and copies ran while one was open for 5% of the time, Pallas kernels for 4%

profile of v1, /device:TPU:11, one launch (start us, length us, event | category | flops | bytes accessed | tf_op | source)
XLA Modules:
  0.0 263.4 jit_solution(9630744194285349024)
XLA Ops:
  7.2 0.0 all-gather.3.cloned.1.call-start
  7.2 0.7 convert_reduce_fusion.1
  7.9 0.1 broadcast_in_dim.28
  8.0 0.1 copy.11
  8.1 0.1 broadcast_in_dim.29
  8.2 1.8 pad_maximum_fusion.1
  10.0 0.0 all-gather.3.cloned.1.call-update
  10.0 0.0 copy-start.8
  10.0 1.6 copy-done.8
  11.6 0.0 copy-start.9
  11.6 1.2 copy-done.9
  12.8 0.8 shard_map.94
  13.6 0.0 copy-start.1
  13.6 1.6 copy-done.1
  15.2 0.0 copy-start.11
  15.2 6.7 %all-to-all-start = ((bf16[16,192,512]{2,1,0:T(8,128)(2,1)}), bf16[16,192,512]{2,1,0:T(8,128)(2,1)S(1)}, u32[]{:S(2)}, u32[]{:S(2)}) async-start(bf16[16,192,512]{2,1,0:T(8,128)(2,1)} %copy-done.1), calls=%async_computation | async-start | bytes 6291456 | tf_op jit(solution)/shard_map/all_to_all | solution.py:288
  21.9 0.0 copy-done.11
  21.9 0.1 broadcast_in_dim.30
  22.0 0.1 convert_element_type.27.ids_ref
  22.1 101.5 %all-gather.3.cloned.1.call-done = bf16[3328,1024]{1,0:T(8,128)(2,1)} async-done(((bf16[208,1024]{1,0:T(8,128)(2,1)}), bf16[3328,1024]{1,0:T(8,128)(2,1)}) %all-gather.3.cloned.1.call-update) | async-done | bytes 6815760 | tf_op jit(solution)/shard_map/all_gather | solution.py:310
  123.6 0.0 copy-start.10
  123.6 1.2 copy-done.10
  124.8 9.4 %shard_map.95 = (bf16[2048,1024]{1,0:T(8,128)(2,1)S(1)}, f32[2048,512]{1,0:T(8,128)S(1)}) custom-call(bf16[16,208,1024]{2,1,0:T(8,128)(2,1)} %bitcast.22, bf16[16,208,1024]{2,1,0:T(8,128)(2,1)} %bitcast.23, bf16[16,208,1024]{2,1,0:T(8,128)(2,1)} %bitcast.24, bf16[512,1024]{1,0:T(8,128)(2,1)S(1)} %copy-done.10, f32[1,1024]{1,0:T(1,128)S(1)} %convert_element_type.27.ids_ref), custom_call_target="tpu_custom_call" | custom-call | flops 7516192768 | bytes 16777216 | tf_op jit(solution)/shard_map/pallas_call | solution.py:156
  134.2 0.0 copy-start.3
  134.2 2.1 copy-done.3
  136.3 2.0 copy-done.6
  138.3 0.0 all-to-all-done.feat_ref.down_ref
  138.3 2.2 copy-done.4
  140.5 2.2 copy-done.7
  142.7 6.4 %shard_map.96 = bf16[16,144,512]{2,1,0:T(8,128)(2,1)S(1)} custom-call(bf16[16,192,512]{2,1,0:T(8,128)(2,1)S(1)} %all-to-all-done.feat_ref.down_ref, bf16[16,192,512]{2,1,0:T(8,128)(2,1)S(1)} %all-to-all-done.feat_ref.down_ref, bf16[16,208,1024]{2,1,0:T(8,128)(2,1)} %bitcast.25, bf16[2048,1024]{1,0:T(8,128)(2,1)S(1)} %copy-done.4, f32[2048,512]{1,0:T(8,128)S(1)} %copy-done.7, ...), custom_call_target="tpu_custom_call" | custom-call | flops 4294967296 | bytes 16777216 | tf_op jit(solution)/shard_map/pallas_call | solution.py:209
  149.1 0.0 copy-start.2
  149.1 1.4 copy-done.2
  150.5 8.8 %all-to-all-start.1 = ((bf16[16,144,512]{2,1,0:T(8,128)(2,1)}), bf16[16,144,512]{2,1,0:T(8,128)(2,1)}, u32[]{:S(2)}, u32[]{:S(2)}) async-start(bf16[16,144,512]{2,1,0:T(8,128)(2,1)} %copy-done.2), calls=%async_computation.1 | async-start | bytes 4718592 | tf_op jit(solution)/shard_map/all_to_all | solution.py:288
  159.3 0.2 slice.17
  159.5 2.0 copy-done.5
  161.5 2.4 convolution_convert_fusion
  163.9 48.6 %all-to-all-done.1 = bf16[16,144,512]{2,1,0:T(8,128)(2,1)} async-done(((bf16[16,144,512]{2,1,0:T(8,128)(2,1)}), bf16[16,144,512]{2,1,0:T(8,128)(2,1)}, u32[]{:S(2)}, u32[]{:S(2)}) %all-to-all-start.1) | async-done | bytes 2359328 | tf_op jit(solution)/shard_map/all_to_all | solution.py:288
  212.5 1.0 slice_reduce_fusion
  213.5 1.2 pad_maximum_fusion
  214.7 4.9 %all-to-all-start.2 = ((bf16[16,80,512]{2,1,0:T(8,128)(2,1)}), bf16[16,80,512]{2,1,0:T(8,128)(2,1)S(1)}, u32[]{:S(2)}, u32[]{:S(2)}) async-start(bf16[16,80,512]{2,1,0:T(8,128)(2,1)} %pad_maximum_fusion), calls=%async_computation.2 | async-start | bytes 2621440 | tf_op jit(solution)/shard_map/all_to_all | solution.py:288
  219.6 0.6 dynamic_slice.3
  220.8 1.9 convert_reduce_fusion
  223.4 1.8 slice_bitcast_fusion
  225.2 2.4 copy.12
  227.6 4.1 %copy.13 = bf16[128,8192]{1,0:T(8,128)(2,1)} copy(bf16[128,8192]{0,1:T(8,128)(2,1)} %bitcast.30) | data formatting | bytes 4194304
  231.7 18.5 %all-to-all-done.2.down_ref.low_ref = bf16[16,80,512]{2,1,0:T(8,128)(2,1)S(1)} async-done(((bf16[16,80,512]{2,1,0:T(8,128)(2,1)}), bf16[16,80,512]{2,1,0:T(8,128)(2,1)S(1)}, u32[]{:S(2)}, u32[]{:S(2)}) %all-to-all-start.2) | async-done | bytes 1310752 | tf_op jit(solution)/shard_map/all_to_all | solution.py:288
  250.2 2.9 %copy-done = bf16[3328,1024]{1,0:T(8,128)(2,1)S(1)} copy-done((bf16[3328,1024]{1,0:T(8,128)(2,1)S(1)}, bf16[3328,1024]{1,0:T(8,128)(2,1)}, u32[]{:S(2)}) %copy-start) | copy-done | bytes 6815768
  253.1 3.5 %shard_map.97 = (f32[64,8192]{1,0:T(8,128)}, f32[64,1024]{1,0:T(8,128)}) custom-call(bf16[16,80,512]{2,1,0:T(8,128)(2,1)S(1)} %all-to-all-done.2.down_ref.low_ref, bf16[16,80,512]{2,1,0:T(8,128)(2,1)S(1)} %all-to-all-done.2.down_ref.low_ref, bf16[16,208,1024]{2,1,0:T(8,128)(2,1)S(1)} %bitcast.27, bf16[16,208,1024]{2,1,0:T(8,128)(2,1)S(1)} %bitcast.28, ...), custom_call_target="tpu_custom_call" | custom-call | flops 536870912 | bytes 8388608 | tf_op jit(solution)/shard_map/pallas_call | solution.py:260
  (10 shorter events, 0.0 us)
Async XLA Ops:
  7.2 116.5 %all-gather.3.cloned.1.call-start = ((), (), s32[]{:S(2)}) async-start(), calls=%async_computation.3 | async-start | bytes 7241728 | tf_op jit(solution)/shard_map/all_gather | solution.py:310
  10.0 1.6 copy-start.8
  11.6 1.2 copy-start.9
  13.6 1.6 copy-start.1
  15.2 6.7 %copy-start.11 = (s32[16]{0:T(128)S(1)}, s32[16]{0:T(128)}, u32[]{:S(2)}) copy-start(s32[16]{0:T(128)} %param.13) | copy-start | bytes 196
  15.2 123.1 %all-to-all-start = ((bf16[16,192,512]{2,1,0:T(8,128)(2,1)}), bf16[16,192,512]{2,1,0:T(8,128)(2,1)S(1)}, u32[]{:S(2)}, u32[]{:S(2)}) async-start(bf16[16,192,512]{2,1,0:T(8,128)(2,1)} %copy-done.1), calls=%async_computation | async-start | bytes 6291456 | tf_op jit(solution)/shard_map/all_to_all | solution.py:288
  123.6 1.2 copy-start.10
  134.2 2.1 copy-start.3
  136.3 2.0 copy-start.6
  138.3 2.2 copy-start.4
  140.5 2.2 copy-start.7
  149.1 1.4 copy-start.2
  150.5 62.0 %all-to-all-start.1 = ((bf16[16,144,512]{2,1,0:T(8,128)(2,1)}), bf16[16,144,512]{2,1,0:T(8,128)(2,1)}, u32[]{:S(2)}, u32[]{:S(2)}) async-start(bf16[16,144,512]{2,1,0:T(8,128)(2,1)} %copy-done.2), calls=%async_computation.1 | async-start | bytes 4718592 | tf_op jit(solution)/shard_map/all_to_all | solution.py:288
  159.3 2.2 copy-start.5
  214.7 35.5 %all-to-all-start.2 = ((bf16[16,80,512]{2,1,0:T(8,128)(2,1)}), bf16[16,80,512]{2,1,0:T(8,128)(2,1)S(1)}, u32[]{:S(2)}, u32[]{:S(2)}) async-start(bf16[16,80,512]{2,1,0:T(8,128)(2,1)} %pad_maximum_fusion), calls=%async_computation.2 | async-start | bytes 2621440 | tf_op jit(solution)/shard_map/all_to_all | solution.py:288
  250.2 2.9 %copy-start = (bf16[3328,1024]{1,0:T(8,128)(2,1)S(1)}, bf16[3328,1024]{1,0:T(8,128)(2,1)}, u32[]{:S(2)}) copy-start(bf16[3328,1024]{1,0:T(8,128)(2,1)} %all-gather.3.cloned.1.call-done) | copy-start | bytes 20447236
Sparse Core Ops, SparseCore 0:
  10.9 112.7 all-gather.2

commit v2 on v1

v2 whole, which is shorter than its diff:
```python
import jax
import jax.numpy as jnp
from jax import lax
from jax.experimental import pallas as pl
from jax.experimental.pallas import tpu as pltpu
from jax.sharding import PartitionSpec as P

adapter_scale = 2.0
LANES = 128
INDEX_ROWS = 16
CAPACITY = 16
STEP = 4


def contract_matrices(left, right, left_dim, right_dim):
    return lax.dot_general(
        left, right, (((left_dim,), (right_dim,)), ((), ())), preferred_element_type=jnp.float32
    )


def frozen_part(cotangent, frozen_key_weight):
    return contract_matrices(
        cotangent, lax.all_gather(frozen_key_weight, "wide", axis=0, tiled=True), 1, 1
    )


def dispatch_body(
    features,
    cotangent,
    frozen_key_weight,
    adapter_down_weight,
    adapter_up_weight,
    row_adapter_index,
    device_adapter,
):
    row_count = features.shape[0]
    peer_count = lax.axis_size("wide")
    device_index = lax.axis_index("wide")
    capacity = max(2, 2 * row_count // peer_count)
    slot_range = jnp.arange(peer_count, dtype=jnp.int32)
    matches = row_adapter_index[:, 0][:, None] == device_adapter[None, :]
    token_slot = jnp.sum(jnp.where(matches, slot_range[None, :], 0), axis=1)
    slot_hit = (token_slot[:, None] == slot_range[None, :]).astype(jnp.int32)
    local_counts = jnp.sum(slot_hit, axis=0)
    token_counts = lax.psum(local_counts, "wide")
    earlier = jnp.cumsum(slot_hit, axis=0) - slot_hit
    token_rank = jnp.sum(earlier * slot_hit, axis=1)
    position = token_slot * capacity + token_rank
    slot_total = peer_count * capacity
    pick = position[None, :] == jnp.arange(slot_total, dtype=jnp.int32)[:, None]
    source_row = jnp.sum(
        jnp.where(pick, jnp.arange(row_count, dtype=jnp.int32)[None, :], 0), axis=1
    )
    filled = jnp.any(pick, axis=1)
    zero_value = jnp.zeros((), jnp.bfloat16)
    send_in = jnp.where(filled[:, None], features[source_row], zero_value).reshape(
        peer_count, capacity, -1
    )
    send_cot = jnp.where(filled[:, None], cotangent[source_row], zero_value).reshape(
        peer_count, capacity, -1
    )
    recv_in, recv_cot = (
        lax.all_to_all(send_in, "wide", split_axis=0, concat_axis=0, tiled=True),
        lax.all_to_all(send_cot, "wide", split_axis=0, concat_axis=0, tiled=True),
    )
    recv_in = recv_in.reshape(slot_total, -1)
    recv_cot = recv_cot.reshape(slot_total, -1)
    down_projection = adapter_down_weight[0]
    up_projection = adapter_up_weight[0]
    low_in = jnp.dot(recv_in, down_projection, preferred_element_type=jnp.float32).astype(
        jnp.bfloat16
    )
    low_rank_output = contract_matrices(recv_cot, up_projection, 1, 1).astype(jnp.bfloat16)
    rows_per_adapter = (
        adapter_scale * contract_matrices(low_rank_output, down_projection, 1, 1)
    ).astype(jnp.bfloat16)
    inverse_permutation = adapter_scale / jnp.maximum(token_counts[device_index], 1).astype(
        jnp.float32
    )
    grad_down = inverse_permutation * contract_matrices(recv_in, low_rank_output, 0, 0)
    grad_up = inverse_permutation * contract_matrices(low_in, recv_cot, 0, 0)
    returned = lax.all_to_all(
        rows_per_adapter.reshape(peer_count, capacity, -1),
        "wide",
        split_axis=0,
        concat_axis=0,
        tiled=True,
    )
    returned = returned.reshape(slot_total, -1)
    adapter_grad = returned[position]
    base_grad = frozen_part(cotangent, frozen_key_weight)
    input_grad = (base_grad + adapter_grad.astype(jnp.float32)).astype(jnp.bfloat16)
    return (input_grad, grad_down[None], grad_up[None])


def params(mebibytes):
    return pltpu.CompilerParams(vmem_limit_bytes=mebibytes * 1024 * 1024)


def place_columns(packed):
    values = packed.astype(jnp.float32)
    chunks = packed.shape[2] // LANES
    return jnp.concatenate(
        [
            values[item, :, j * LANES : (j + 1) * LANES]
            for item in range(packed.shape[0])
            for j in range(chunks)
        ],
        axis=0,
    )


def payload_kernel(cot_ref, up_ref, index_ref, adapters_ref, out_ref):
    rows = cot_ref.shape[0]
    rank = up_ref.shape[0]
    peers = adapters_ref.shape[0]
    out_ref[:rows, :] = cot_ref[...]
    out_ref[rows : rows + rank, :] = up_ref[...]
    index = index_ref[...]
    slot = jnp.zeros(index.shape, jnp.int32)
    for w in range(peers):
        slot = jnp.where(index == adapters_ref[w], w, slot)
    slot_range = lax.broadcasted_iota(jnp.int32, (peers, rows), 0)
    hits = jnp.where(slot_range == slot, 1.0, 0.0)
    before = lax.broadcasted_iota(jnp.int32, (rows, rows), 0)
    after = lax.broadcasted_iota(jnp.int32, (rows, rows), 1)
    earlier = jnp.where(before < after, 1.0, 0.0).astype(jnp.bfloat16)
    ranks = contract_matrices(hits.astype(jnp.bfloat16), earlier, 1, 0)
    order = jnp.sum(hits * ranks, axis=0, keepdims=True)
    place = slot.astype(jnp.float32) * CAPACITY + order
    marks = jnp.broadcast_to(place, (rows, rows)).T.astype(jnp.bfloat16)
    for j in range(rows // INDEX_ROWS):
        out_ref[rows + rank :, j * LANES : (j + 1) * LANES] = marks[
            j * INDEX_ROWS : (j + 1) * INDEX_ROWS, :
        ]


def build_payload(cotangent, up, index, adapters):
    total = cotangent.shape[0] + up.shape[0] + INDEX_ROWS
    vmem = pl.BlockSpec(memory_space=pltpu.VMEM)
    return pl.pallas_call(
        payload_kernel,
        in_specs=[vmem, vmem, vmem, pl.BlockSpec(memory_space=pltpu.SMEM)],
        out_shape=jax.ShapeDtypeStruct((total, cotangent.shape[1]), jnp.bfloat16),
        compiler_params=params(58),
        cost_estimate=pl.CostEstimate(flops=0, bytes_accessed=1 << 20, transcendentals=0),
    )(cotangent, up, index, adapters)


def pack_kernel(features_ref, down_ref, out_ref):
    rows = features_ref.shape[0]
    share = out_ref.shape[2]
    for d in range(out_ref.shape[0]):
        span = slice(d * share, (d + 1) * share)
        out_ref[d, :rows, :] = features_ref[:, span]
        out_ref[d, rows:, :] = down_ref[:, span]


def pack_columns(features, down, peer_count):
    rows, width = features.shape
    rank = down.shape[0]
    share = width // peer_count
    return pl.pallas_call(
        pack_kernel,
        grid=(peer_count // 2,),
        in_specs=[
            pl.BlockSpec((rows, 2 * share), lambda d: (0, d)),
            pl.BlockSpec((rank, 2 * share), lambda d: (0, d)),
        ],
        out_specs=pl.BlockSpec((2, rows + rank, share), lambda d: (d, 0, 0)),
        out_shape=jax.ShapeDtypeStruct((peer_count, rows + rank, share), jnp.bfloat16),
        compiler_params=params(58),
        cost_estimate=pl.CostEstimate(flops=0, bytes_accessed=6 << 20, transcendentals=0),
    )(features, down)


def adapter_lanes(j):
    lane = lax.broadcasted_iota(jnp.int32, (1, LANES), 1)
    return (2 * j + lane // (LANES // 2)).astype(jnp.float32)


def low_out_kernel(cot_ref, up_ref, place_ref, weight_ref, low_ref, base_ref):
    keys = cot_ref.shape[2]
    cot = cot_ref[...].reshape(-1, keys)
    slot = jnp.floor(place_columns(place_ref[...]) / CAPACITY)
    low = contract_matrices(cot, up_ref[...].reshape(-1, keys), 1, 1)
    for j in range(low.shape[1] // LANES):
        span = slice(j * LANES, (j + 1) * LANES)
        low_ref[:, span] = jnp.where(slot == adapter_lanes(j), low[:, span], 0.0).astype(
            jnp.bfloat16
        )
    base_ref[...] = contract_matrices(cot, weight_ref[...], 1, 1)


def low_out(gathered, weight, rows, rank):
    peer_count, _, keys = gathered.shape
    share = weight.shape[0]
    block = STEP * rows
    slots = peer_count * rank
    once = pl.Buffered(1)
    return pl.pallas_call(
        low_out_kernel,
        grid=(peer_count // STEP,),
        in_specs=[
            pl.BlockSpec((STEP, rows, keys), lambda s: (s, 0, 0)),
            pl.BlockSpec(
                (peer_count, rank, keys), lambda s: (0, rows // rank, 0), pipeline_mode=once
            ),
            pl.BlockSpec(
                (STEP, INDEX_ROWS, keys), lambda s: (s, (rows + rank) // INDEX_ROWS, 0)
            ),
            pl.BlockSpec((share, keys), lambda s: (0, 0), pipeline_mode=once),
        ],
        out_specs=[
            pl.BlockSpec((block, slots), lambda s: (s, 0)),
            pl.BlockSpec((block, share), lambda s: (s, 0)),
        ],
        out_shape=[
            jax.ShapeDtypeStruct((peer_count * rows, slots), jnp.bfloat16),
            jax.ShapeDtypeStruct((peer_count * rows, share), jnp.float32),
        ],
        compiler_params=params(58),
        cost_estimate=pl.CostEstimate(flops=7 << 30, bytes_accessed=16 << 20, transcendentals=0),
    )(gathered, gathered, gathered, weight)


def share_kernel(feat_ref, down_ref, place_ref, low_ref, base_ref, out_ref, grad_ref):
    step = pl.program_id(0)
    items, rows, share = feat_ref.shape
    peers, rank, _ = down_ref.shape
    down = down_ref[...].reshape(-1, share)
    feat = feat_ref[...].reshape(-1, share)
    low = low_ref[...]
    grad = base_ref[...] + adapter_scale * contract_matrices(low, down, 1, 0)
    out_ref[pl.ds(step * items, items), :rows, :] = grad.astype(jnp.bfloat16).reshape(
        items, rows, share
    )

    @pl.when(step == 0)
    def _():
        grad_ref[...] = contract_matrices(low, feat, 0, 0)

    @pl.when(step > 0)
    def _():
        grad_ref[...] += contract_matrices(low, feat, 0, 0)

    partial = contract_matrices(feat, down, 1, 1)
    place = place_columns(place_ref[...])
    slot = jnp.floor(place / CAPACITY)
    total = jnp.zeros_like(place)
    for j in range(partial.shape[1] // LANES):
        span = slice(j * LANES, (j + 1) * LANES)
        total = total + jnp.where(slot == adapter_lanes(j), partial[:, span], 0.0)
    total = (total + pltpu.roll(total, LANES // 2, 1)).astype(jnp.bfloat16)
    places = lax.broadcasted_iota(jnp.int32, (peers * CAPACITY, LANES), 0).astype(jnp.float32)
    picked = []
    for item in range(items):
        span = slice(item * rows, (item + 1) * rows)
        row = place[span, :].T[:1, :]
        pick = jnp.where(places == row, 1.0, 0.0).astype(jnp.bfloat16)
        picked.append(contract_matrices(pick, total[span, :], 1, 0))
    left = lax.broadcasted_iota(jnp.int32, (CAPACITY, LANES), 1) < LANES // 2
    lanes = pl.ds(pl.multiple_of(step * LANES, LANES), LANES)
    for w in range(peers):
        span = slice(w * CAPACITY, (w + 1) * CAPACITY)
        for half in range(2):
            pair = jnp.where(left, picked[half][span, :], picked[half + 2][span, :])
            first = rows + rank + half * CAPACITY
            out_ref[w, first : first + CAPACITY, lanes] = pair.astype(jnp.bfloat16)

    @pl.when(step == pl.num_programs(0) - 1)
    def _():
        for w in range(peers):
            out_ref[w, rows : rows + rank, :] = grad_ref[w * rank : (w + 1) * rank, :].astype(
                jnp.bfloat16
            )


def share_results(received, gathered, low, base, rows, rank):
    peer_count, _, share = received.shape
    keys = gathered.shape[2]
    block = STEP * rows
    slots = peer_count * rank
    total = rows + rank + 2 * CAPACITY
    once = pl.Buffered(1)
    return pl.pallas_call(
        share_kernel,
        grid=(peer_count // STEP,),
        in_specs=[
            pl.BlockSpec((STEP, rows, share), lambda s: (s, 0, 0)),
            pl.BlockSpec(
                (peer_count, rank, share), lambda s: (0, rows // rank, 0), pipeline_mode=once
            ),
            pl.BlockSpec(
                (STEP, INDEX_ROWS, keys), lambda s: (s, (rows + rank) // INDEX_ROWS, 0)
            ),
            pl.BlockSpec((block, slots), lambda s: (s, 0)),
            pl.BlockSpec((block, share), lambda s: (s, 0)),
        ],
        out_specs=pl.BlockSpec((peer_count, total, share), lambda s: (0, 0, 0)),
        out_shape=jax.ShapeDtypeStruct((peer_count, total, share), jnp.bfloat16),
        scratch_shapes=[pltpu.VMEM((slots, share), jnp.float32)],
        compiler_params=params(58),
        cost_estimate=pl.CostEstimate(flops=7 << 30, bytes_accessed=16 << 20, transcendentals=0),
    )(received, received, gathered, low, base)


def select_kernel(own_ref, cot_ref, place_ref, rows_ref, scale_ref):
    step = pl.program_id(0)
    items, rows, _ = cot_ref.shape
    place = place_columns(place_ref[...])
    first = own_ref[0] * CAPACITY
    wanted = first + lax.broadcasted_iota(jnp.int32, (CAPACITY, LANES), 0)
    wanted = wanted.astype(jnp.float32)

    @pl.when(step == 0)
    def _():
        scale_ref[...] = jnp.zeros_like(scale_ref)

    for item in range(items):
        row = place[item * rows : (item + 1) * rows, :].T[:1, :]
        pick = jnp.where(wanted == row, 1.0, 0.0)
        scale_ref[...] += jnp.sum(pick, axis=0, keepdims=True)
        chosen = contract_matrices(pick.astype(jnp.bfloat16), cot_ref[item], 1, 0)
        rows_ref[item * CAPACITY : (item + 1) * CAPACITY, :] = chosen.astype(jnp.bfloat16)

    @pl.when(step == pl.num_programs(0) - 1)
    def _():
        count = jnp.sum(scale_ref[...], axis=1, keepdims=True)
        scale_ref[...] = adapter_scale / jnp.maximum(jnp.broadcast_to(count, (1, LANES)), 1.0)


def select_rows(own, gathered, rows, rank):
    peer_count, _, keys = gathered.shape
    return pl.pallas_call(
        select_kernel,
        grid=(peer_count // STEP,),
        in_specs=[
            pl.BlockSpec(memory_space=pltpu.SMEM),
            pl.BlockSpec((STEP, rows, keys), lambda s: (s, 0, 0)),
            pl.BlockSpec(
                (STEP, INDEX_ROWS, keys), lambda s: (s, (rows + rank) // INDEX_ROWS, 0)
            ),
        ],
        out_specs=[
            pl.BlockSpec((STEP * CAPACITY, keys), lambda s: (s, 0)),
            pl.BlockSpec((1, LANES), lambda s: (0, 0)),
        ],
        out_shape=[
            jax.ShapeDtypeStruct((peer_count * CAPACITY, keys), jnp.bfloat16),
            jax.ShapeDtypeStruct((1, LANES), jnp.float32),
        ],
        compiler_params=params(58),
        cost_estimate=pl.CostEstimate(flops=1 << 29, bytes_accessed=8 << 20, transcendentals=0),
    )(own, gathered, gathered)


def finish_kernel(part_ref, cot_ref, scale_ref, grad_ref, gd_ref, gu_ref, acc):
    step = pl.program_id(0)
    items, _, share = part_ref.shape
    rows = grad_ref.shape[0]
    rank = gd_ref.shape[0]
    scale = scale_ref[...]

    @pl.when(step == 0)
    def _():
        acc[...] = jnp.zeros_like(acc)

    for item in range(items):
        span = slice(item * share, (item + 1) * share)
        grad_ref[:, span] = part_ref[item, :rows, :]
        gd_ref[:, span] = scale[0, 0] * part_ref[item, rows : rows + rank, :].astype(jnp.float32)
        acc[...] += part_ref[item, rows + rank :, :].astype(jnp.float32)

    @pl.when(step == pl.num_programs(0) - 1)
    def _():
        pieces = []
        for source in range(cot_ref.shape[0] // CAPACITY):
            chunk, half, first = source // 4, source % 4 // 2, source % 2 * CAPACITY
            piece = acc[first : first + CAPACITY, chunk * LANES : (chunk + 1) * LANES]
            pieces.append(pltpu.roll(piece, LANES // 2, 1) if half else piece)
        low = jnp.concatenate(pieces, axis=0).astype(jnp.bfloat16)
        gu_ref[...] = scale[0, 0] * contract_matrices(low, cot_ref[...], 0, 0)[:rank, :]


def finish(parts, chosen, scale, rows, rank):
    peer_count, total, share = parts.shape
    slots, keys = chosen.shape
    return pl.pallas_call(
        finish_kernel,
        grid=(peer_count // STEP,),
        in_specs=[
            pl.BlockSpec((STEP, total, share), lambda s: (s, 0, 0)),
            pl.BlockSpec((slots, keys), lambda s: (0, 0)),
            pl.BlockSpec((1, LANES), lambda s: (0, 0)),
        ],
        out_specs=[
            pl.BlockSpec((rows, STEP * share), lambda s: (0, s)),
            pl.BlockSpec((rank, STEP * share), lambda s: (0, s)),
            pl.BlockSpec((rank, keys), lambda s: (0, 0)),
        ],
        out_shape=[
            jax.ShapeDtypeStruct((rows, peer_count * share), jnp.bfloat16),
            jax.ShapeDtypeStruct((rank, peer_count * share), jnp.float32),
            jax.ShapeDtypeStruct((rank, keys), jnp.float32),
        ],
        scratch_shapes=[pltpu.VMEM((2 * CAPACITY, share), jnp.float32)],
        compiler_params=params(58),
        cost_estimate=pl.CostEstimate(flops=1 << 27, bytes_accessed=8 << 20, transcendentals=0),
    )(parts, chosen, scale)


def swap(block, mask):
    peer_count = lax.axis_size("wide")
    return lax.ppermute(block, "wide", [(i, i ^ mask) for i in range(peer_count)])


def spread(payload, packed):
    far, near, beside, core = 12, 4, 2, 1
    mirrored, packed = lax.optimization_barrier((swap(payload, far), packed))
    held = [(0, payload), (far, mirrored)]
    for mask in (near, beside, core):
        held = held + [(shift ^ mask, swap(block, mask)) for shift, block in held]
    return lax.optimization_barrier((packed, held))


def exchange(block):
    return lax.all_to_all(block, "wide", split_axis=0, concat_axis=0, tiled=True)


def column_body(
    features,
    cotangent,
    frozen_key_weight,
    adapter_down_weight,
    adapter_up_weight,
    row_adapter_index,
    device_adapter,
):
    rows = features.shape[0]
    rank = adapter_up_weight.shape[1]
    peer_count = lax.axis_size("wide")
    device_index = lax.axis_index("wide")
    payload = build_payload(
        cotangent, adapter_up_weight[0], row_adapter_index.reshape(1, rows), device_adapter
    )
    packed = pack_columns(features, adapter_down_weight[0].T, peer_count)
    packed, held = spread(payload, packed)
    received = exchange(packed)
    gathered = jnp.zeros((peer_count,) + payload.shape, payload.dtype)
    for shift, block in held:
        gathered = lax.dynamic_update_slice(gathered, block[None], (device_index ^ shift, 0, 0))
    low, base = low_out(gathered, frozen_key_weight, rows, rank)
    parts = exchange(share_results(received, gathered, low, base, rows, rank))
    own = jnp.full((1,), device_index, jnp.int32)
    chosen, scale = select_rows(own, gathered, rows, rank)
    input_grad, grad_down, grad_up = finish(parts, chosen, scale, rows, rank)
    return (input_grad, grad_down.T[None], grad_up[None])


def solution(mesh):
    in_specs = (
        P(("groups", "wide"), None),
        P(("groups", "wide"), None),
        P("wide", None),
        P(("groups", "wide"), None, None),
        P(("groups", "wide"), None, None),
        P(("groups", "wide"), None),
        P("groups"),
    )
    out_specs = (
        P(("groups", "wide"), None),
        P(("groups", "wide"), None, None),
        P(("groups", "wide"), None, None),
    )

    def body(*arrays):
        rows, width = arrays[0].shape
        keys = arrays[1].shape[1]
        rank = arrays[4].shape[1]
        peer_count = mesh.shape["wide"]
        by_columns = (
            peer_count == STEP * STEP
            and peer_count * rank <= keys
            and rank * 2 == LANES
            and rows == LANES
            and rows // INDEX_ROWS * LANES == keys
            and peer_count * rank == 2 * (width // peer_count)
        )
        return (column_body if by_columns else dispatch_body)(*arrays)

    return jax.shard_map(body, mesh=mesh, in_specs=in_specs, out_specs=out_specs, check_vma=False)
```

time: 264 us -> 239 us (0.905)
  waiting for transfers between devices: 169 us -> 145 us
  Pallas kernels: 20 us -> 42.5 us
  between operations: 15.5 us -> 0.88 us
  starting transfers between devices: 20.5 us -> 29.3 us
  local copies, waits for them, and re-layouts: 29.9 us -> 21.1 us
  other arithmetic: 6.59 us -> 0 us
    all_gather x1 -> x0, waiting for transfers between devices: 102 us -> none  [column_body(): gathered = lax.all_gather(payload, 'wide', axis=0)]
    all_to_all x3 -> x2, waiting for transfers between devices: 67.1 us -> 118 us  [exchange(): lax.all_to_all(block, 'wide', split_axis=0, concat_axis=0, tiled=True)]
    ppermute x0 -> x15, waiting for transfers between devices: none -> 26.2 us  [swap(): lax.ppermute(block, 'wide', [(i, i ^ mask) for i in range(peer_count)])]
    unnamed x26 -> x60, local copies, waits for them, and re-layouts: 24.5 us -> 3.6 us
    ppermute x0 -> x15, starting transfers between devices: none -> 18.4 us  [swap(): lax.ppermute(block, 'wide', [(i, i ^ mask) for i in range(peer_count)])]
    dynamic_update_slice x0 -> x16, local copies, waits for them, and re-layouts: none -> 13.7 us  [column_body(): lax.dynamic_update_slice(gathered, block[None], (device_index ^ shift, 0,...]
    pallas_call x1 -> x3, Pallas kernels: 0.76 us -> 12.6 us  [the longest x1 6.1 us: pack_columns(): pl.pallas_call(pack_kernel, grid=(peer_count // 2,), in_specs=[pl.BlockSp...]
    all_to_all x3 -> x2, starting transfers between devices: 20.4 us -> 10.9 us  [exchange(): lax.all_to_all(block, 'wide', split_axis=0, concat_axis=0, tiled=True)]
  transfers between devices with their start and end apart: 4 -> 17, of which waited for: 3 -> 7; matrix products, arithmetic and copies ran while one was open for 5% -> 7% of each run, Pallas kernels for 4% -> 9%
where the time goes in v2:
time: 239 us; the launch traced here: 238 us
  waiting for transfers between devices  145 us (61%)
  Pallas kernels  42.5 us (18%)
  starting transfers between devices  29.3 us (12%)
  local copies, waits for them, and re-layouts  21.1 us (9%)
    all_to_all x2, waiting for transfers between devices, exchange(): lax.all_to_all(block, 'wide', split_axis=0, concat_axis=0, tiled=True)  118 us
    ppermute x15, waiting for transfers between devices, swap(): lax.ppermute(block, 'wide', [(i, i ^ mask) for i in range(peer_count)])  26.2 us
    ppermute x15, starting transfers between devices, swap(): lax.ppermute(block, 'wide', [(i, i ^ mask) for i in range(peer_count)])  18.4 us
    pallas_call x1, Pallas kernels, share_results(): pl.pallas_call(share_kernel, grid=(peer_count // STEP,), in_specs=[pl.Blo...  14.1 us
    dynamic_update_slice x16, local copies, waits for them, and re-layouts, column_body(): lax.dynamic_update_slice(gathered, block[None], (device_index ^ shift, 0,...  13.7 us
    all_to_all x2, starting transfers between devices, exchange(): lax.all_to_all(block, 'wide', split_axis=0, concat_axis=0, tiled=True)  10.9 us
    pallas_call x1, Pallas kernels, low_out(): pl.pallas_call(low_out_kernel, grid=(peer_count // STEP,), in_specs=[pl.B...  10.6 us
    pallas_call x1, Pallas kernels, pack_columns(): pl.pallas_call(pack_kernel, grid=(peer_count // 2,), in_specs=[pl.BlockSp...  6.1 us
  transfers between devices with their start and end apart: 17, of which 7 were waited for; matrix products, arithmetic and copies ran while one was open for 7% of the time, Pallas kernels for 9%

profile of v2, /device:TPU:11, one launch (start us, length us, event | category | flops | bytes accessed | tf_op | source)
XLA Modules:
  0.0 238.3 jit_solution(4731679683773948416)
XLA Ops:
  0.6 2.0 shard_map.94
  2.7 1.3 collective-permute-start
  4.0 2.2 collective-permute-start.1
  6.2 0.3 collective-permute-start.3
  6.4 1.5 collective-permute-start.7
  7.9 6.1 %shard_map.95 = bf16[16,192,512]{2,1,0:T(8,128)(2,1)} custom-call(bf16[128,8192]{1,0:T(8,128)(2,1)} %features_ref.1, bf16[64,8192]{1,0:T(8,128)(2,1)} %bitcast.42), custom_call_target="tpu_custom_call" | custom-call | bytes 6291456 | tf_op jit(solution)/shard_map/pallas_call | solution.py:163
  14.0 8.8 %collective-permute-done = bf16[208,1024]{1,0:T(8,128)(2,1)S(1)} collective-permute-done((bf16[208,1024]{1,0:T(8,128)(2,1)}, bf16[208,1024]{1,0:T(8,128)(2,1)S(1)}, u32[]{:S(2)}, u32[]{:S(2)}) %collective-permute-start) | collective-permute-done | bytes 426016 | tf_op jit(solution)/shard_map/ppermute | solution.py:415
  22.9 0.3 collective-permute-start.4
  23.1 1.7 collective-permute-done.1
  24.8 0.3 collective-permute-start.5
  25.1 2.0 collective-permute-start.8
  27.2 6.3 %collective-permute-done.2 = bf16[208,1024]{1,0:T(8,128)(2,1)S(1)} collective-permute-done((bf16[208,1024]{1,0:T(8,128)(2,1)S(1)}, bf16[208,1024]{1,0:T(8,128)(2,1)S(1)}, u32[]{:S(2)}, u32[]{:S(2)}) %collective-permute-start.2) | collective-permute-done | bytes 426016 | tf_op jit(solution)/shard_map/ppermute | solution.py:415
  33.5 0.3 collective-permute-start.6
  33.7 3.3 %collective-permute-start.11 = (bf16[208,1024]{1,0:T(8,128)(2,1)S(1)}, bf16[208,1024]{1,0:T(8,128)(2,1)S(1)}, u32[]{:S(2)}, u32[]{:S(2)}) collective-permute-start(bf16[208,1024]{1,0:T(8,128)(2,1)S(1)} %collective-permute-done.3), channel_id=1, source_target_pairs={{0,1},{1,0},{2,3},{3,2},{4,5},{5,4},{6,7},{7,6},{8,9},{9,8},{10,11... | collective-permute-start | bytes 1277960 | tf_op jit(solution)/shard_map/ppermute | solution.py:415
  37.0 5.0 %collective-permute-done.5 = bf16[208,1024]{1,0:T(8,128)(2,1)S(1)} collective-permute-done((bf16[208,1024]{1,0:T(8,128)(2,1)S(1)}, bf16[208,1024]{1,0:T(8,128)(2,1)S(1)}, u32[]{:S(2)}, u32[]{:S(2)}) %collective-permute-start.5) | collective-permute-done | bytes 426016 | tf_op jit(solution)/shard_map/ppermute | solution.py:415
  42.0 4.2 %collective-permute-start.10 = (bf16[208,1024]{1,0:T(8,128)(2,1)S(1)}, bf16[208,1024]{1,0:T(8,128)(2,1)S(1)}, u32[]{:S(2)}, u32[]{:S(2)}) collective-permute-start(bf16[208,1024]{1,0:T(8,128)(2,1)S(1)} %collective-permute-done.2), channel_id=1, source_target_pairs={{0,1},{1,0},{2,3},{3,2},{4,5},{5,4},{6,7},{7,6},{8,9},{9,8},{10,11... | collective-permute-start | bytes 1277960 | tf_op jit(solution)/shard_map/ppermute | solution.py:415
  46.2 0.4 collective-permute-start.13
  46.7 4.4 %collective-permute-done.6 = bf16[208,1024]{1,0:T(8,128)(2,1)S(1)} collective-permute-done((bf16[208,1024]{1,0:T(8,128)(2,1)S(1)}, bf16[208,1024]{1,0:T(8,128)(2,1)S(1)}, u32[]{:S(2)}, u32[]{:S(2)}) %collective-permute-start.6) | collective-permute-done | bytes 426016 | tf_op jit(solution)/shard_map/ppermute | solution.py:415
  51.1 2.3 collective-permute-start.14
  53.5 0.7 copy-done.20
  54.3 0.1 copy-done.22
  54.4 0.8 copy-done.28
  55.3 6.0 %all-to-all-start = ((bf16[16,192,512]{2,1,0:T(8,128)(2,1)}), bf16[16,192,512]{2,1,0:T(8,128)(2,1)S(1)}, u32[]{:S(2)}, u32[]{:S(2)}) async-start(bf16[16,192,512]{2,1,0:T(8,128)(2,1)} %shard_map.95), calls=%async_computation | async-start | bytes 6291456 | tf_op jit(solution)/shard_map/all_to_all | solution.py:428
  61.4 3.8 %broadcast_in_dim.60 = bf16[16,208,1024]{2,1,0:T(8,128)(2,1)} broadcast(bf16[]{:T(256)} %constant.16.clone.1), dimensions={} | broadcast | bytes 6815746 | tf_op jit(solution)/shard_map/broadcast_in_dim | solution.py:450
  65.2 0.8 bitcast_dynamic-update-slice_fusion.15
  66.0 0.8 bitcast_dynamic-update-slice_fusion.14
  66.9 0.8 bitcast_dynamic-update-slice_fusion.13
  67.6 0.8 bitcast_dynamic-update-slice_fusion.12
  68.4 0.8 bitcast_dynamic-update-slice_fusion.11
  69.2 0.8 bitcast_dynamic-update-slice_fusion.10
  70.0 0.8 bitcast_dynamic-update-slice_fusion.9
  70.9 0.8 bitcast_dynamic-update-slice_fusion.8
  71.6 0.8 bitcast_dynamic-update-slice_fusion.7
  72.4 0.8 bitcast_dynamic-update-slice_fusion.6
  73.2 0.8 bitcast_dynamic-update-slice_fusion.5
  74.0 0.8 bitcast_dynamic-update-slice_fusion.4
  74.8 0.8 bitcast_dynamic-update-slice_fusion.3
  75.6 0.8 bitcast_dynamic-update-slice_fusion.2
  76.4 0.8 bitcast_dynamic-update-slice_fusion.1
  77.2 1.8 bitcast_dynamic-update-slice_fusion.cot_ref.up_ref.place_ref
  79.0 10.6 %shard_map.96 = (bf16[2048,1024]{1,0:T(8,128)(2,1)}, f32[2048,512]{1,0:T(8,128)}) custom-call(bf16[16,208,1024]{2,1,0:T(8,128)(2,1)} %bitcast_dynamic-update-slice_fusion.cot_ref.up_ref.place_ref, bf16[16,208,1024]{2,1,0:T(8,128)(2,1)} %bitcast_dynamic-update-slice_fusion.cot_ref.up_ref.place_ref, ...), custom_call_target="tpu_custom_call" | custom-call | flops 7516192768 | bytes 16777216 | tf_op jit(solution)/shard_map/pallas_call | solution.py:201
  89.6 41.6 %all-to-all-done.feat_ref.down_ref = bf16[16,192,512]{2,1,0:T(8,128)(2,1)S(1)} async-done(((bf16[16,192,512]{2,1,0:T(8,128)(2,1)}), bf16[16,192,512]{2,1,0:T(8,128)(2,1)S(1)}, u32[]{:S(2)}, u32[]{:S(2)}) %all-to-all-start) | async-done | bytes 3145760 | tf_op jit(solution)/shard_map/all_to_all | solution.py:428
  131.2 1.7 copy-done
  132.9 14.1 %shard_map.97 = bf16[16,224,512]{2,1,0:T(8,128)(2,1)} custom-call(bf16[16,192,512]{2,1,0:T(8,128)(2,1)} %copy-done, bf16[16,192,512]{2,1,0:T(8,128)(2,1)} %copy-done, bf16[16,208,1024]{2,1,0:T(8,128)(2,1)} %bitcast_dynamic-update-slice_fusion.cot_ref.up_ref.place_ref, bf16[2048,1024]{1,0:T(8,128)(2,1)} %get-tuple-element.80.low_ref, ...), custom_call_target="tpu_custom_call" | custom-call | flops 7516192768 | bytes 16777216 | tf_op jit(solution)/shard_map/pallas_call | solution.py:286
  147.0 4.9 %all-to-all-start.1 = ((bf16[16,224,512]{2,1,0:T(8,128)(2,1)}), bf16[16,224,512]{2,1,0:T(8,128)(2,1)}, u32[]{:S(2)}, u32[]{:S(2)}) async-start(bf16[16,224,512]{2,1,0:T(8,128)(2,1)} %shard_map.97), calls=%async_computation.1 | async-start | bytes 7340032 | tf_op jit(solution)/shard_map/all_to_all | solution.py:428
  151.9 4.5 %shard_map.98 = (bf16[256,1024]{1,0:T(8,128)(2,1)}, f32[1,128]{1,0:T(1,128)}) custom-call(s32[1]{0:T(128)} %bitcast.20.own_ref, bf16[16,208,1024]{2,1,0:T(8,128)(2,1)} %bitcast_dynamic-update-slice_fusion.cot_ref.up_ref.place_ref, bf16[16,208,1024]{2,1,0:T(8,128)(2,1)} %bitcast_dynamic-update-slice_fusion.cot_ref.up_ref.place_ref), custom_call_target="tpu_custom_call" | custom-call | flops 536870912 | bytes 8388608 | tf_op jit(solution)/shard_map/pallas_call | solution.py:335
  156.4 76.8 %all-to-all-done.1.part_ref = bf16[16,224,512]{2,1,0:T(8,128)(2,1)} async-done(((bf16[16,224,512]{2,1,0:T(8,128)(2,1)}), bf16[16,224,512]{2,1,0:T(8,128)(2,1)}, u32[]{:S(2)}, u32[]{:S(2)}) %all-to-all-start.1) | async-done | bytes 3670048 | tf_op jit(solution)/shard_map/all_to_all | solution.py:428
  233.2 5.2 %shard_map.99 = (bf16[128,8192]{1,0:T(8,128)(2,1)}, f32[64,8192]{1,0:T(8,128)}, f32[64,1024]{1,0:T(8,128)}) custom-call(bf16[16,224,512]{2,1,0:T(8,128)(2,1)} %all-to-all-done.1.part_ref, bf16[256,1024]{1,0:T(8,128)(2,1)} %get-tuple-element.82.cot_ref, f32[1,128]{1,0:T(1,128)} %get-tuple-element.83.scale_ref), custom_call_target="tpu_custom_call" | custom-call | flops 134217728 | bytes 8388608 | tf_op jit(solution)/shard_map/pallas_call | solution.py:389
  (69 shorter events, 0.4 us)
Async XLA Ops:
  2.7 20.2 %collective-permute-start = (bf16[208,1024]{1,0:T(8,128)(2,1)}, bf16[208,1024]{1,0:T(8,128)(2,1)S(1)}, u32[]{:S(2)}, u32[]{:S(2)}) collective-permute-start(bf16[208,1024]{1,0:T(8,128)(2,1)} %shard_map.94), channel_id=1, source_target_pairs={{0,12},{1,13},{2,14},{3,15},{4,8},{5,9},{6,10},{7,11},{8,4},{9,5},... | collective-permute-start | bytes 1277960 | tf_op jit(solution)/shard_map/ppermute | solution.py:415
  4.0 20.8 %collective-permute-start.1 = (bf16[208,1024]{1,0:T(8,128)(2,1)}, bf16[208,1024]{1,0:T(8,128)(2,1)S(1)}, u32[]{:S(2)}, u32[]{:S(2)}) collective-permute-start(bf16[208,1024]{1,0:T(8,128)(2,1)} %shard_map.94), channel_id=1, source_target_pairs={{0,4},{1,5},{2,6},{3,7},{4,0},{5,1},{6,2},{7,3},{8,12},{9,13},{10,... | collective-permute-start | bytes 1277960 | tf_op jit(solution)/shard_map/ppermute | solution.py:415
  6.2 18.9 %collective-permute-start.3 = (bf16[208,1024]{1,0:T(8,128)(2,1)}, bf16[208,1024]{1,0:T(8,128)(2,1)S(1)}, u32[]{:S(2)}, u32[]{:S(2)}) collective-permute-start(bf16[208,1024]{1,0:T(8,128)(2,1)} %shard_map.94), channel_id=1, source_target_pairs={{0,2},{1,3},{2,0},{3,1},{4,6},{5,7},{6,4},{7,5},{8,10},{9,11},{10,... | collective-permute-start | bytes 1277960 | tf_op jit(solution)/shard_map/ppermute | solution.py:415
  6.4 20.7 %collective-permute-start.7 = (bf16[208,1024]{1,0:T(8,128)(2,1)}, bf16[208,1024]{1,0:T(8,128)(2,1)S(1)}, u32[]{:S(2)}, u32[]{:S(2)}) collective-permute-start(bf16[208,1024]{1,0:T(8,128)(2,1)} %shard_map.94), channel_id=1, source_target_pairs={{0,1},{1,0},{2,3},{3,2},{4,5},{5,4},{6,7},{7,6},{8,9},{9,8},{10,11... | collective-permute-start | bytes 1277960 | tf_op jit(solution)/shard_map/ppermute | solution.py:415
  22.9 32.4 %copy-start.6 = (bf16[208,1024]{1,0:T(8,128)(2,1)}, bf16[208,1024]{1,0:T(8,128)(2,1)S(1)}, u32[]{:S(2)}) copy-start(bf16[208,1024]{1,0:T(8,128)(2,1)S(1)} %collective-permute-done) | copy-start | bytes 1277956
  22.9 10.6 %collective-permute-start.2 = (bf16[208,1024]{1,0:T(8,128)(2,1)S(1)}, bf16[208,1024]{1,0:T(8,128)(2,1)S(1)}, u32[]{:S(2)}, u32[]{:S(2)}) collective-permute-start(bf16[208,1024]{1,0:T(8,128)(2,1)S(1)} %collective-permute-done), channel_id=1, source_target_pairs={{0,4},{1,5},{2,6},{3,7},{4,0},{5,1},{6,2},{7,3},{8,12},{9,13},{10,... | collective-permute-start | bytes 1277960 | tf_op jit(solution)/shard_map/ppermute | solution.py:415
  22.9 10.9 %collective-permute-start.4 = (bf16[208,1024]{1,0:T(8,128)(2,1)S(1)}, bf16[208,1024]{1,0:T(8,128)(2,1)S(1)}, u32[]{:S(2)}, u32[]{:S(2)}) collective-permute-start(bf16[208,1024]{1,0:T(8,128)(2,1)S(1)} %collective-permute-done), channel_id=1, source_target_pairs={{0,2},{1,3},{2,0},{3,1},{4,6},{5,7},{6,4},{7,5},{8,10},{9,11},{10,... | collective-permute-start | bytes 1277960 | tf_op jit(solution)/shard_map/ppermute | solution.py:415
  24.8 30.4 %copy-start.8 = (bf16[208,1024]{1,0:T(8,128)(2,1)}, bf16[208,1024]{1,0:T(8,128)(2,1)S(1)}, u32[]{:S(2)}) copy-start(bf16[208,1024]{1,0:T(8,128)(2,1)S(1)} %collective-permute-done.1) | copy-start | bytes 1277956
  24.8 17.2 %collective-permute-start.5 = (bf16[208,1024]{1,0:T(8,128)(2,1)S(1)}, bf16[208,1024]{1,0:T(8,128)(2,1)S(1)}, u32[]{:S(2)}, u32[]{:S(2)}) collective-permute-start(bf16[208,1024]{1,0:T(8,128)(2,1)S(1)} %collective-permute-done.1), channel_id=1, source_target_pairs={{0,2},{1,3},{2,0},{3,1},{4,6},{5,7},{6,4},{7,5},{8,10},{9,11},{10,... | collective-permute-start | bytes 1277960 | tf_op jit(solution)/shard_map/ppermute | solution.py:415
  25.1 30.2 %copy-start.4 = (bf16[208,1024]{1,0:T(8,128)(2,1)}, bf16[208,1024]{1,0:T(8,128)(2,1)S(1)}, u32[]{:S(2)}) copy-start(bf16[208,1024]{1,0:T(8,128)(2,1)S(1)} %collective-permute-done.3) | copy-start | bytes 1277956
  25.1 21.1 %collective-permute-start.8 = (bf16[208,1024]{1,0:T(8,128)(2,1)S(1)}, bf16[208,1024]{1,0:T(8,128)(2,1)S(1)}, u32[]{:S(2)}, u32[]{:S(2)}) collective-permute-start(bf16[208,1024]{1,0:T(8,128)(2,1)S(1)} %collective-permute-done), channel_id=1, source_target_pairs={{0,1},{1,0},{2,3},{3,2},{4,5},{5,4},{6,7},{7,6},{8,9},{9,8},{10,11... | collective-permute-start | bytes 1277960 | tf_op jit(solution)/shard_map/ppermute | solution.py:415
  27.1 28.2 %copy-start.2 = (bf16[208,1024]{1,0:T(8,128)(2,1)}, bf16[208,1024]{1,0:T(8,128)(2,1)S(1)}, u32[]{:S(2)}) copy-start(bf16[208,1024]{1,0:T(8,128)(2,1)S(1)} %collective-permute-done.7) | copy-start | bytes 1277956
  27.1 19.1 %collective-permute-start.9 = (bf16[208,1024]{1,0:T(8,128)(2,1)S(1)}, bf16[208,1024]{1,0:T(8,128)(2,1)S(1)}, u32[]{:S(2)}, u32[]{:S(2)}) collective-permute-start(bf16[208,1024]{1,0:T(8,128)(2,1)S(1)} %collective-permute-done.1), channel_id=1, source_target_pairs={{0,1},{1,0},{2,3},{3,2},{4,5},{5,4},{6,7},{7,6},{8,9},{9,8},{10,11... | collective-permute-start | bytes 1277960 | tf_op jit(solution)/shard_map/ppermute | solution.py:415
  33.5 20.0 %copy-start.18 = (bf16[208,1024]{1,0:T(8,128)(2,1)}, bf16[208,1024]{1,0:T(8,128)(2,1)S(1)}, u32[]{:S(2)}) copy-start(bf16[208,1024]{1,0:T(8,128)(2,1)S(1)} %collective-permute-done.2) | copy-start | bytes 1277956
  33.5 17.6 %collective-permute-start.6 = (bf16[208,1024]{1,0:T(8,128)(2,1)S(1)}, bf16[208,1024]{1,0:T(8,128)(2,1)S(1)}, u32[]{:S(2)}, u32[]{:S(2)}) collective-permute-start(bf16[208,1024]{1,0:T(8,128)(2,1)S(1)} %collective-permute-done.2), channel_id=1, source_target_pairs={{0,2},{1,3},{2,0},{3,1},{4,6},{5,7},{6,4},{7,5},{8,10},{9,11},{10,... | collective-permute-start | bytes 1277960 | tf_op jit(solution)/shard_map/ppermute | solution.py:415
  33.7 21.5 %copy-start.12 = (bf16[208,1024]{1,0:T(8,128)(2,1)}, bf16[208,1024]{1,0:T(8,128)(2,1)S(1)}, u32[]{:S(2)}) copy-start(bf16[208,1024]{1,0:T(8,128)(2,1)S(1)} %collective-permute-done.4) | copy-start | bytes 1277956
  33.7 19.6 %collective-permute-start.11 = (bf16[208,1024]{1,0:T(8,128)(2,1)S(1)}, bf16[208,1024]{1,0:T(8,128)(2,1)S(1)}, u32[]{:S(2)}, u32[]{:S(2)}) collective-permute-start(bf16[208,1024]{1,0:T(8,128)(2,1)S(1)} %collective-permute-done.3), channel_id=1, source_target_pairs={{0,1},{1,0},{2,3},{3,2},{4,5},{5,4},{6,7},{7,6},{8,9},{9,8},{10,11... | collective-permute-start | bytes 1277960 | tf_op jit(solution)/shard_map/ppermute | solution.py:415
  42.0 11.4 %copy-start.16 = (bf16[208,1024]{1,0:T(8,128)(2,1)}, bf16[208,1024]{1,0:T(8,128)(2,1)S(1)}, u32[]{:S(2)}) copy-start(bf16[208,1024]{1,0:T(8,128)(2,1)S(1)} %collective-permute-done.5) | copy-start | bytes 1277956
  42.0 11.4 %collective-permute-start.10 = (bf16[208,1024]{1,0:T(8,128)(2,1)S(1)}, bf16[208,1024]{1,0:T(8,128)(2,1)S(1)}, u32[]{:S(2)}, u32[]{:S(2)}) collective-permute-start(bf16[208,1024]{1,0:T(8,128)(2,1)S(1)} %collective-permute-done.2), channel_id=1, source_target_pairs={{0,1},{1,0},{2,3},{3,2},{4,5},{5,4},{6,7},{7,6},{8,9},{9,8},{10,11... | collective-permute-start | bytes 1277960 | tf_op jit(solution)/shard_map/ppermute | solution.py:415
  46.1 9.2 %copy-start.10 = (bf16[208,1024]{1,0:T(8,128)(2,1)}, bf16[208,1024]{1,0:T(8,128)(2,1)S(1)}, u32[]{:S(2)}) copy-start(bf16[208,1024]{1,0:T(8,128)(2,1)S(1)} %collective-permute-done.8) | copy-start | bytes 1277956
  46.1 7.3 %collective-permute-start.12 = (bf16[208,1024]{1,0:T(8,128)(2,1)S(1)}, bf16[208,1024]{1,0:T(8,128)(2,1)S(1)}, u32[]{:S(2)}, u32[]{:S(2)}) collective-permute-start(bf16[208,1024]{1,0:T(8,128)(2,1)S(1)} %collective-permute-done.4), channel_id=1, source_target_pairs={{0,1},{1,0},{2,3},{3,2},{4,5},{5,4},{6,7},{7,6},{8,9},{9,8},{10,11... | collective-permute-start | bytes 1277960 | tf_op jit(solution)/shard_map/ppermute | solution.py:415
  46.2 9.1 %copy-start.14 = (bf16[208,1024]{1,0:T(8,128)(2,1)}, bf16[208,1024]{1,0:T(8,128)(2,1)S(1)}, u32[]{:S(2)}) copy-start(bf16[208,1024]{1,0:T(8,128)(2,1)S(1)} %collective-permute-done.9) | copy-start | bytes 1277956
  46.2 7.2 %collective-permute-start.13 = (bf16[208,1024]{1,0:T(8,128)(2,1)S(1)}, bf16[208,1024]{1,0:T(8,128)(2,1)S(1)}, u32[]{:S(2)}, u32[]{:S(2)}) collective-permute-start(bf16[208,1024]{1,0:T(8,128)(2,1)S(1)} %collective-permute-done.5), channel_id=1, source_target_pairs={{0,1},{1,0},{2,3},{3,2},{4,5},{5,4},{6,7},{7,6},{8,9},{9,8},{10,11... | collective-permute-start | bytes 1277960 | tf_op jit(solution)/shard_map/ppermute | solution.py:415
  51.1 2.4 copy-start.26
  51.1 4.2 %collective-permute-start.14 = (bf16[208,1024]{1,0:T(8,128)(2,1)S(1)}, bf16[208,1024]{1,0:T(8,128)(2,1)}, u32[]{:S(2)}, u32[]{:S(2)}) collective-permute-start(bf16[208,1024]{1,0:T(8,128)(2,1)S(1)} %collective-permute-done.6), channel_id=1, source_target_pairs={{0,1},{1,0},{2,3},{3,2},{4,5},{5,4},{6,7},{7,6},{8,9},{9,8},{10,11... | collective-permute-start | bytes 1277960 | tf_op jit(solution)/shard_map/ppermute | solution.py:415
  53.4 0.8 copy-start.20
  53.4 0.9 copy-start.24
  53.4 1.0 copy-start.22
  54.4 0.8 copy-start.28
  55.3 75.9 %all-to-all-start = ((bf16[16,192,512]{2,1,0:T(8,128)(2,1)}), bf16[16,192,512]{2,1,0:T(8,128)(2,1)S(1)}, u32[]{:S(2)}, u32[]{:S(2)}) async-start(bf16[16,192,512]{2,1,0:T(8,128)(2,1)} %shard_map.95), calls=%async_computation | async-start | bytes 6291456 | tf_op jit(solution)/shard_map/all_to_all | solution.py:428
  61.3 3.9 %copy-start.1 = (bf16[208,1024]{1,0:T(8,128)(2,1)S(1)}, bf16[208,1024]{1,0:T(8,128)(2,1)}, u32[]{:S(2)}) copy-start(bf16[208,1024]{1,0:T(8,128)(2,1)} %shard_map.94) | copy-start | bytes 1277956
  61.3 4.7 %copy-start.7 = (bf16[208,1024]{1,0:T(8,128)(2,1)S(1)}, bf16[208,1024]{1,0:T(8,128)(2,1)}, u32[]{:S(2)}) copy-start(bf16[208,1024]{1,0:T(8,128)(2,1)} %copy-done.6) | copy-start | bytes 1277956
  61.3 5.5 %copy-start.9 = (bf16[208,1024]{1,0:T(8,128)(2,1)S(1)}, bf16[208,1024]{1,0:T(8,128)(2,1)}, u32[]{:S(2)}) copy-start(bf16[208,1024]{1,0:T(8,128)(2,1)} %copy-done.8) | copy-start | bytes 1277956
  61.4 6.3 %copy-start.19 = (bf16[208,1024]{1,0:T(8,128)(2,1)S(1)}, bf16[208,1024]{1,0:T(8,128)(2,1)}, u32[]{:S(2)}) copy-start(bf16[208,1024]{1,0:T(8,128)(2,1)} %copy-done.18) | copy-start | bytes 1277956
  61.4 7.1 %copy-start.5 = (bf16[208,1024]{1,0:T(8,128)(2,1)S(1)}, bf16[208,1024]{1,0:T(8,128)(2,1)}, u32[]{:S(2)}) copy-start(bf16[208,1024]{1,0:T(8,128)(2,1)} %copy-done.4) | copy-start | bytes 1277956
  61.4 7.9 %copy-start.13 = (bf16[208,1024]{1,0:T(8,128)(2,1)S(1)}, bf16[208,1024]{1,0:T(8,128)(2,1)}, u32[]{:S(2)}) copy-start(bf16[208,1024]{1,0:T(8,128)(2,1)} %copy-done.12) | copy-start | bytes 1277956
  61.4 8.7 %copy-start.17 = (bf16[208,1024]{1,0:T(8,128)(2,1)S(1)}, bf16[208,1024]{1,0:T(8,128)(2,1)}, u32[]{:S(2)}) copy-start(bf16[208,1024]{1,0:T(8,128)(2,1)} %copy-done.16) | copy-start | bytes 1277956
  61.4 9.5 %copy-start.27 = (bf16[208,1024]{1,0:T(8,128)(2,1)S(1)}, bf16[208,1024]{1,0:T(8,128)(2,1)}, u32[]{:S(2)}) copy-start(bf16[208,1024]{1,0:T(8,128)(2,1)} %copy-done.26) | copy-start | bytes 1277956
  61.4 10.2 %copy-start.3 = (bf16[208,1024]{1,0:T(8,128)(2,1)S(1)}, bf16[208,1024]{1,0:T(8,128)(2,1)}, u32[]{:S(2)}) copy-start(bf16[208,1024]{1,0:T(8,128)(2,1)} %copy-done.2) | copy-start | bytes 1277956
  61.4 11.0 %copy-start.11 = (bf16[208,1024]{1,0:T(8,128)(2,1)S(1)}, bf16[208,1024]{1,0:T(8,128)(2,1)}, u32[]{:S(2)}) copy-start(bf16[208,1024]{1,0:T(8,128)(2,1)} %copy-done.10) | copy-start | bytes 1277956
  61.4 11.8 %copy-start.15 = (bf16[208,1024]{1,0:T(8,128)(2,1)S(1)}, bf16[208,1024]{1,0:T(8,128)(2,1)}, u32[]{:S(2)}) copy-start(bf16[208,1024]{1,0:T(8,128)(2,1)} %copy-done.14) | copy-start | bytes 1277956
  61.4 12.6 %copy-start.25 = (bf16[208,1024]{1,0:T(8,128)(2,1)S(1)}, bf16[208,1024]{1,0:T(8,128)(2,1)}, u32[]{:S(2)}) copy-start(bf16[208,1024]{1,0:T(8,128)(2,1)} %copy-done.24) | copy-start | bytes 1277956
  65.2 9.6 %copy-start.21 = (bf16[208,1024]{1,0:T(8,128)(2,1)S(1)}, bf16[208,1024]{1,0:T(8,128)(2,1)}, u32[]{:S(2)}) copy-start(bf16[208,1024]{1,0:T(8,128)(2,1)} %copy-done.20) | copy-start | bytes 1277956
  65.2 10.4 %copy-start.23 = (bf16[208,1024]{1,0:T(8,128)(2,1)S(1)}, bf16[208,1024]{1,0:T(8,128)(2,1)}, u32[]{:S(2)}) copy-start(bf16[208,1024]{1,0:T(8,128)(2,1)} %copy-done.22) | copy-start | bytes 1277956
  65.2 11.2 %copy-start.29 = (bf16[208,1024]{1,0:T(8,128)(2,1)S(1)}, bf16[208,1024]{1,0:T(8,128)(2,1)}, u32[]{:S(2)}) copy-start(bf16[208,1024]{1,0:T(8,128)(2,1)} %copy-done.28) | copy-start | bytes 1277956
  131.2 1.7 copy-start
  147.0 86.1 %all-to-all-start.1 = ((bf16[16,224,512]{2,1,0:T(8,128)(2,1)}), bf16[16,224,512]{2,1,0:T(8,128)(2,1)}, u32[]{:S(2)}, u32[]{:S(2)}) async-start(bf16[16,224,512]{2,1,0:T(8,128)(2,1)} %shard_map.97), calls=%async_computation.1 | async-start | bytes 7340032 | tf_op jit(solution)/shard_map/all_to_all | solution.py:428

commit v3 on v2

--- a/solution.py
+++ b/solution.py
@@ -142,7 +142,7 @@
         payload_kernel,
         in_specs=[vmem, vmem, vmem, pl.BlockSpec(memory_space=pltpu.SMEM)],
         out_shape=jax.ShapeDtypeStruct((total, cotangent.shape[1]), jnp.bfloat16),
-        compiler_params=params(58),
+        compiler_params=params(56),
         cost_estimate=pl.CostEstimate(flops=0, bytes_accessed=1 << 20, transcendentals=0),
     )(cotangent, up, index, adapters)
 
@@ -169,7 +169,7 @@
         ],
         out_specs=pl.BlockSpec((2, rows + rank, share), lambda d: (d, 0, 0)),
         out_shape=jax.ShapeDtypeStruct((peer_count, rows + rank, share), jnp.bfloat16),
-        compiler_params=params(58),
+        compiler_params=params(56),
         cost_estimate=pl.CostEstimate(flops=0, bytes_accessed=6 << 20, transcendentals=0),
     )(features, down)
 
@@ -184,11 +184,11 @@
     cot = cot_ref[...].reshape(-1, keys)
     slot = jnp.floor(place_columns(place_ref[...]) / CAPACITY)
     low = contract_matrices(cot, up_ref[...].reshape(-1, keys), 1, 1)
+    total = jnp.zeros_like(slot)
     for j in range(low.shape[1] // LANES):
         span = slice(j * LANES, (j + 1) * LANES)
-        low_ref[:, span] = jnp.where(slot == adapter_lanes(j), low[:, span], 0.0).astype(
-            jnp.bfloat16
-        )
+        total = total + jnp.where(slot == adapter_lanes(j), low[:, span], 0.0)
+    low_ref[...] = (total + pltpu.roll(total, LANES // 2, 1)).astype(jnp.bfloat16)
     base_ref[...] = contract_matrices(cot, weight_ref[...], 1, 1)
 
 
@@ -196,7 +196,6 @@
     peer_count, _, keys = gathered.shape
     share = weight.shape[0]
     block = STEP * rows
-    slots = peer_count * rank
     once = pl.Buffered(1)
     return pl.pallas_call(
         low_out_kernel,
@@ -212,14 +211,14 @@
             pl.BlockSpec((share, keys), lambda s: (0, 0), pipeline_mode=once),
         ],
         out_specs=[
-            pl.BlockSpec((block, slots), lambda s: (s, 0)),
+            pl.BlockSpec((block, LANES), lambda s: (s, 0)),
             pl.BlockSpec((block, share), lambda s: (s, 0)),
         ],
         out_shape=[
-            jax.ShapeDtypeStruct((peer_count * rows, slots), jnp.bfloat16),
+            jax.ShapeDtypeStruct((peer_count * rows, LANES), jnp.bfloat16),
             jax.ShapeDtypeStruct((peer_count * rows, share), jnp.float32),
         ],
-        compiler_params=params(58),
+        compiler_params=params(56),
         cost_estimate=pl.CostEstimate(flops=7 << 30, bytes_accessed=16 << 20, transcendentals=0),
     )(gathered, gathered, gathered, weight)
 
@@ -228,29 +227,30 @@
     step = pl.program_id(0)
     items, rows, share = feat_ref.shape
     peers, rank, _ = down_ref.shape
+
+    @pl.when(step == 0)
+    def _():
+        grad_ref[...] = jnp.zeros_like(grad_ref)
+
     down = down_ref[...].reshape(-1, share)
     feat = feat_ref[...].reshape(-1, share)
-    low = low_ref[...]
+    place = place_columns(place_ref[...])
+    slot = jnp.floor(place / CAPACITY)
+    folded = low_ref[...].astype(jnp.float32)
+    partial = contract_matrices(feat, down, 1, 1)
+    total = jnp.zeros_like(place)
+    spread_low = []
+    for j in range(partial.shape[1] // LANES):
+        span = slice(j * LANES, (j + 1) * LANES)
+        mine = slot == adapter_lanes(j)
+        total = total + jnp.where(mine, partial[:, span], 0.0)
+        spread_low.append(jnp.where(mine, folded, 0.0).astype(jnp.bfloat16))
+    low = jnp.concatenate(spread_low, axis=1)
+    grad_ref[...] += contract_matrices(low, feat, 0, 0)
     grad = base_ref[...] + adapter_scale * contract_matrices(low, down, 1, 0)
     out_ref[pl.ds(step * items, items), :rows, :] = grad.astype(jnp.bfloat16).reshape(
         items, rows, share
     )
-
-    @pl.when(step == 0)
-    def _():
-        grad_ref[...] = contract_matrices(low, feat, 0, 0)
-
-    @pl.when(step > 0)
-    def _():
-        grad_ref[...] += contract_matrices(low, feat, 0, 0)
-
-    partial = contract_matrices(feat, down, 1, 1)
-    place = place_columns(place_ref[...])
-    slot = jnp.floor(place / CAPACITY)
-    total = jnp.zeros_like(place)
-    for j in range(partial.shape[1] // LANES):
-        span = slice(j * LANES, (j + 1) * LANES)
-        total = total + jnp.where(slot == adapter_lanes(j), partial[:, span], 0.0)
     total = (total + pltpu.roll(total, LANES // 2, 1)).astype(jnp.bfloat16)
     places = lax.broadcasted_iota(jnp.int32, (peers * CAPACITY, LANES), 0).astype(jnp.float32)
     picked = []
@@ -294,13 +294,13 @@
             pl.BlockSpec(
                 (STEP, INDEX_ROWS, keys), lambda s: (s, (rows + rank) // INDEX_ROWS, 0)
             ),
-            pl.BlockSpec((block, slots), lambda s: (s, 0)),
+            pl.BlockSpec((block, LANES), lambda s: (s, 0)),
             pl.BlockSpec((block, share), lambda s: (s, 0)),
         ],
         out_specs=pl.BlockSpec((peer_count, total, share), lambda s: (0, 0, 0)),
         out_shape=jax.ShapeDtypeStruct((peer_count, total, share), jnp.bfloat16),
         scratch_shapes=[pltpu.VMEM((slots, share), jnp.float32)],
-        compiler_params=params(58),
+        compiler_params=params(56),
         cost_estimate=pl.CostEstimate(flops=7 << 30, bytes_accessed=16 << 20, transcendentals=0),
     )(received, received, gathered, low, base)
 
@@ -350,7 +350,7 @@
             jax.ShapeDtypeStruct((peer_count * CAPACITY, keys), jnp.bfloat16),
             jax.ShapeDtypeStruct((1, LANES), jnp.float32),
         ],
-        compiler_params=params(58),
+        compiler_params=params(56),
         cost_estimate=pl.CostEstimate(flops=1 << 29, bytes_accessed=8 << 20, transcendentals=0),
     )(own, gathered, gathered)
 
@@ -405,7 +405,7 @@
             jax.ShapeDtypeStruct((rank, keys), jnp.float32),
         ],
         scratch_shapes=[pltpu.VMEM((2 * CAPACITY, share), jnp.float32)],
-        compiler_params=params(58),
+        compiler_params=params(56),
         cost_estimate=pl.CostEstimate(flops=1 << 27, bytes_accessed=8 << 20, transcendentals=0),
     )(parts, chosen, scale)
 
@@ -421,7 +421,11 @@
     held = [(0, payload), (far, mirrored)]
     for mask in (near, beside, core):
         held = held + [(shift ^ mask, swap(block, mask)) for shift, block in held]
-    return lax.optimization_barrier((packed, held))
+    for place in [6, 7]:
+        shift, block = held[place]
+        packed, block = lax.optimization_barrier((packed, block))
+        held[place] = (shift, block)
+    return packed, held
 
 
 def exchange(block):

time: 239 us -> 225 us (0.941)
  local copies, waits for them, and re-layouts: 21.1 us -> 6.39 us
  waiting for transfers between devices: 145 us -> 155 us
  starting transfers between devices: 29.3 us -> 22.6 us
    ppermute x15, waiting for transfers between devices: 26.2 us -> 67 us  [swap(): lax.ppermute(block, 'wide', [(i, i ^ mask) for i in range(peer_count)])]
    all_to_all x2, waiting for transfers between devices: 118 us -> 87.6 us  [exchange(): lax.all_to_all(block, 'wide', split_axis=0, concat_axis=0, tiled=True)]
    dynamic_update_slice x16, local copies, waits for them, and re-layouts: 13.7 us -> 2.61 us  [column_body(): lax.dynamic_update_slice(gathered, block[None], (device_index ^ shift, 0,...]
    ppermute x15, starting transfers between devices: 18.4 us -> 10 us  [swap(): lax.ppermute(block, 'wide', [(i, i ^ mask) for i in range(peer_count)])]
    broadcast_in_dim x1, local copies, waits for them, and re-layouts: 3.77 us -> 0.86 us  [column_body(): gathered = jnp.zeros((peer_count,) + payload.shape, payload.dtype)]
  transfers between devices with their start and end apart: 17 -> 17, of which waited for: 7 -> 11; matrix products, arithmetic and copies ran while one was open for 7% -> 2% of each run, Pallas kernels for 9% -> 9%
where the time goes in v3:
time: 225 us
  waiting for transfers between devices  155 us (69%)
  Pallas kernels  40.2 us (18%)
  starting transfers between devices  22.6 us (10%)
  local copies, waits for them, and re-layouts  6.39 us (3%)
    all_to_all x2, waiting for transfers between devices, exchange(): lax.all_to_all(block, 'wide', split_axis=0, concat_axis=0, tiled=True)  87.6 us
    ppermute x15, waiting for transfers between devices, swap(): lax.ppermute(block, 'wide', [(i, i ^ mask) for i in range(peer_count)])  67 us
    all_to_all x2, starting transfers between devices, exchange(): lax.all_to_all(block, 'wide', split_axis=0, concat_axis=0, tiled=True)  12.5 us
    pallas_call x1, Pallas kernels, share_results(): pl.pallas_call(share_kernel, grid=(peer_count // STEP,), in_specs=[pl.Blo...  11.8 us
    pallas_call x1, Pallas kernels, low_out(): pl.pallas_call(low_out_kernel, grid=(peer_count // STEP,), in_specs=[pl.B...  10.6 us
    ppermute x15, starting transfers between devices, swap(): lax.ppermute(block, 'wide', [(i, i ^ mask) for i in range(peer_count)])  10 us
    pallas_call x1, Pallas kernels, pack_columns(): pl.pallas_call(pack_kernel, grid=(peer_count // 2,), in_specs=[pl.BlockSp...  6.11 us
    pallas_call x1, Pallas kernels, finish(): pl.pallas_call(finish_kernel, grid=(peer_count // STEP,), in_specs=[pl.Bl...  5.18 us
  transfers between devices with their start and end apart: 17, of which 11 were waited for; matrix products, arithmetic and copies ran while one was open for 2% of the time, Pallas kernels for 9%

profile of v3, /device:TPU:11, one launch (start us, length us, event | category | flops | bytes accessed | tf_op | source)
XLA Modules:
  0.0 224.6 jit_solution(10822520941291362768)
XLA Ops:
  0.6 2.0 shard_map.94
  2.7 1.3 collective-permute-start
  4.0 2.2 collective-permute-start.1
  6.2 6.1 %shard_map.95 = bf16[16,192,512]{2,1,0:T(8,128)(2,1)} custom-call(bf16[128,8192]{1,0:T(8,128)(2,1)} %features_ref.1, bf16[64,8192]{1,0:T(8,128)(2,1)} %bitcast.42), custom_call_target="tpu_custom_call" | custom-call | bytes 6291456 | tf_op jit(solution)/shard_map/pallas_call | solution.py:163
  12.3 10.5 %collective-permute-done = bf16[208,1024]{1,0:T(8,128)(2,1)S(1)} collective-permute-done((bf16[208,1024]{1,0:T(8,128)(2,1)}, bf16[208,1024]{1,0:T(8,128)(2,1)S(1)}, u32[]{:S(2)}, u32[]{:S(2)}) %collective-permute-start) | collective-permute-done | bytes 426016 | tf_op jit(solution)/shard_map/ppermute | solution.py:415
  22.8 0.0 collective-permute-start.3
  22.8 2.0 collective-permute-done.1
  24.8 0.3 collective-permute-start.2
  25.1 0.0 copy-done.6
  25.1 8.4 %collective-permute-done.3 = bf16[208,1024]{1,0:T(8,128)(2,1)S(1)} collective-permute-done((bf16[208,1024]{1,0:T(8,128)(2,1)S(1)}, bf16[208,1024]{1,0:T(8,128)(2,1)S(1)}, u32[]{:S(2)}, u32[]{:S(2)}) %collective-permute-start.3) | collective-permute-done | bytes 426016 | tf_op jit(solution)/shard_map/ppermute | solution.py:415
  33.5 0.3 collective-permute-start.4
  33.7 0.6 collective-permute-done.2
  34.3 9.5 %collective-permute-done.4 = bf16[208,1024]{1,0:T(8,128)(2,1)S(1)} collective-permute-done((bf16[208,1024]{1,0:T(8,128)(2,1)S(1)}, bf16[208,1024]{1,0:T(8,128)(2,1)S(1)}, u32[]{:S(2)}, u32[]{:S(2)}) %collective-permute-start.4) | collective-permute-done | bytes 426016 | tf_op jit(solution)/shard_map/ppermute | solution.py:415
  43.7 7.7 %all-to-all-start = ((bf16[16,192,512]{2,1,0:T(8,128)(2,1)}), bf16[16,192,512]{2,1,0:T(8,128)(2,1)}, u32[]{:S(2)}, u32[]{:S(2)}) async-start(bf16[16,192,512]{2,1,0:T(8,128)(2,1)} %shard_map.95), calls=%async_computation | async-start | bytes 6291456 | tf_op jit(solution)/shard_map/all_to_all | solution.py:432
  51.5 0.0 copy-done.1
  51.5 0.3 collective-permute-start.5
  51.8 0.6 collective-permute-start.7
  52.4 0.9 broadcast_in_dim.60
  53.4 0.1 copy-done.7
  53.4 1.2 collective-permute-start.6
  54.6 0.3 collective-permute-start.8
  54.9 0.2 collective-permute-start.9
  55.2 23.6 %collective-permute-done.5 = bf16[208,1024]{1,0:T(8,128)(2,1)} collective-permute-done((bf16[208,1024]{1,0:T(8,128)(2,1)S(1)}, bf16[208,1024]{1,0:T(8,128)(2,1)}, u32[]{:S(2)}, u32[]{:S(2)}) %collective-permute-start.5) | collective-permute-done | bytes 426016 | tf_op jit(solution)/shard_map/ppermute | solution.py:415
  78.8 1.3 collective-permute-start.11
  80.3 1.0 bitcast_dynamic-update-slice_fusion.11
  81.3 10.8 %collective-permute-done.6 = bf16[208,1024]{1,0:T(8,128)(2,1)S(1)} collective-permute-done((bf16[208,1024]{1,0:T(8,128)(2,1)S(1)}, bf16[208,1024]{1,0:T(8,128)(2,1)S(1)}, u32[]{:S(2)}, u32[]{:S(2)}) %collective-permute-start.6) | collective-permute-done | bytes 426016 | tf_op jit(solution)/shard_map/ppermute | solution.py:415
  92.1 1.3 collective-permute-start.10
  93.6 0.0 collective-permute-done.7
  93.6 0.1 collective-permute-start.12
  93.7 1.0 bitcast_dynamic-update-slice_fusion.7
  94.7 0.0 collective-permute-done.8
  94.7 0.6 collective-permute-start.13
  95.3 0.0 collective-permute-done.9
  95.3 0.1 collective-permute-start.14
  95.4 0.0 collective-permute-done.10
  95.5 0.0 collective-permute-done.11
  95.6 0.0 collective-permute-done.12
  95.6 1.0 collective-permute-done.13
  96.7 0.6 collective-permute-done.14
  97.3 0.0 copy-start
  97.3 2.8 %copy-done = bf16[16,208,1024]{2,1,0:T(8,128)(2,1)} copy-done((bf16[16,208,1024]{2,1,0:T(8,128)(2,1)}, bf16[16,208,1024]{2,1,0:T(8,128)(2,1)S(1)}, u32[]{:S(2)}) %copy-start) | copy-done | bytes 6815768
  100.1 10.6 %shard_map.96 = (bf16[2048,128]{1,0:T(8,128)(2,1)}, f32[2048,512]{1,0:T(8,128)}) custom-call(bf16[16,208,1024]{2,1,0:T(8,128)(2,1)} %copy-done, bf16[16,208,1024]{2,1,0:T(8,128)(2,1)} %copy-done, bf16[16,208,1024]{2,1,0:T(8,128)(2,1)} %copy-done, bf16[512,1024]{1,0:T(8,128)(2,1)} %weight_ref.1), custom_call_target="tpu_custom_call" | custom-call | flops 7516192768 | bytes 16777216 | tf_op jit(solution)/shard_map/pallas_call | solution.py:200
  110.8 10.9 %all-to-all-done.feat_ref.down_ref = bf16[16,192,512]{2,1,0:T(8,128)(2,1)} async-done(((bf16[16,192,512]{2,1,0:T(8,128)(2,1)}), bf16[16,192,512]{2,1,0:T(8,128)(2,1)}, u32[]{:S(2)}, u32[]{:S(2)}) %all-to-all-start) | async-done | bytes 3145760 | tf_op jit(solution)/shard_map/all_to_all | solution.py:432
  121.6 11.8 %shard_map.97 = bf16[16,224,512]{2,1,0:T(8,128)(2,1)} custom-call(bf16[16,192,512]{2,1,0:T(8,128)(2,1)} %all-to-all-done.feat_ref.down_ref, bf16[16,192,512]{2,1,0:T(8,128)(2,1)} %all-to-all-done.feat_ref.down_ref, bf16[16,208,1024]{2,1,0:T(8,128)(2,1)} %copy-done, bf16[2048,128]{1,0:T(8,128)(2,1)} %get-tuple-element.22.low_ref, ...), custom_call_target="tpu_custom_call" | custom-call | flops 7516192768 | bytes 16777216 | tf_op jit(solution)/shard_map/pallas_call | solution.py:286
  133.4 4.8 %all-to-all-start.1 = ((bf16[16,224,512]{2,1,0:T(8,128)(2,1)}), bf16[16,224,512]{2,1,0:T(8,128)(2,1)}, u32[]{:S(2)}, u32[]{:S(2)}) async-start(bf16[16,224,512]{2,1,0:T(8,128)(2,1)} %shard_map.97), calls=%async_computation.1 | async-start | bytes 7340032 | tf_op jit(solution)/shard_map/all_to_all | solution.py:432
  138.2 4.5 %shard_map.98 = (bf16[256,1024]{1,0:T(8,128)(2,1)}, f32[1,128]{1,0:T(1,128)}) custom-call(s32[1]{0:T(128)} %bitcast.20.own_ref, bf16[16,208,1024]{2,1,0:T(8,128)(2,1)} %copy-done, bf16[16,208,1024]{2,1,0:T(8,128)(2,1)} %copy-done), custom_call_target="tpu_custom_call" | custom-call | flops 536870912 | bytes 8388608 | tf_op jit(solution)/shard_map/pallas_call | solution.py:335
  142.7 76.8 %all-to-all-done.1.part_ref = bf16[16,224,512]{2,1,0:T(8,128)(2,1)} async-done(((bf16[16,224,512]{2,1,0:T(8,128)(2,1)}), bf16[16,224,512]{2,1,0:T(8,128)(2,1)}, u32[]{:S(2)}, u32[]{:S(2)}) %all-to-all-start.1) | async-done | bytes 3670048 | tf_op jit(solution)/shard_map/all_to_all | solution.py:432
  219.5 5.2 %shard_map.99 = (bf16[128,8192]{1,0:T(8,128)(2,1)}, f32[64,8192]{1,0:T(8,128)}, f32[64,1024]{1,0:T(8,128)}) custom-call(bf16[16,224,512]{2,1,0:T(8,128)(2,1)} %all-to-all-done.1.part_ref, bf16[256,1024]{1,0:T(8,128)(2,1)} %get-tuple-element.24.cot_ref, f32[1,128]{1,0:T(1,128)} %get-tuple-element.25.scale_ref), custom_call_target="tpu_custom_call" | custom-call | flops 134217728 | bytes 8388608 | tf_op jit(solution)/shard_map/pallas_call | solution.py:389
  (25 shorter events, 0.5 us)
Async XLA Ops:
  2.7 48.8 %copy-start.1 = (bf16[208,1024]{1,0:T(8,128)(2,1)S(1)}, bf16[208,1024]{1,0:T(8,128)(2,1)}, u32[]{:S(2)}) copy-start(bf16[208,1024]{1,0:T(8,128)(2,1)} %shard_map.94) | copy-start | bytes 1277956
  2.7 20.1 %collective-permute-start = (bf16[208,1024]{1,0:T(8,128)(2,1)}, bf16[208,1024]{1,0:T(8,128)(2,1)S(1)}, u32[]{:S(2)}, u32[]{:S(2)}) collective-permute-start(bf16[208,1024]{1,0:T(8,128)(2,1)} %shard_map.94), channel_id=1, source_target_pairs={{0,12},{1,13},{2,14},{3,15},{4,8},{5,9},{6,10},{7,11},{8,4},{9,5},... | collective-permute-start | bytes 1277960 | tf_op jit(solution)/shard_map/ppermute | solution.py:415
  4.0 20.8 %collective-permute-start.1 = (bf16[208,1024]{1,0:T(8,128)(2,1)}, bf16[208,1024]{1,0:T(8,128)(2,1)S(1)}, u32[]{:S(2)}, u32[]{:S(2)}) collective-permute-start(bf16[208,1024]{1,0:T(8,128)(2,1)} %shard_map.94), channel_id=1, source_target_pairs={{0,4},{1,5},{2,6},{3,7},{4,0},{5,1},{6,2},{7,3},{8,12},{9,13},{10,... | collective-permute-start | bytes 1277960 | tf_op jit(solution)/shard_map/ppermute | solution.py:415
  22.8 2.3 %copy-start.6 = (bf16[208,1024]{1,0:T(8,128)(2,1)}, bf16[208,1024]{1,0:T(8,128)(2,1)S(1)}, u32[]{:S(2)}) copy-start(bf16[208,1024]{1,0:T(8,128)(2,1)S(1)} %collective-permute-done) | copy-start | bytes 1277956
  22.8 10.7 %collective-permute-start.3 = (bf16[208,1024]{1,0:T(8,128)(2,1)S(1)}, bf16[208,1024]{1,0:T(8,128)(2,1)S(1)}, u32[]{:S(2)}, u32[]{:S(2)}) collective-permute-start(bf16[208,1024]{1,0:T(8,128)(2,1)S(1)} %collective-permute-done), channel_id=1, source_target_pairs={{0,4},{1,5},{2,6},{3,7},{4,0},{5,1},{6,2},{7,3},{8,12},{9,13},{10,... | collective-permute-start | bytes 1277960 | tf_op jit(solution)/shard_map/ppermute | solution.py:415
  24.8 9.5 %copy-start.4 = (bf16[208,1024]{1,0:T(8,128)(2,1)}, bf16[208,1024]{1,0:T(8,128)(2,1)S(1)}, u32[]{:S(2)}) copy-start(bf16[208,1024]{1,0:T(8,128)(2,1)S(1)} %collective-permute-done.1) | copy-start | bytes 1277956
  24.8 9.5 %collective-permute-start.2 = (bf16[208,1024]{1,0:T(8,128)(2,1)S(1)}, bf16[208,1024]{1,0:T(8,128)(2,1)S(1)}, u32[]{:S(2)}, u32[]{:S(2)}) collective-permute-start(bf16[208,1024]{1,0:T(8,128)(2,1)S(1)} %collective-permute-done.1), channel_id=1, source_target_pairs={{0,2},{1,3},{2,0},{3,1},{4,6},{5,7},{6,4},{7,5},{8,10},{9,11},{10,... | collective-permute-start | bytes 1277960 | tf_op jit(solution)/shard_map/ppermute | solution.py:415
  33.5 0.8 copy-start.2
  33.5 10.3 %collective-permute-start.4 = (bf16[208,1024]{1,0:T(8,128)(2,1)S(1)}, bf16[208,1024]{1,0:T(8,128)(2,1)S(1)}, u32[]{:S(2)}, u32[]{:S(2)}) collective-permute-start(bf16[208,1024]{1,0:T(8,128)(2,1)S(1)} %collective-permute-done.3), channel_id=1, source_target_pairs={{0,2},{1,3},{2,0},{3,1},{4,6},{5,7},{6,4},{7,5},{8,10},{9,11},{10,... | collective-permute-start | bytes 1277960 | tf_op jit(solution)/shard_map/ppermute | solution.py:415
  43.7 77.9 %all-to-all-start = ((bf16[16,192,512]{2,1,0:T(8,128)(2,1)}), bf16[16,192,512]{2,1,0:T(8,128)(2,1)}, u32[]{:S(2)}, u32[]{:S(2)}) async-start(bf16[16,192,512]{2,1,0:T(8,128)(2,1)} %shard_map.95), calls=%async_computation | async-start | bytes 6291456 | tf_op jit(solution)/shard_map/all_to_all | solution.py:432
  51.5 27.3 %collective-permute-start.5 = (bf16[208,1024]{1,0:T(8,128)(2,1)S(1)}, bf16[208,1024]{1,0:T(8,128)(2,1)}, u32[]{:S(2)}, u32[]{:S(2)}) collective-permute-start(bf16[208,1024]{1,0:T(8,128)(2,1)S(1)} %copy-done.1), channel_id=1, source_target_pairs={{0,2},{1,3},{2,0},{3,1},{4,6},{5,7},{6,4},{7,5},{8,10},{9,11},{10,... | collective-permute-start | bytes 1277960 | tf_op jit(solution)/shard_map/ppermute | solution.py:415
  51.8 41.8 %collective-permute-start.7 = (bf16[208,1024]{1,0:T(8,128)(2,1)S(1)}, bf16[208,1024]{1,0:T(8,128)(2,1)}, u32[]{:S(2)}, u32[]{:S(2)}) collective-permute-start(bf16[208,1024]{1,0:T(8,128)(2,1)S(1)} %copy-done.1), channel_id=1, source_target_pairs={{0,1},{1,0},{2,3},{3,2},{4,5},{5,4},{6,7},{7,6},{8,9},{9,8},{10,11... | collective-permute-start | bytes 1277960 | tf_op jit(solution)/shard_map/ppermute | solution.py:415
  52.4 1.0 copy-start.7
  52.4 2.5 %copy-start.5 = (bf16[208,1024]{1,0:T(8,128)(2,1)S(1)}, bf16[208,1024]{1,0:T(8,128)(2,1)}, u32[]{:S(2)}) copy-start(bf16[208,1024]{1,0:T(8,128)(2,1)} %copy-done.4) | copy-start | bytes 1277956
  52.4 27.8 %copy-start.3 = (bf16[208,1024]{1,0:T(8,128)(2,1)S(1)}, bf16[208,1024]{1,0:T(8,128)(2,1)}, u32[]{:S(2)}) copy-start(bf16[208,1024]{1,0:T(8,128)(2,1)} %copy-done.2) | copy-start | bytes 1277956
  53.4 38.7 %collective-permute-start.6 = (bf16[208,1024]{1,0:T(8,128)(2,1)S(1)}, bf16[208,1024]{1,0:T(8,128)(2,1)S(1)}, u32[]{:S(2)}, u32[]{:S(2)}) collective-permute-start(bf16[208,1024]{1,0:T(8,128)(2,1)S(1)} %copy-done.7), channel_id=1, source_target_pairs={{0,2},{1,3},{2,0},{3,1},{4,6},{5,7},{6,4},{7,5},{8,10},{9,11},{10,... | collective-permute-start | bytes 1277960 | tf_op jit(solution)/shard_map/ppermute | solution.py:415
  54.6 40.1 %collective-permute-start.8 = (bf16[208,1024]{1,0:T(8,128)(2,1)S(1)}, bf16[208,1024]{1,0:T(8,128)(2,1)S(1)}, u32[]{:S(2)}, u32[]{:S(2)}) collective-permute-start(bf16[208,1024]{1,0:T(8,128)(2,1)S(1)} %copy-done.7), channel_id=1, source_target_pairs={{0,1},{1,0},{2,3},{3,2},{4,5},{5,4},{6,7},{7,6},{8,9},{9,8},{10,11... | collective-permute-start | bytes 1277960 | tf_op jit(solution)/shard_map/ppermute | solution.py:415
  54.9 40.4 %collective-permute-start.9 = (bf16[208,1024]{1,0:T(8,128)(2,1)S(1)}, bf16[208,1024]{1,0:T(8,128)(2,1)S(1)}, u32[]{:S(2)}, u32[]{:S(2)}) collective-permute-start(bf16[208,1024]{1,0:T(8,128)(2,1)S(1)} %copy-done.5), channel_id=1, source_target_pairs={{0,1},{1,0},{2,3},{3,2},{4,5},{5,4},{6,7},{7,6},{8,9},{9,8},{10,11... | collective-permute-start | bytes 1277960 | tf_op jit(solution)/shard_map/ppermute | solution.py:415
  78.8 16.7 %collective-permute-start.11 = (bf16[208,1024]{1,0:T(8,128)(2,1)}, bf16[208,1024]{1,0:T(8,128)(2,1)S(1)}, u32[]{:S(2)}, u32[]{:S(2)}) collective-permute-start(bf16[208,1024]{1,0:T(8,128)(2,1)} %collective-permute-done.5), channel_id=1, source_target_pairs={{0,1},{1,0},{2,3},{3,2},{4,5},{5,4},{6,7},{7,6},{8,9},{9,8},{10,11... | collective-permute-start | bytes 1277960 | tf_op jit(solution)/shard_map/ppermute | solution.py:415
  92.1 3.3 %collective-permute-start.10 = (bf16[208,1024]{1,0:T(8,128)(2,1)S(1)}, bf16[208,1024]{1,0:T(8,128)(2,1)S(1)}, u32[]{:S(2)}, u32[]{:S(2)}) collective-permute-start(bf16[208,1024]{1,0:T(8,128)(2,1)S(1)} %copy-done.3), channel_id=1, source_target_pairs={{0,1},{1,0},{2,3},{3,2},{4,5},{5,4},{6,7},{7,6},{8,9},{9,8},{10,11... | collective-permute-start | bytes 1277960 | tf_op jit(solution)/shard_map/ppermute | solution.py:415
  93.6 2.0 collective-permute-start.12
  94.7 2.0 collective-permute-start.13
  95.3 2.0 collective-permute-start.14
  97.3 2.8 %copy-start = (bf16[16,208,1024]{2,1,0:T(8,128)(2,1)}, bf16[16,208,1024]{2,1,0:T(8,128)(2,1)S(1)}, u32[]{:S(2)}) copy-start(bf16[16,208,1024]{2,1,0:T(8,128)(2,1)S(1)} %bitcast_dynamic-update-slice_fusion.cot_ref.up_ref.place_ref) | copy-start | bytes 20447236
  133.4 86.1 %all-to-all-start.1 = ((bf16[16,224,512]{2,1,0:T(8,128)(2,1)}), bf16[16,224,512]{2,1,0:T(8,128)(2,1)}, u32[]{:S(2)}, u32[]{:S(2)}) async-start(bf16[16,224,512]{2,1,0:T(8,128)(2,1)} %shard_map.97), calls=%async_computation.1 | async-start | bytes 7340032 | tf_op jit(solution)/shard_map/all_to_all | solution.py:432

commit v4 on v3

--- a/solution.py
+++ b/solution.py
@@ -10,6 +10,7 @@
 INDEX_ROWS = 16
 CAPACITY = 16
 STEP = 4
+WIDE_STEP = 8
 
 
 def contract_matrices(left, right, left_dim, right_dim):
@@ -223,7 +224,7 @@
     )(gathered, gathered, gathered, weight)
 
 
-def share_kernel(feat_ref, down_ref, place_ref, low_ref, base_ref, out_ref, grad_ref):
+def share_kernel(feat_ref, down_ref, place_ref, low_ref, base_ref, sent_ref, grad_ref, out_ref, sems):
     step = pl.program_id(0)
     items, rows, share = feat_ref.shape
     peers, rank, _ = down_ref.shape
@@ -248,9 +249,11 @@
     low = jnp.concatenate(spread_low, axis=1)
     grad_ref[...] += contract_matrices(low, feat, 0, 0)
     grad = base_ref[...] + adapter_scale * contract_matrices(low, down, 1, 0)
-    out_ref[pl.ds(step * items, items), :rows, :] = grad.astype(jnp.bfloat16).reshape(
-        items, rows, share
-    )
+    block = pl.ds(step * items, items)
+    out_ref[block, :rows, :] = grad.astype(jnp.bfloat16).reshape(items, rows, share)
+    pltpu.make_async_copy(
+        out_ref.at[block, pl.ds(0, rows), :], sent_ref.at[block, pl.ds(0, rows), :], sems.at[step]
+    ).start()
     total = (total + pltpu.roll(total, LANES // 2, 1)).astype(jnp.bfloat16)
     places = lax.broadcasted_iota(jnp.int32, (peers * CAPACITY, LANES), 0).astype(jnp.float32)
     picked = []
@@ -274,6 +277,18 @@
             out_ref[w, rows : rows + rank, :] = grad_ref[w * rank : (w + 1) * rank, :].astype(
                 jnp.bfloat16
             )
+        steps = peers // items
+        tail = pl.ds(rows, rank + 2 * CAPACITY)
+        rest = pltpu.make_async_copy(
+            out_ref.at[:, tail, :], sent_ref.at[:, tail, :], sems.at[steps]
+        )
+        rest.start()
+        for s in range(steps):
+            done = pl.ds(s * items, items)
+            pltpu.make_async_copy(
+                out_ref.at[done, pl.ds(0, rows), :], sent_ref.at[done, pl.ds(0, rows), :], sems.at[s]
+            ).wait()
+        rest.wait()
 
 
 def share_results(received, gathered, low, base, rows, rank):
@@ -297,9 +312,13 @@
             pl.BlockSpec((block, LANES), lambda s: (s, 0)),
             pl.BlockSpec((block, share), lambda s: (s, 0)),
         ],
-        out_specs=pl.BlockSpec((peer_count, total, share), lambda s: (0, 0, 0)),
+        out_specs=pl.BlockSpec(memory_space=pl.ANY),
         out_shape=jax.ShapeDtypeStruct((peer_count, total, share), jnp.bfloat16),
-        scratch_shapes=[pltpu.VMEM((slots, share), jnp.float32)],
+        scratch_shapes=[
+            pltpu.VMEM((slots, share), jnp.float32),
+            pltpu.VMEM((peer_count, total, share), jnp.bfloat16),
+            pltpu.SemaphoreType.DMA((peer_count // STEP + 1,)),
+        ],
         compiler_params=params(56),
         cost_estimate=pl.CostEstimate(flops=7 << 30, bytes_accessed=16 << 20, transcendentals=0),
     )(received, received, gathered, low, base)
@@ -388,15 +407,15 @@
     slots, keys = chosen.shape
     return pl.pallas_call(
         finish_kernel,
-        grid=(peer_count // STEP,),
+        grid=(peer_count // WIDE_STEP,),
         in_specs=[
-            pl.BlockSpec((STEP, total, share), lambda s: (s, 0, 0)),
+            pl.BlockSpec((WIDE_STEP, total, share), lambda s: (s, 0, 0)),
             pl.BlockSpec((slots, keys), lambda s: (0, 0)),
             pl.BlockSpec((1, LANES), lambda s: (0, 0)),
         ],
         out_specs=[
-            pl.BlockSpec((rows, STEP * share), lambda s: (0, s)),
-            pl.BlockSpec((rank, STEP * share), lambda s: (0, s)),
+            pl.BlockSpec((rows, WIDE_STEP * share), lambda s: (0, s)),
+            pl.BlockSpec((rank, WIDE_STEP * share), lambda s: (0, s)),
             pl.BlockSpec((rank, keys), lambda s: (0, 0)),
         ],
         out_shape=[
@@ -421,7 +440,7 @@
     held = [(0, payload), (far, mirrored)]
     for mask in (near, beside, core):
         held = held + [(shift ^ mask, swap(block, mask)) for shift, block in held]
-    for place in [6, 7]:
+    for place in [4, 3, 6]:
         shift, block = held[place]
         packed, block = lax.optimization_barrier((packed, block))
         held[place] = (shift, block)

time: 225 us -> 215 us (0.956)
  waiting for transfers between devices: 155 us -> 145 us
    all_to_all x2, waiting for transfers between devices: 87.6 us -> 81.3 us  [exchange(): lax.all_to_all(block, 'wide', split_axis=0, concat_axis=0, tiled=True)]
    ppermute x15, waiting for transfers between devices: 67 us -> 64.1 us  [swap(): lax.ppermute(block, 'wide', [(i, i ^ mask) for i in range(peer_count)])]
  transfers between devices with their start and end apart: 17 -> 17, of which waited for: 11 -> 9; matrix products, arithmetic and copies ran while one was open for 2% -> 1% of each run, Pallas kernels for 9% -> 10%
where the time goes in v4:
time: 215 us
  waiting for transfers between devices  145 us (67%)
  Pallas kernels  38.4 us (18%)
  starting transfers between devices  23.3 us (11%)
  local copies, waits for them, and re-layouts  6.69 us (3%)
    all_to_all x2, waiting for transfers between devices, exchange(): lax.all_to_all(block, 'wide', split_axis=0, concat_axis=0, tiled=True)  81.3 us
    ppermute x15, waiting for transfers between devices, swap(): lax.ppermute(block, 'wide', [(i, i ^ mask) for i in range(peer_count)])  64.1 us
    all_to_all x2, starting transfers between devices, exchange(): lax.all_to_all(block, 'wide', split_axis=0, concat_axis=0, tiled=True)  13.7 us
    pallas_call x1, Pallas kernels, share_results(): pl.pallas_call(share_kernel, grid=(peer_count // STEP,), in_specs=[pl.Blo...  11.1 us
    pallas_call x1, Pallas kernels, low_out(): pl.pallas_call(low_out_kernel, grid=(peer_count // STEP,), in_specs=[pl.B...  10.6 us
    ppermute x15, starting transfers between devices, swap(): lax.ppermute(block, 'wide', [(i, i ^ mask) for i in range(peer_count)])  9.55 us
    pallas_call x1, Pallas kernels, pack_columns(): pl.pallas_call(pack_kernel, grid=(peer_count // 2,), in_specs=[pl.BlockSp...  6.11 us
    pallas_call x1, Pallas kernels, select_rows(): pl.pallas_call(select_kernel, grid=(peer_count // STEP,), in_specs=[pl.Bl...  4.47 us
  transfers between devices with their start and end apart: 17, of which 9 were waited for; matrix products, arithmetic and copies ran while one was open for 1% of the time, Pallas kernels for 10%

profile of v4, /device:TPU:11, one launch (start us, length us, event | category | flops | bytes accessed | tf_op | source)
XLA Modules:
  0.0 214.6 jit_solution(12376361040543480618)
XLA Ops:
  0.6 2.0 shard_map.94
  2.7 1.3 collective-permute-start
  4.0 2.2 %collective-permute-start.3 = (bf16[208,1024]{1,0:T(8,128)(2,1)}, bf16[208,1024]{1,0:T(8,128)(2,1)S(1)}, u32[]{:S(2)}, u32[]{:S(2)}) collective-permute-start(bf16[208,1024]{1,0:T(8,128)(2,1)} %shard_map.94), channel_id=1, source_target_pairs={{0,4},{1,5},{2,6},{3,7},{4,0},{5,1},{6,2},{7,3},{8,12},{9,13},{10,... | collective-permute-start | bytes 1277960 | tf_op jit(solution)/shard_map/ppermute | solution.py:434
  6.2 0.3 collective-permute-start.1
  6.4 6.1 %shard_map.95 = bf16[16,192,512]{2,1,0:T(8,128)(2,1)} custom-call(bf16[128,8192]{1,0:T(8,128)(2,1)} %features_ref.1, bf16[64,8192]{1,0:T(8,128)(2,1)} %bitcast.42), custom_call_target="tpu_custom_call" | custom-call | bytes 6291456 | tf_op jit(solution)/shard_map/pallas_call | solution.py:164
  12.5 10.3 %collective-permute-done = bf16[208,1024]{1,0:T(8,128)(2,1)S(1)} collective-permute-done((bf16[208,1024]{1,0:T(8,128)(2,1)}, bf16[208,1024]{1,0:T(8,128)(2,1)S(1)}, u32[]{:S(2)}, u32[]{:S(2)}) %collective-permute-start) | collective-permute-done | bytes 426016 | tf_op jit(solution)/shard_map/ppermute | solution.py:434
  22.8 0.0 collective-permute-start.2
  22.8 2.0 collective-permute-done.3
  24.8 0.3 collective-permute-start.4
  25.1 0.0 collective-permute-done.1
  25.1 0.5 copy-done.2
  25.6 7.9 %collective-permute-done.2 = bf16[208,1024]{1,0:T(8,128)(2,1)S(1)} collective-permute-done((bf16[208,1024]{1,0:T(8,128)(2,1)S(1)}, bf16[208,1024]{1,0:T(8,128)(2,1)S(1)}, u32[]{:S(2)}, u32[]{:S(2)}) %collective-permute-start.2) | collective-permute-done | bytes 426016 | tf_op jit(solution)/shard_map/ppermute | solution.py:434
  33.5 0.0 copy-done.6
  33.5 0.8 copy-done.4
  34.3 0.0 collective-permute-done.4
  34.3 8.0 %all-to-all-start = ((bf16[16,192,512]{2,1,0:T(8,128)(2,1)}), bf16[16,192,512]{2,1,0:T(8,128)(2,1)}, u32[]{:S(2)}, u32[]{:S(2)}) async-start(bf16[16,192,512]{2,1,0:T(8,128)(2,1)} %shard_map.95), calls=%async_computation | async-start | bytes 6291456 | tf_op jit(solution)/shard_map/all_to_all | solution.py:451
  42.3 0.0 copy-done.1
  42.3 0.4 collective-permute-start.7
  42.8 0.9 broadcast_in_dim.60
  43.7 0.1 copy-done.7
  43.8 0.3 collective-permute-start.5
  44.0 0.4 collective-permute-start.8
  44.5 0.1 collective-permute-start.9
  44.6 0.4 collective-permute-start.11
  45.2 24.4 %collective-permute-done.5 = bf16[208,1024]{1,0:T(8,128)(2,1)S(1)} collective-permute-done((bf16[208,1024]{1,0:T(8,128)(2,1)S(1)}, bf16[208,1024]{1,0:T(8,128)(2,1)S(1)}, u32[]{:S(2)}, u32[]{:S(2)}) %collective-permute-start.5) | collective-permute-done | bytes 426016 | tf_op jit(solution)/shard_map/ppermute | solution.py:434
  69.6 2.0 collective-permute-start.6
  71.6 17.9 %collective-permute-done.6 = bf16[208,1024]{1,0:T(8,128)(2,1)S(1)} collective-permute-done((bf16[208,1024]{1,0:T(8,128)(2,1)S(1)}, bf16[208,1024]{1,0:T(8,128)(2,1)S(1)}, u32[]{:S(2)}, u32[]{:S(2)}) %collective-permute-start.6) | collective-permute-done | bytes 426016 | tf_op jit(solution)/shard_map/ppermute | solution.py:434
  89.6 1.2 collective-permute-start.10
  90.8 0.0 collective-permute-done.7
  90.8 0.1 collective-permute-start.12
  90.9 1.0 bitcast_dynamic-update-slice_fusion.7
  91.9 0.0 collective-permute-done.8
  91.9 0.6 collective-permute-start.13
  92.5 0.0 collective-permute-done.9
  92.6 0.1 collective-permute-start.14
  92.7 0.0 collective-permute-done.10
  92.7 0.0 collective-permute-done.11
  92.8 0.0 collective-permute-done.12
  92.9 1.0 collective-permute-done.13
  93.9 0.6 collective-permute-done.14
  94.6 2.8 %copy-done = bf16[16,208,1024]{2,1,0:T(8,128)(2,1)} copy-done((bf16[16,208,1024]{2,1,0:T(8,128)(2,1)}, bf16[16,208,1024]{2,1,0:T(8,128)(2,1)S(1)}, u32[]{:S(2)}) %copy-start) | copy-done | bytes 6815768
  97.4 10.6 %shard_map.96 = (bf16[2048,128]{1,0:T(8,128)(2,1)}, f32[2048,512]{1,0:T(8,128)}) custom-call(bf16[16,208,1024]{2,1,0:T(8,128)(2,1)} %copy-done, bf16[16,208,1024]{2,1,0:T(8,128)(2,1)} %copy-done, bf16[16,208,1024]{2,1,0:T(8,128)(2,1)} %copy-done, bf16[512,1024]{1,0:T(8,128)(2,1)} %weight_ref.1), custom_call_target="tpu_custom_call" | custom-call | flops 7516192768 | bytes 16777216 | tf_op jit(solution)/shard_map/pallas_call | solution.py:201
  108.0 4.5 %all-to-all-done.feat_ref.down_ref = bf16[16,192,512]{2,1,0:T(8,128)(2,1)} async-done(((bf16[16,192,512]{2,1,0:T(8,128)(2,1)}), bf16[16,192,512]{2,1,0:T(8,128)(2,1)}, u32[]{:S(2)}, u32[]{:S(2)}) %all-to-all-start) | async-done | bytes 3145760 | tf_op jit(solution)/shard_map/all_to_all | solution.py:451
  112.5 11.1 %shard_map.97 = bf16[16,224,512]{2,1,0:T(8,128)(2,1)} custom-call(bf16[16,192,512]{2,1,0:T(8,128)(2,1)} %all-to-all-done.feat_ref.down_ref, bf16[16,192,512]{2,1,0:T(8,128)(2,1)} %all-to-all-done.feat_ref.down_ref, bf16[16,208,1024]{2,1,0:T(8,128)(2,1)} %copy-done, bf16[2048,128]{1,0:T(8,128)(2,1)} %get-tuple-element.26.low_ref, ...), custom_call_target="tpu_custom_call" | custom-call | flops 7516192768 | bytes 16777216 | tf_op jit(solution)/shard_map/pallas_call | solution.py:301
  123.6 5.7 %all-to-all-start.1 = ((bf16[16,224,512]{2,1,0:T(8,128)(2,1)}), bf16[16,224,512]{2,1,0:T(8,128)(2,1)}, u32[]{:S(2)}, u32[]{:S(2)}) async-start(bf16[16,224,512]{2,1,0:T(8,128)(2,1)} %shard_map.97), calls=%async_computation.1 | async-start | bytes 7340032 | tf_op jit(solution)/shard_map/all_to_all | solution.py:451
  129.3 4.5 %shard_map.98 = (bf16[256,1024]{1,0:T(8,128)(2,1)}, f32[1,128]{1,0:T(1,128)}) custom-call(s32[1]{0:T(128)} %bitcast.20.own_ref, bf16[16,208,1024]{2,1,0:T(8,128)(2,1)} %copy-done, bf16[16,208,1024]{2,1,0:T(8,128)(2,1)} %copy-done), custom_call_target="tpu_custom_call" | custom-call | flops 536870912 | bytes 8388608 | tf_op jit(solution)/shard_map/pallas_call | solution.py:354
  133.7 76.8 %all-to-all-done.1.part_ref = bf16[16,224,512]{2,1,0:T(8,128)(2,1)} async-done(((bf16[16,224,512]{2,1,0:T(8,128)(2,1)}), bf16[16,224,512]{2,1,0:T(8,128)(2,1)}, u32[]{:S(2)}, u32[]{:S(2)}) %all-to-all-start.1) | async-done | bytes 3670048 | tf_op jit(solution)/shard_map/all_to_all | solution.py:451
  210.5 4.1 %shard_map.99 = (bf16[128,8192]{1,0:T(8,128)(2,1)}, f32[64,8192]{1,0:T(8,128)}, f32[64,1024]{1,0:T(8,128)}) custom-call(bf16[16,224,512]{2,1,0:T(8,128)(2,1)} %all-to-all-done.1.part_ref, bf16[256,1024]{1,0:T(8,128)(2,1)} %get-tuple-element.28.cot_ref, f32[1,128]{1,0:T(1,128)} %get-tuple-element.29.scale_ref), custom_call_target="tpu_custom_call" | custom-call | flops 134217728 | bytes 8388608 | tf_op jit(solution)/shard_map/pallas_call | solution.py:408
  (25 shorter events, 0.6 us)
Async XLA Ops:
  2.7 39.7 %copy-start.1 = (bf16[208,1024]{1,0:T(8,128)(2,1)S(1)}, bf16[208,1024]{1,0:T(8,128)(2,1)}, u32[]{:S(2)}) copy-start(bf16[208,1024]{1,0:T(8,128)(2,1)} %shard_map.94) | copy-start | bytes 1277956
  2.7 20.1 %collective-permute-start = (bf16[208,1024]{1,0:T(8,128)(2,1)}, bf16[208,1024]{1,0:T(8,128)(2,1)S(1)}, u32[]{:S(2)}, u32[]{:S(2)}) collective-permute-start(bf16[208,1024]{1,0:T(8,128)(2,1)} %shard_map.94), channel_id=1, source_target_pairs={{0,12},{1,13},{2,14},{3,15},{4,8},{5,9},{6,10},{7,11},{8,4},{9,5},... | collective-permute-start | bytes 1277960 | tf_op jit(solution)/shard_map/ppermute | solution.py:434
  4.0 20.8 %collective-permute-start.3 = (bf16[208,1024]{1,0:T(8,128)(2,1)}, bf16[208,1024]{1,0:T(8,128)(2,1)S(1)}, u32[]{:S(2)}, u32[]{:S(2)}) collective-permute-start(bf16[208,1024]{1,0:T(8,128)(2,1)} %shard_map.94), channel_id=1, source_target_pairs={{0,4},{1,5},{2,6},{3,7},{4,0},{5,1},{6,2},{7,3},{8,12},{9,13},{10,... | collective-permute-start | bytes 1277960 | tf_op jit(solution)/shard_map/ppermute | solution.py:434
  6.2 18.9 %collective-permute-start.1 = (bf16[208,1024]{1,0:T(8,128)(2,1)}, bf16[208,1024]{1,0:T(8,128)(2,1)S(1)}, u32[]{:S(2)}, u32[]{:S(2)}) collective-permute-start(bf16[208,1024]{1,0:T(8,128)(2,1)} %shard_map.94), channel_id=1, source_target_pairs={{0,2},{1,3},{2,0},{3,1},{4,6},{5,7},{6,4},{7,5},{8,10},{9,11},{10,... | collective-permute-start | bytes 1277960 | tf_op jit(solution)/shard_map/ppermute | solution.py:434
  22.8 10.7 %copy-start.6 = (bf16[208,1024]{1,0:T(8,128)(2,1)}, bf16[208,1024]{1,0:T(8,128)(2,1)S(1)}, u32[]{:S(2)}) copy-start(bf16[208,1024]{1,0:T(8,128)(2,1)S(1)} %collective-permute-done) | copy-start | bytes 1277956
  22.8 10.7 %collective-permute-start.2 = (bf16[208,1024]{1,0:T(8,128)(2,1)S(1)}, bf16[208,1024]{1,0:T(8,128)(2,1)S(1)}, u32[]{:S(2)}, u32[]{:S(2)}) collective-permute-start(bf16[208,1024]{1,0:T(8,128)(2,1)S(1)} %collective-permute-done), channel_id=1, source_target_pairs={{0,4},{1,5},{2,6},{3,7},{4,0},{5,1},{6,2},{7,3},{8,12},{9,13},{10,... | collective-permute-start | bytes 1277960 | tf_op jit(solution)/shard_map/ppermute | solution.py:434
  24.8 0.8 copy-start.2
  24.8 9.5 %collective-permute-start.4 = (bf16[208,1024]{1,0:T(8,128)(2,1)S(1)}, bf16[208,1024]{1,0:T(8,128)(2,1)S(1)}, u32[]{:S(2)}, u32[]{:S(2)}) collective-permute-start(bf16[208,1024]{1,0:T(8,128)(2,1)S(1)} %collective-permute-done.3), channel_id=1, source_target_pairs={{0,2},{1,3},{2,0},{3,1},{4,6},{5,7},{6,4},{7,5},{8,10},{9,11},{10,... | collective-permute-start | bytes 1277960 | tf_op jit(solution)/shard_map/ppermute | solution.py:434
  33.5 0.8 copy-start.4
  34.3 78.2 %all-to-all-start = ((bf16[16,192,512]{2,1,0:T(8,128)(2,1)}), bf16[16,192,512]{2,1,0:T(8,128)(2,1)}, u32[]{:S(2)}, u32[]{:S(2)}) async-start(bf16[16,192,512]{2,1,0:T(8,128)(2,1)} %shard_map.95), calls=%async_computation | async-start | bytes 6291456 | tf_op jit(solution)/shard_map/all_to_all | solution.py:451
  42.3 48.5 %collective-permute-start.7 = (bf16[208,1024]{1,0:T(8,128)(2,1)S(1)}, bf16[208,1024]{1,0:T(8,128)(2,1)}, u32[]{:S(2)}, u32[]{:S(2)}) collective-permute-start(bf16[208,1024]{1,0:T(8,128)(2,1)S(1)} %copy-done.1), channel_id=1, source_target_pairs={{0,1},{1,0},{2,3},{3,2},{4,5},{5,4},{6,7},{7,6},{8,9},{9,8},{10,11... | collective-permute-start | bytes 1277960 | tf_op jit(solution)/shard_map/ppermute | solution.py:434
  42.8 1.0 copy-start.7
  42.8 1.7 copy-start.3
  42.8 2.3 %copy-start.5 = (bf16[208,1024]{1,0:T(8,128)(2,1)S(1)}, bf16[208,1024]{1,0:T(8,128)(2,1)}, u32[]{:S(2)}) copy-start(bf16[208,1024]{1,0:T(8,128)(2,1)} %copy-done.4) | copy-start | bytes 1277956
  43.8 25.8 %collective-permute-start.5 = (bf16[208,1024]{1,0:T(8,128)(2,1)S(1)}, bf16[208,1024]{1,0:T(8,128)(2,1)S(1)}, u32[]{:S(2)}, u32[]{:S(2)}) collective-permute-start(bf16[208,1024]{1,0:T(8,128)(2,1)S(1)} %copy-done.7), channel_id=1, source_target_pairs={{0,2},{1,3},{2,0},{3,1},{4,6},{5,7},{6,4},{7,5},{8,10},{9,11},{10,... | collective-permute-start | bytes 1277960 | tf_op jit(solution)/shard_map/ppermute | solution.py:434
  44.0 47.9 %collective-permute-start.8 = (bf16[208,1024]{1,0:T(8,128)(2,1)S(1)}, bf16[208,1024]{1,0:T(8,128)(2,1)S(1)}, u32[]{:S(2)}, u32[]{:S(2)}) collective-permute-start(bf16[208,1024]{1,0:T(8,128)(2,1)S(1)} %copy-done.7), channel_id=1, source_target_pairs={{0,1},{1,0},{2,3},{3,2},{4,5},{5,4},{6,7},{7,6},{8,9},{9,8},{10,11... | collective-permute-start | bytes 1277960 | tf_op jit(solution)/shard_map/ppermute | solution.py:434
  44.5 48.1 %collective-permute-start.9 = (bf16[208,1024]{1,0:T(8,128)(2,1)S(1)}, bf16[208,1024]{1,0:T(8,128)(2,1)S(1)}, u32[]{:S(2)}, u32[]{:S(2)}) collective-permute-start(bf16[208,1024]{1,0:T(8,128)(2,1)S(1)} %copy-done.3), channel_id=1, source_target_pairs={{0,1},{1,0},{2,3},{3,2},{4,5},{5,4},{6,7},{7,6},{8,9},{9,8},{10,11... | collective-permute-start | bytes 1277960 | tf_op jit(solution)/shard_map/ppermute | solution.py:434
  44.6 48.2 %collective-permute-start.11 = (bf16[208,1024]{1,0:T(8,128)(2,1)S(1)}, bf16[208,1024]{1,0:T(8,128)(2,1)S(1)}, u32[]{:S(2)}, u32[]{:S(2)}) collective-permute-start(bf16[208,1024]{1,0:T(8,128)(2,1)S(1)} %collective-permute-done.1), channel_id=1, source_target_pairs={{0,1},{1,0},{2,3},{3,2},{4,5},{5,4},{6,7},{7,6},{8,9},{9,8},{10,11... | collective-permute-start | bytes 1277960 | tf_op jit(solution)/shard_map/ppermute | solution.py:434
  69.6 20.0 %collective-permute-start.6 = (bf16[208,1024]{1,0:T(8,128)(2,1)S(1)}, bf16[208,1024]{1,0:T(8,128)(2,1)S(1)}, u32[]{:S(2)}, u32[]{:S(2)}) collective-permute-start(bf16[208,1024]{1,0:T(8,128)(2,1)S(1)} %copy-done.5), channel_id=1, source_target_pairs={{0,2},{1,3},{2,0},{3,1},{4,6},{5,7},{6,4},{7,5},{8,10},{9,11},{10,... | collective-permute-start | bytes 1277960 | tf_op jit(solution)/shard_map/ppermute | solution.py:434
  89.6 3.1 %collective-permute-start.10 = (bf16[208,1024]{1,0:T(8,128)(2,1)S(1)}, bf16[208,1024]{1,0:T(8,128)(2,1)S(1)}, u32[]{:S(2)}, u32[]{:S(2)}) collective-permute-start(bf16[208,1024]{1,0:T(8,128)(2,1)S(1)} %copy-done.5), channel_id=1, source_target_pairs={{0,1},{1,0},{2,3},{3,2},{4,5},{5,4},{6,7},{7,6},{8,9},{9,8},{10,11... | collective-permute-start | bytes 1277960 | tf_op jit(solution)/shard_map/ppermute | solution.py:434
  90.8 2.0 collective-permute-start.12
  91.9 2.0 collective-permute-start.13
  92.6 2.0 collective-permute-start.14
  94.5 2.8 %copy-start = (bf16[16,208,1024]{2,1,0:T(8,128)(2,1)}, bf16[16,208,1024]{2,1,0:T(8,128)(2,1)S(1)}, u32[]{:S(2)}) copy-start(bf16[16,208,1024]{2,1,0:T(8,128)(2,1)S(1)} %bitcast_dynamic-update-slice_fusion.cot_ref.up_ref.place_ref) | copy-start | bytes 20447236
  123.6 87.0 %all-to-all-start.1 = ((bf16[16,224,512]{2,1,0:T(8,128)(2,1)}), bf16[16,224,512]{2,1,0:T(8,128)(2,1)}, u32[]{:S(2)}, u32[]{:S(2)}) async-start(bf16[16,224,512]{2,1,0:T(8,128)(2,1)} %shard_map.97), calls=%async_computation.1 | async-start | bytes 7340032 | tf_op jit(solution)/shard_map/all_to_all | solution.py:451

commit v5 on v4

--- a/solution.py
+++ b/solution.py
@@ -238,22 +238,21 @@
     place = place_columns(place_ref[...])
     slot = jnp.floor(place / CAPACITY)
     folded = low_ref[...].astype(jnp.float32)
-    partial = contract_matrices(feat, down, 1, 1)
-    total = jnp.zeros_like(place)
-    spread_low = []
-    for j in range(partial.shape[1] // LANES):
-        span = slice(j * LANES, (j + 1) * LANES)
-        mine = slot == adapter_lanes(j)
-        total = total + jnp.where(mine, partial[:, span], 0.0)
-        spread_low.append(jnp.where(mine, folded, 0.0).astype(jnp.bfloat16))
-    low = jnp.concatenate(spread_low, axis=1)
-    grad_ref[...] += contract_matrices(low, feat, 0, 0)
+    masks = [slot == adapter_lanes(j) for j in range(down.shape[0] // LANES)]
+    low = jnp.concatenate(
+        [jnp.where(mine, folded, 0.0).astype(jnp.bfloat16) for mine in masks], axis=1
+    )
     grad = base_ref[...] + adapter_scale * contract_matrices(low, down, 1, 0)
     block = pl.ds(step * items, items)
     out_ref[block, :rows, :] = grad.astype(jnp.bfloat16).reshape(items, rows, share)
     pltpu.make_async_copy(
         out_ref.at[block, pl.ds(0, rows), :], sent_ref.at[block, pl.ds(0, rows), :], sems.at[step]
     ).start()
+    partial = contract_matrices(feat, down, 1, 1)
+    grad_ref[...] += contract_matrices(low, feat, 0, 0)
+    total = jnp.zeros_like(place)
+    for j, mine in enumerate(masks):
+        total = total + jnp.where(mine, partial[:, j * LANES : (j + 1) * LANES], 0.0)
     total = (total + pltpu.roll(total, LANES // 2, 1)).astype(jnp.bfloat16)
     places = lax.broadcasted_iota(jnp.int32, (peers * CAPACITY, LANES), 0).astype(jnp.float32)
     picked = []
@@ -369,7 +368,7 @@
             jax.ShapeDtypeStruct((peer_count * CAPACITY, keys), jnp.bfloat16),
             jax.ShapeDtypeStruct((1, LANES), jnp.float32),
         ],
-        compiler_params=params(56),
+        compiler_params=params(44),
         cost_estimate=pl.CostEstimate(flops=1 << 29, bytes_accessed=8 << 20, transcendentals=0),
     )(own, gathered, gathered)
 
@@ -424,7 +423,7 @@
             jax.ShapeDtypeStruct((rank, keys), jnp.float32),
         ],
         scratch_shapes=[pltpu.VMEM((2 * CAPACITY, share), jnp.float32)],
-        compiler_params=params(56),
+        compiler_params=params(44),
         cost_estimate=pl.CostEstimate(flops=1 << 27, bytes_accessed=8 << 20, transcendentals=0),
     )(parts, chosen, scale)
 
@@ -444,7 +443,8 @@
         shift, block = held[place]
         packed, block = lax.optimization_barrier((packed, block))
         held[place] = (shift, block)
-    return packed, held
+    late = [5, 7, 13, 15]
+    return packed, [held[i] for i in range(16) if i not in late] + [held[i] for i in late]
 
 
 def exchange(block):

time: 215 us -> 214 us (level)
  Pallas kernels: 38.4 us -> 35.3 us
  local copies, waits for them, and re-layouts: 6.69 us -> 9.32 us
    ppermute x15, waiting for transfers between devices: 64.1 us -> 55 us  [swap(): lax.ppermute(block, 'wide', [(i, i ^ mask) for i in range(peer_count)])]
    all_to_all x2, waiting for transfers between devices: 81.3 us -> 89.9 us  [exchange(): lax.all_to_all(block, 'wide', split_axis=0, concat_axis=0, tiled=True)]
    pallas_call x1, Pallas kernels: 4.47 us -> 1.58 us  [select_rows(): pl.pallas_call(select_kernel, grid=(peer_count // STEP,), in_specs=[pl.Bl...]
    unnamed x16 -> x14, local copies, waits for them, and re-layouts: 4.23 us -> 5.86 us
  transfers between devices with their start and end apart: 17 -> 17, of which waited for: 9 -> 9; matrix products, arithmetic and copies ran while one was open for 1% -> 2% of each run, Pallas kernels for 10% -> 9%
where the time goes in v5:
time: 214 us; the launch traced here: 213 us
  waiting for transfers between devices  145 us (68%)
  Pallas kernels  35.3 us (16%)
  starting transfers between devices  23.1 us (11%)
  local copies, waits for them, and re-layouts  9.32 us (4%)
    all_to_all x2, waiting for transfers between devices, exchange(): lax.all_to_all(block, 'wide', split_axis=0, concat_axis=0, tiled=True)  89.9 us
    ppermute x15, waiting for transfers between devices, swap(): lax.ppermute(block, 'wide', [(i, i ^ mask) for i in range(peer_count)])  55 us
    all_to_all x2, starting transfers between devices, exchange(): lax.all_to_all(block, 'wide', split_axis=0, concat_axis=0, tiled=True)  12.8 us
    pallas_call x1, Pallas kernels, share_results(): pl.pallas_call(share_kernel, grid=(peer_count // STEP,), in_specs=[pl.Blo...  11 us
    pallas_call x1, Pallas kernels, low_out(): pl.pallas_call(low_out_kernel, grid=(peer_count // STEP,), in_specs=[pl.B...  10.6 us
    ppermute x15, starting transfers between devices, swap(): lax.ppermute(block, 'wide', [(i, i ^ mask) for i in range(peer_count)])  10.4 us
    pallas_call x1, Pallas kernels, pack_columns(): pl.pallas_call(pack_kernel, grid=(peer_count // 2,), in_specs=[pl.BlockSp...  6.1 us
    unnamed x14, local copies, waits for them, and re-layouts  5.86 us
  transfers between devices with their start and end apart: 17, of which 9 were waited for; matrix products, arithmetic and copies ran while one was open for 2% of the time, Pallas kernels for 9%

profile of v5, /device:TPU:11, one launch (start us, length us, event | category | flops | bytes accessed | tf_op | source)
XLA Modules:
  0.0 213.5 jit_solution(6749602324426166317)
XLA Ops:
  0.6 2.0 shard_map.94
  2.7 1.3 collective-permute-start
  4.0 2.2 %collective-permute-start.3 = (bf16[208,1024]{1,0:T(8,128)(2,1)}, bf16[208,1024]{1,0:T(8,128)(2,1)S(1)}, u32[]{:S(2)}, u32[]{:S(2)}) collective-permute-start(bf16[208,1024]{1,0:T(8,128)(2,1)} %shard_map.94), channel_id=1, source_target_pairs={{0,4},{1,5},{2,6},{3,7},{4,0},{5,1},{6,2},{7,3},{8,12},{9,13},{10,... | collective-permute-start | bytes 1277960 | tf_op jit(solution)/shard_map/ppermute | solution.py:433
  6.2 0.3 collective-permute-start.1
  6.4 6.1 %shard_map.95 = bf16[16,192,512]{2,1,0:T(8,128)(2,1)} custom-call(bf16[128,8192]{1,0:T(8,128)(2,1)} %features_ref.1, bf16[64,8192]{1,0:T(8,128)(2,1)} %bitcast.42), custom_call_target="tpu_custom_call" | custom-call | bytes 6291456 | tf_op jit(solution)/shard_map/pallas_call | solution.py:164
  12.5 10.3 %collective-permute-done = bf16[208,1024]{1,0:T(8,128)(2,1)S(1)} collective-permute-done((bf16[208,1024]{1,0:T(8,128)(2,1)}, bf16[208,1024]{1,0:T(8,128)(2,1)S(1)}, u32[]{:S(2)}, u32[]{:S(2)}) %collective-permute-start) | collective-permute-done | bytes 426016 | tf_op jit(solution)/shard_map/ppermute | solution.py:433
  22.8 0.0 collective-permute-start.2
  22.8 2.0 collective-permute-done.3
  24.8 0.3 collective-permute-start.4
  25.1 0.0 collective-permute-done.1
  25.1 0.0 copy-done.3
  25.1 8.5 %collective-permute-done.2 = bf16[208,1024]{1,0:T(8,128)(2,1)} collective-permute-done((bf16[208,1024]{1,0:T(8,128)(2,1)S(1)}, bf16[208,1024]{1,0:T(8,128)(2,1)}, u32[]{:S(2)}, u32[]{:S(2)}) %collective-permute-start.2) | collective-permute-done | bytes 426016 | tf_op jit(solution)/shard_map/ppermute | solution.py:433
  33.6 0.8 collective-permute-done.4
  34.4 7.9 %all-to-all-start = ((bf16[16,192,512]{2,1,0:T(8,128)(2,1)}), bf16[16,192,512]{2,1,0:T(8,128)(2,1)}, u32[]{:S(2)}, u32[]{:S(2)}) async-start(bf16[16,192,512]{2,1,0:T(8,128)(2,1)} %shard_map.95), calls=%async_computation | async-start | bytes 6291456 | tf_op jit(solution)/shard_map/all_to_all | solution.py:451
  42.3 0.4 collective-permute-start.5
  42.8 0.9 broadcast_in_dim.60
  43.7 0.1 copy-done.4
  43.8 0.1 collective-permute-start.6
  43.9 0.3 collective-permute-start.11
  44.2 0.0 copy-done.6
  44.2 0.6 collective-permute-start.7
  44.8 0.0 collective-permute-start.9
  44.9 1.0 bitcast_dynamic-update-slice_fusion.12
  46.1 0.0 collective-permute-done.5
  46.1 0.6 collective-permute-start.8
  46.7 1.0 bitcast_dynamic-update-slice_fusion.9
  47.7 0.0 collective-permute-done.6
  47.7 1.3 collective-permute-start.12
  49.0 0.0 collective-permute-done.7
  49.0 0.4 collective-permute-start.10
  49.4 20.2 %collective-permute-done.11 = bf16[208,1024]{1,0:T(8,128)(2,1)S(1)} collective-permute-done((bf16[208,1024]{1,0:T(8,128)(2,1)S(1)}, bf16[208,1024]{1,0:T(8,128)(2,1)S(1)}, u32[]{:S(2)}, u32[]{:S(2)}) %collective-permute-start.11) | collective-permute-done | bytes 426016 | tf_op jit(solution)/shard_map/ppermute | solution.py:433
  69.6 1.3 collective-permute-start.13
  70.9 12.1 %collective-permute-done.12 = bf16[208,1024]{1,0:T(8,128)(2,1)S(1)} collective-permute-done((bf16[208,1024]{1,0:T(8,128)(2,1)}, bf16[208,1024]{1,0:T(8,128)(2,1)S(1)}, u32[]{:S(2)}, u32[]{:S(2)}) %collective-permute-start.12) | collective-permute-done | bytes 426016 | tf_op jit(solution)/shard_map/ppermute | solution.py:433
  83.1 1.3 collective-permute-start.14
  84.4 0.0 collective-permute-done.8
  84.4 0.0 collective-permute-done.9
  84.5 0.0 collective-permute-done.10
  84.7 0.0 collective-permute-done.13
  84.7 1.1 collective-permute-done.14
  85.9 2.8 %copy-done = bf16[16,208,1024]{2,1,0:T(8,128)(2,1)} copy-done((bf16[16,208,1024]{2,1,0:T(8,128)(2,1)}, bf16[16,208,1024]{2,1,0:T(8,128)(2,1)S(1)}, u32[]{:S(2)}) %copy-start) | copy-done | bytes 6815768
  88.7 10.6 %shard_map.96 = (bf16[2048,128]{1,0:T(8,128)(2,1)}, f32[2048,512]{1,0:T(8,128)}) custom-call(bf16[16,208,1024]{2,1,0:T(8,128)(2,1)} %copy-done, bf16[16,208,1024]{2,1,0:T(8,128)(2,1)} %copy-done, bf16[16,208,1024]{2,1,0:T(8,128)(2,1)} %copy-done, bf16[512,1024]{1,0:T(8,128)(2,1)} %weight_ref.1), custom_call_target="tpu_custom_call" | custom-call | flops 7516192768 | bytes 16777216 | tf_op jit(solution)/shard_map/pallas_call | solution.py:201
  99.3 13.2 %all-to-all-done.feat_ref.down_ref = bf16[16,192,512]{2,1,0:T(8,128)(2,1)} async-done(((bf16[16,192,512]{2,1,0:T(8,128)(2,1)}), bf16[16,192,512]{2,1,0:T(8,128)(2,1)}, u32[]{:S(2)}, u32[]{:S(2)}) %all-to-all-start) | async-done | bytes 3145760 | tf_op jit(solution)/shard_map/all_to_all | solution.py:451
  112.5 11.0 %shard_map.97 = bf16[16,224,512]{2,1,0:T(8,128)(2,1)} custom-call(bf16[16,192,512]{2,1,0:T(8,128)(2,1)} %all-to-all-done.feat_ref.down_ref, bf16[16,192,512]{2,1,0:T(8,128)(2,1)} %all-to-all-done.feat_ref.down_ref, bf16[16,208,1024]{2,1,0:T(8,128)(2,1)} %copy-done, bf16[2048,128]{1,0:T(8,128)(2,1)} %get-tuple-element.26.low_ref, ...), custom_call_target="tpu_custom_call" | custom-call | flops 7516192768 | bytes 16777216 | tf_op jit(solution)/shard_map/pallas_call | solution.py:300
  123.5 4.8 %all-to-all-start.1 = ((bf16[16,224,512]{2,1,0:T(8,128)(2,1)}), bf16[16,224,512]{2,1,0:T(8,128)(2,1)}, u32[]{:S(2)}, u32[]{:S(2)}) async-start(bf16[16,224,512]{2,1,0:T(8,128)(2,1)} %shard_map.97), calls=%async_computation.1 | async-start | bytes 7340032 | tf_op jit(solution)/shard_map/all_to_all | solution.py:451
  128.3 2.9 %copy-done.1 = bf16[16,208,1024]{2,1,0:T(8,128)(2,1)S(1)} copy-done((bf16[16,208,1024]{2,1,0:T(8,128)(2,1)S(1)}, bf16[16,208,1024]{2,1,0:T(8,128)(2,1)}, u32[]{:S(2)}) %copy-start.1) | copy-done | bytes 6815768
  131.3 1.6 shard_map.98
  132.8 76.7 %all-to-all-done.1.part_ref = bf16[16,224,512]{2,1,0:T(8,128)(2,1)} async-done(((bf16[16,224,512]{2,1,0:T(8,128)(2,1)}), bf16[16,224,512]{2,1,0:T(8,128)(2,1)}, u32[]{:S(2)}, u32[]{:S(2)}) %all-to-all-start.1) | async-done | bytes 3670048 | tf_op jit(solution)/shard_map/all_to_all | solution.py:451
  209.6 3.9 %shard_map.99 = (bf16[128,8192]{1,0:T(8,128)(2,1)}, f32[64,8192]{1,0:T(8,128)}, f32[64,1024]{1,0:T(8,128)}) custom-call(bf16[16,224,512]{2,1,0:T(8,128)(2,1)} %all-to-all-done.1.part_ref, bf16[256,1024]{1,0:T(8,128)(2,1)S(1)} %get-tuple-element.28.cot_ref, f32[1,128]{1,0:T(1,128)S(1)} %get-tuple-element.29.scale_ref), custom_call_target="tpu_custom_call" | custom-call | flops 134217728 | bytes 8388608 | tf_op jit(solution)/shard_map/pallas_call | solution.py:407
  (23 shorter events, 0.5 us)
Async XLA Ops:
  2.7 39.7 %copy-start.2 = (bf16[208,1024]{1,0:T(8,128)(2,1)S(1)}, bf16[208,1024]{1,0:T(8,128)(2,1)}, u32[]{:S(2)}) copy-start(bf16[208,1024]{1,0:T(8,128)(2,1)} %shard_map.94) | copy-start | bytes 1277956
  2.7 20.1 %collective-permute-start = (bf16[208,1024]{1,0:T(8,128)(2,1)}, bf16[208,1024]{1,0:T(8,128)(2,1)S(1)}, u32[]{:S(2)}, u32[]{:S(2)}) collective-permute-start(bf16[208,1024]{1,0:T(8,128)(2,1)} %shard_map.94), channel_id=1, source_target_pairs={{0,12},{1,13},{2,14},{3,15},{4,8},{5,9},{6,10},{7,11},{8,4},{9,5},... | collective-permute-start | bytes 1277960 | tf_op jit(solution)/shard_map/ppermute | solution.py:433
  4.0 20.8 %collective-permute-start.3 = (bf16[208,1024]{1,0:T(8,128)(2,1)}, bf16[208,1024]{1,0:T(8,128)(2,1)S(1)}, u32[]{:S(2)}, u32[]{:S(2)}) collective-permute-start(bf16[208,1024]{1,0:T(8,128)(2,1)} %shard_map.94), channel_id=1, source_target_pairs={{0,4},{1,5},{2,6},{3,7},{4,0},{5,1},{6,2},{7,3},{8,12},{9,13},{10,... | collective-permute-start | bytes 1277960 | tf_op jit(solution)/shard_map/ppermute | solution.py:433
  6.2 18.9 %collective-permute-start.1 = (bf16[208,1024]{1,0:T(8,128)(2,1)}, bf16[208,1024]{1,0:T(8,128)(2,1)S(1)}, u32[]{:S(2)}, u32[]{:S(2)}) collective-permute-start(bf16[208,1024]{1,0:T(8,128)(2,1)} %shard_map.94), channel_id=1, source_target_pairs={{0,2},{1,3},{2,0},{3,1},{4,6},{5,7},{6,4},{7,5},{8,10},{9,11},{10,... | collective-permute-start | bytes 1277960 | tf_op jit(solution)/shard_map/ppermute | solution.py:433
  22.8 2.3 %copy-start.3 = (bf16[208,1024]{1,0:T(8,128)(2,1)}, bf16[208,1024]{1,0:T(8,128)(2,1)S(1)}, u32[]{:S(2)}) copy-start(bf16[208,1024]{1,0:T(8,128)(2,1)S(1)} %collective-permute-done) | copy-start | bytes 1277956
  22.8 10.8 %collective-permute-start.2 = (bf16[208,1024]{1,0:T(8,128)(2,1)S(1)}, bf16[208,1024]{1,0:T(8,128)(2,1)}, u32[]{:S(2)}, u32[]{:S(2)}) collective-permute-start(bf16[208,1024]{1,0:T(8,128)(2,1)S(1)} %collective-permute-done), channel_id=1, source_target_pairs={{0,4},{1,5},{2,6},{3,7},{4,0},{5,1},{6,2},{7,3},{8,12},{9,13},{10,... | collective-permute-start | bytes 1277960 | tf_op jit(solution)/shard_map/ppermute | solution.py:433
  24.8 8.8 %copy-start.5 = (bf16[208,1024]{1,0:T(8,128)(2,1)}, bf16[208,1024]{1,0:T(8,128)(2,1)S(1)}, u32[]{:S(2)}) copy-start(bf16[208,1024]{1,0:T(8,128)(2,1)S(1)} %collective-permute-done.3) | copy-start | bytes 1277956
  24.8 9.6 %collective-permute-start.4 = (bf16[208,1024]{1,0:T(8,128)(2,1)S(1)}, bf16[208,1024]{1,0:T(8,128)(2,1)S(1)}, u32[]{:S(2)}, u32[]{:S(2)}) collective-permute-start(bf16[208,1024]{1,0:T(8,128)(2,1)S(1)} %collective-permute-done.3), channel_id=1, source_target_pairs={{0,2},{1,3},{2,0},{3,1},{4,6},{5,7},{6,4},{7,5},{8,10},{9,11},{10,... | collective-permute-start | bytes 1277960 | tf_op jit(solution)/shard_map/ppermute | solution.py:433
  34.4 78.1 %all-to-all-start = ((bf16[16,192,512]{2,1,0:T(8,128)(2,1)}), bf16[16,192,512]{2,1,0:T(8,128)(2,1)}, u32[]{:S(2)}, u32[]{:S(2)}) async-start(bf16[16,192,512]{2,1,0:T(8,128)(2,1)} %shard_map.95), calls=%async_computation | async-start | bytes 6291456 | tf_op jit(solution)/shard_map/all_to_all | solution.py:451
  42.3 3.7 %collective-permute-start.5 = (bf16[208,1024]{1,0:T(8,128)(2,1)S(1)}, bf16[208,1024]{1,0:T(8,128)(2,1)}, u32[]{:S(2)}, u32[]{:S(2)}) collective-permute-start(bf16[208,1024]{1,0:T(8,128)(2,1)S(1)} %copy-done.2), channel_id=1, source_target_pairs={{0,1},{1,0},{2,3},{3,2},{4,5},{5,4},{6,7},{7,6},{8,9},{9,8},{10,11... | collective-permute-start | bytes 1277960 | tf_op jit(solution)/shard_map/ppermute | solution.py:433
  42.8 1.0 copy-start.4
  42.8 1.4 copy-start.6
  43.8 3.9 %collective-permute-start.6 = (bf16[208,1024]{1,0:T(8,128)(2,1)S(1)}, bf16[208,1024]{1,0:T(8,128)(2,1)S(1)}, u32[]{:S(2)}, u32[]{:S(2)}) collective-permute-start(bf16[208,1024]{1,0:T(8,128)(2,1)S(1)} %copy-done.4), channel_id=1, source_target_pairs={{0,1},{1,0},{2,3},{3,2},{4,5},{5,4},{6,7},{7,6},{8,9},{9,8},{10,11... | collective-permute-start | bytes 1277960 | tf_op jit(solution)/shard_map/ppermute | solution.py:433
  43.9 25.6 %collective-permute-start.11 = (bf16[208,1024]{1,0:T(8,128)(2,1)S(1)}, bf16[208,1024]{1,0:T(8,128)(2,1)S(1)}, u32[]{:S(2)}, u32[]{:S(2)}) collective-permute-start(bf16[208,1024]{1,0:T(8,128)(2,1)S(1)} %copy-done.4), channel_id=1, source_target_pairs={{0,2},{1,3},{2,0},{3,1},{4,6},{5,7},{6,4},{7,5},{8,10},{9,11},{10,... | collective-permute-start | bytes 1277960 | tf_op jit(solution)/shard_map/ppermute | solution.py:433
  44.2 4.8 %collective-permute-start.7 = (bf16[208,1024]{1,0:T(8,128)(2,1)S(1)}, bf16[208,1024]{1,0:T(8,128)(2,1)S(1)}, u32[]{:S(2)}, u32[]{:S(2)}) collective-permute-start(bf16[208,1024]{1,0:T(8,128)(2,1)S(1)} %copy-done.6), channel_id=1, source_target_pairs={{0,1},{1,0},{2,3},{3,2},{4,5},{5,4},{6,7},{7,6},{8,9},{9,8},{10,11... | collective-permute-start | bytes 1277960 | tf_op jit(solution)/shard_map/ppermute | solution.py:433
  44.8 39.6 %collective-permute-start.9 = (bf16[208,1024]{1,0:T(8,128)(2,1)S(1)}, bf16[208,1024]{1,0:T(8,128)(2,1)S(1)}, u32[]{:S(2)}, u32[]{:S(2)}) collective-permute-start(bf16[208,1024]{1,0:T(8,128)(2,1)S(1)} %collective-permute-done.1), channel_id=1, source_target_pairs={{0,1},{1,0},{2,3},{3,2},{4,5},{5,4},{6,7},{7,6},{8,9},{9,8},{10,11... | collective-permute-start | bytes 1277960 | tf_op jit(solution)/shard_map/ppermute | solution.py:433
  46.1 38.3 %collective-permute-start.8 = (bf16[208,1024]{1,0:T(8,128)(2,1)}, bf16[208,1024]{1,0:T(8,128)(2,1)S(1)}, u32[]{:S(2)}, u32[]{:S(2)}) collective-permute-start(bf16[208,1024]{1,0:T(8,128)(2,1)} %collective-permute-done.2), channel_id=1, source_target_pairs={{0,1},{1,0},{2,3},{3,2},{4,5},{5,4},{6,7},{7,6},{8,9},{9,8},{10,11... | collective-permute-start | bytes 1277960 | tf_op jit(solution)/shard_map/ppermute | solution.py:433
  47.7 35.4 %collective-permute-start.12 = (bf16[208,1024]{1,0:T(8,128)(2,1)}, bf16[208,1024]{1,0:T(8,128)(2,1)S(1)}, u32[]{:S(2)}, u32[]{:S(2)}) collective-permute-start(bf16[208,1024]{1,0:T(8,128)(2,1)} %collective-permute-done.2), channel_id=1, source_target_pairs={{0,2},{1,3},{2,0},{3,1},{4,6},{5,7},{6,4},{7,5},{8,10},{9,11},{10,... | collective-permute-start | bytes 1277960 | tf_op jit(solution)/shard_map/ppermute | solution.py:433
  49.0 35.5 %collective-permute-start.10 = (bf16[208,1024]{1,0:T(8,128)(2,1)S(1)}, bf16[208,1024]{1,0:T(8,128)(2,1)S(1)}, u32[]{:S(2)}, u32[]{:S(2)}) collective-permute-start(bf16[208,1024]{1,0:T(8,128)(2,1)S(1)} %collective-permute-done.4), channel_id=1, source_target_pairs={{0,1},{1,0},{2,3},{3,2},{4,5},{5,4},{6,7},{7,6},{8,9},{9,8},{10,11... | collective-permute-start | bytes 1277960 | tf_op jit(solution)/shard_map/ppermute | solution.py:433
  69.6 15.1 %collective-permute-start.13 = (bf16[208,1024]{1,0:T(8,128)(2,1)S(1)}, bf16[208,1024]{1,0:T(8,128)(2,1)S(1)}, u32[]{:S(2)}, u32[]{:S(2)}) collective-permute-start(bf16[208,1024]{1,0:T(8,128)(2,1)S(1)} %collective-permute-done.11), channel_id=1, source_target_pairs={{0,1},{1,0},{2,3},{3,2},{4,5},{5,4},{6,7},{7,6},{8,9},{9,8},{10,11... | collective-permute-start | bytes 1277960 | tf_op jit(solution)/shard_map/ppermute | solution.py:433
  83.1 2.7 %collective-permute-start.14 = (bf16[208,1024]{1,0:T(8,128)(2,1)S(1)}, bf16[208,1024]{1,0:T(8,128)(2,1)S(1)}, u32[]{:S(2)}, u32[]{:S(2)}) collective-permute-start(bf16[208,1024]{1,0:T(8,128)(2,1)S(1)} %collective-permute-done.12), channel_id=1, source_target_pairs={{0,1},{1,0},{2,3},{3,2},{4,5},{5,4},{6,7},{7,6},{8,9},{9,8},{10,11... | collective-permute-start | bytes 1277960 | tf_op jit(solution)/shard_map/ppermute | solution.py:433
  85.8 2.8 %copy-start = (bf16[16,208,1024]{2,1,0:T(8,128)(2,1)}, bf16[16,208,1024]{2,1,0:T(8,128)(2,1)S(1)}, u32[]{:S(2)}) copy-start(bf16[16,208,1024]{2,1,0:T(8,128)(2,1)S(1)} %bitcast_dynamic-update-slice_fusion.cot_ref.up_ref.place_ref) | copy-start | bytes 20447236
  123.5 86.1 %all-to-all-start.1 = ((bf16[16,224,512]{2,1,0:T(8,128)(2,1)}), bf16[16,224,512]{2,1,0:T(8,128)(2,1)}, u32[]{:S(2)}, u32[]{:S(2)}) async-start(bf16[16,224,512]{2,1,0:T(8,128)(2,1)} %shard_map.97), calls=%async_computation.1 | async-start | bytes 7340032 | tf_op jit(solution)/shard_map/all_to_all | solution.py:451
  128.3 2.9 %copy-start.1 = (bf16[16,208,1024]{2,1,0:T(8,128)(2,1)S(1)}, bf16[16,208,1024]{2,1,0:T(8,128)(2,1)}, u32[]{:S(2)}) copy-start(bf16[16,208,1024]{2,1,0:T(8,128)(2,1)} %copy-done) | copy-start | bytes 20447236

commit v6 on v5

--- a/solution.py
+++ b/solution.py
@@ -180,7 +180,7 @@
     return (2 * j + lane // (LANES // 2)).astype(jnp.float32)
 
 
-def low_out_kernel(cot_ref, up_ref, place_ref, weight_ref, low_ref, base_ref):
+def low_out_kernel(cot_ref, up_ref, place_ref, weight_ref, low_ref, base_ref, pick_ref):
     keys = cot_ref.shape[2]
     cot = cot_ref[...].reshape(-1, keys)
     slot = jnp.floor(place_columns(place_ref[...]) / CAPACITY)
@@ -191,6 +191,12 @@
         total = total + jnp.where(slot == adapter_lanes(j), low[:, span], 0.0)
     low_ref[...] = (total + pltpu.roll(total, LANES // 2, 1)).astype(jnp.bfloat16)
     base_ref[...] = contract_matrices(cot, weight_ref[...], 1, 1)
+    items, places, rows = pick_ref.shape
+    place = place_columns(place_ref[...])
+    wanted = lax.broadcasted_iota(jnp.int32, (places, rows), 0).astype(jnp.float32)
+    for item in range(items):
+        row = place[item * rows : (item + 1) * rows, :].T[:1, :]
+        pick_ref[item] = jnp.where(wanted == row, 1.0, 0.0).astype(jnp.bfloat16)
 
 
 def low_out(gathered, weight, rows, rank):
@@ -214,17 +220,19 @@
         out_specs=[
             pl.BlockSpec((block, LANES), lambda s: (s, 0)),
             pl.BlockSpec((block, share), lambda s: (s, 0)),
+            pl.BlockSpec((STEP, peer_count * CAPACITY, rows), lambda s: (s, 0, 0)),
         ],
         out_shape=[
             jax.ShapeDtypeStruct((peer_count * rows, LANES), jnp.bfloat16),
             jax.ShapeDtypeStruct((peer_count * rows, share), jnp.float32),
+            jax.ShapeDtypeStruct((peer_count, peer_count * CAPACITY, rows), jnp.bfloat16),
         ],
         compiler_params=params(56),
         cost_estimate=pl.CostEstimate(flops=7 << 30, bytes_accessed=16 << 20, transcendentals=0),
     )(gathered, gathered, gathered, weight)
 
 
-def share_kernel(feat_ref, down_ref, place_ref, low_ref, base_ref, sent_ref, grad_ref, out_ref, sems):
+def share_kernel(feat_ref, down_ref, place_ref, low_ref, base_ref, pick_ref, sent_ref, grad_ref, out_ref, sems):
     step = pl.program_id(0)
     items, rows, share = feat_ref.shape
     peers, rank, _ = down_ref.shape
@@ -254,13 +262,10 @@
     for j, mine in enumerate(masks):
         total = total + jnp.where(mine, partial[:, j * LANES : (j + 1) * LANES], 0.0)
     total = (total + pltpu.roll(total, LANES // 2, 1)).astype(jnp.bfloat16)
-    places = lax.broadcasted_iota(jnp.int32, (peers * CAPACITY, LANES), 0).astype(jnp.float32)
     picked = []
     for item in range(items):
         span = slice(item * rows, (item + 1) * rows)
-        row = place[span, :].T[:1, :]
-        pick = jnp.where(places == row, 1.0, 0.0).astype(jnp.bfloat16)
-        picked.append(contract_matrices(pick, total[span, :], 1, 0))
+        picked.append(contract_matrices(pick_ref[item], total[span, :], 1, 0))
     left = lax.broadcasted_iota(jnp.int32, (CAPACITY, LANES), 1) < LANES // 2
     lanes = pl.ds(pl.multiple_of(step * LANES, LANES), LANES)
     for w in range(peers):
@@ -290,7 +295,7 @@
         rest.wait()
 
 
-def share_results(received, gathered, low, base, rows, rank):
+def share_results(received, gathered, low, base, picks, rows, rank):
     peer_count, _, share = received.shape
     keys = gathered.shape[2]
     block = STEP * rows
@@ -310,6 +315,7 @@
             ),
             pl.BlockSpec((block, LANES), lambda s: (s, 0)),
             pl.BlockSpec((block, share), lambda s: (s, 0)),
+            pl.BlockSpec((STEP, peer_count * CAPACITY, rows), lambda s: (s, 0, 0)),
         ],
         out_specs=pl.BlockSpec(memory_space=pl.ANY),
         out_shape=jax.ShapeDtypeStruct((peer_count, total, share), jnp.bfloat16),
@@ -320,7 +326,7 @@
         ],
         compiler_params=params(56),
         cost_estimate=pl.CostEstimate(flops=7 << 30, bytes_accessed=16 << 20, transcendentals=0),
-    )(received, received, gathered, low, base)
+    )(received, received, gathered, low, base, picks)
 
 
 def select_kernel(own_ref, cot_ref, place_ref, rows_ref, scale_ref):
@@ -473,8 +479,8 @@
     gathered = jnp.zeros((peer_count,) + payload.shape, payload.dtype)
     for shift, block in held:
         gathered = lax.dynamic_update_slice(gathered, block[None], (device_index ^ shift, 0, 0))
-    low, base = low_out(gathered, frozen_key_weight, rows, rank)
-    parts = exchange(share_results(received, gathered, low, base, rows, rank))
+    low, base, picks = low_out(gathered, frozen_key_weight, rows, rank)
+    parts = exchange(share_results(received, gathered, low, base, picks, rows, rank))
     own = jnp.full((1,), device_index, jnp.int32)
     chosen, scale = select_rows(own, gathered, rows, rank)
     input_grad, grad_down, grad_up = finish(parts, chosen, scale, rows, rank)

time: 214 us -> 214 us (level)
  no operation moved by 1% of the time
where the time goes in v6:
time: 214 us
  waiting for transfers between devices  145 us (68%)
  Pallas kernels  35.4 us (17%)
  starting transfers between devices  23.1 us (11%)
  local copies, waits for them, and re-layouts  9.32 us (4%)
    all_to_all x2, waiting for transfers between devices, exchange(): lax.all_to_all(block, 'wide', split_axis=0, concat_axis=0, tiled=True)  89.8 us
    ppermute x15, waiting for transfers between devices, swap(): lax.ppermute(block, 'wide', [(i, i ^ mask) for i in range(peer_count)])  55 us
    all_to_all x2, starting transfers between devices, exchange(): lax.all_to_all(block, 'wide', split_axis=0, concat_axis=0, tiled=True)  12.8 us
    pallas_call x1, Pallas kernels, share_results(): pl.pallas_call(share_kernel, grid=(peer_count // STEP,), in_specs=[pl.Blo...  11 us
    pallas_call x1, Pallas kernels, low_out(): pl.pallas_call(low_out_kernel, grid=(peer_count // STEP,), in_specs=[pl.B...  10.7 us
    ppermute x15, starting transfers between devices, swap(): lax.ppermute(block, 'wide', [(i, i ^ mask) for i in range(peer_count)])  10.4 us
    pallas_call x1, Pallas kernels, pack_columns(): pl.pallas_call(pack_kernel, grid=(peer_count // 2,), in_specs=[pl.BlockSp...  6.1 us
    unnamed x14, local copies, waits for them, and re-layouts  5.86 us
  transfers between devices with their start and end apart: 17, of which 9 were waited for; matrix products, arithmetic and copies ran while one was open for 2% of the time, Pallas kernels for 9%

profile of v6, /device:TPU:11, one launch (start us, length us, event | category | flops | bytes accessed | tf_op | source)
XLA Modules:
  0.0 213.5 jit_solution(11136370275349272474)
XLA Ops:
  0.6 2.0 shard_map.94
  2.7 1.3 collective-permute-start
  4.0 2.2 %collective-permute-start.3 = (bf16[208,1024]{1,0:T(8,128)(2,1)}, bf16[208,1024]{1,0:T(8,128)(2,1)S(1)}, u32[]{:S(2)}, u32[]{:S(2)}) collective-permute-start(bf16[208,1024]{1,0:T(8,128)(2,1)} %shard_map.94), channel_id=1, source_target_pairs={{0,4},{1,5},{2,6},{3,7},{4,0},{5,1},{6,2},{7,3},{8,12},{9,13},{10,... | collective-permute-start | bytes 1277960 | tf_op jit(solution)/shard_map/ppermute | solution.py:439
  6.2 0.3 collective-permute-start.1
  6.4 6.1 %shard_map.95 = bf16[16,192,512]{2,1,0:T(8,128)(2,1)} custom-call(bf16[128,8192]{1,0:T(8,128)(2,1)} %features_ref.1, bf16[64,8192]{1,0:T(8,128)(2,1)} %bitcast.42), custom_call_target="tpu_custom_call" | custom-call | bytes 6291456 | tf_op jit(solution)/shard_map/pallas_call | solution.py:164
  12.5 10.3 %collective-permute-done = bf16[208,1024]{1,0:T(8,128)(2,1)S(1)} collective-permute-done((bf16[208,1024]{1,0:T(8,128)(2,1)}, bf16[208,1024]{1,0:T(8,128)(2,1)S(1)}, u32[]{:S(2)}, u32[]{:S(2)}) %collective-permute-start) | collective-permute-done | bytes 426016 | tf_op jit(solution)/shard_map/ppermute | solution.py:439
  22.8 0.0 collective-permute-start.2
  22.8 2.0 collective-permute-done.3
  24.8 0.3 collective-permute-start.4
  25.1 0.0 collective-permute-done.1
  25.1 0.0 copy-done.3
  25.1 8.5 %collective-permute-done.2 = bf16[208,1024]{1,0:T(8,128)(2,1)} collective-permute-done((bf16[208,1024]{1,0:T(8,128)(2,1)S(1)}, bf16[208,1024]{1,0:T(8,128)(2,1)}, u32[]{:S(2)}, u32[]{:S(2)}) %collective-permute-start.2) | collective-permute-done | bytes 426016 | tf_op jit(solution)/shard_map/ppermute | solution.py:439
  33.6 0.8 collective-permute-done.4
  34.4 7.9 %all-to-all-start = ((bf16[16,192,512]{2,1,0:T(8,128)(2,1)}), bf16[16,192,512]{2,1,0:T(8,128)(2,1)}, u32[]{:S(2)}, u32[]{:S(2)}) async-start(bf16[16,192,512]{2,1,0:T(8,128)(2,1)} %shard_map.95), calls=%async_computation | async-start | bytes 6291456 | tf_op jit(solution)/shard_map/all_to_all | solution.py:457
  42.3 0.4 collective-permute-start.5
  42.8 0.9 broadcast_in_dim.60
  43.7 0.1 copy-done.4
  43.8 0.1 collective-permute-start.6
  43.9 0.3 collective-permute-start.11
  44.2 0.0 copy-done.6
  44.2 0.6 collective-permute-start.7
  44.8 0.0 collective-permute-start.9
  44.9 1.0 bitcast_dynamic-update-slice_fusion.12
  46.1 0.0 collective-permute-done.5
  46.1 0.6 collective-permute-start.8
  46.7 1.0 bitcast_dynamic-update-slice_fusion.9
  47.7 0.0 collective-permute-done.6
  47.7 1.3 collective-permute-start.12
  49.0 0.0 collective-permute-done.7
  49.0 0.4 collective-permute-start.10
  49.4 20.2 %collective-permute-done.11 = bf16[208,1024]{1,0:T(8,128)(2,1)S(1)} collective-permute-done((bf16[208,1024]{1,0:T(8,128)(2,1)S(1)}, bf16[208,1024]{1,0:T(8,128)(2,1)S(1)}, u32[]{:S(2)}, u32[]{:S(2)}) %collective-permute-start.11) | collective-permute-done | bytes 426016 | tf_op jit(solution)/shard_map/ppermute | solution.py:439
  69.6 1.3 collective-permute-start.13
  70.9 12.1 %collective-permute-done.12 = bf16[208,1024]{1,0:T(8,128)(2,1)S(1)} collective-permute-done((bf16[208,1024]{1,0:T(8,128)(2,1)}, bf16[208,1024]{1,0:T(8,128)(2,1)S(1)}, u32[]{:S(2)}, u32[]{:S(2)}) %collective-permute-start.12) | collective-permute-done | bytes 426016 | tf_op jit(solution)/shard_map/ppermute | solution.py:439
  83.1 1.3 collective-permute-start.14
  84.4 0.0 collective-permute-done.8
  84.4 0.0 collective-permute-done.9
  84.5 0.0 collective-permute-done.10
  84.7 0.0 collective-permute-done.13
  84.7 1.1 collective-permute-done.14
  85.9 2.8 %copy-done = bf16[16,208,1024]{2,1,0:T(8,128)(2,1)} copy-done((bf16[16,208,1024]{2,1,0:T(8,128)(2,1)}, bf16[16,208,1024]{2,1,0:T(8,128)(2,1)S(1)}, u32[]{:S(2)}) %copy-start) | copy-done | bytes 6815768
  88.7 10.7 %shard_map.96 = (bf16[2048,128]{1,0:T(8,128)(2,1)}, f32[2048,512]{1,0:T(8,128)}, bf16[16,256,128]{2,1,0:T(8,128)(2,1)}) custom-call(bf16[16,208,1024]{2,1,0:T(8,128)(2,1)} %copy-done, bf16[16,208,1024]{2,1,0:T(8,128)(2,1)} %copy-done, bf16[16,208,1024]{2,1,0:T(8,128)(2,1)} %copy-done, bf16[512,1024]{1,0:T(8,128)(2,1)} %weight_ref.1), custom_call_target="tpu_custom_call" | custom-call | flops 7516192768 | bytes 16777216 | tf_op jit(solution)/shard_map/pallas_call | solution.py:207
  99.4 13.1 %all-to-all-done.feat_ref.down_ref = bf16[16,192,512]{2,1,0:T(8,128)(2,1)} async-done(((bf16[16,192,512]{2,1,0:T(8,128)(2,1)}), bf16[16,192,512]{2,1,0:T(8,128)(2,1)}, u32[]{:S(2)}, u32[]{:S(2)}) %all-to-all-start) | async-done | bytes 3145760 | tf_op jit(solution)/shard_map/all_to_all | solution.py:457
  112.5 11.0 %shard_map.97 = bf16[16,224,512]{2,1,0:T(8,128)(2,1)} custom-call(bf16[16,192,512]{2,1,0:T(8,128)(2,1)} %all-to-all-done.feat_ref.down_ref, bf16[16,192,512]{2,1,0:T(8,128)(2,1)} %all-to-all-done.feat_ref.down_ref, bf16[16,208,1024]{2,1,0:T(8,128)(2,1)} %copy-done, bf16[2048,128]{1,0:T(8,128)(2,1)} %get-tuple-element.27.low_ref, ...), custom_call_target="tpu_custom_call" | custom-call | flops 7516192768 | bytes 16777216 | tf_op jit(solution)/shard_map/pallas_call | solution.py:305
  123.5 4.8 %all-to-all-start.1 = ((bf16[16,224,512]{2,1,0:T(8,128)(2,1)}), bf16[16,224,512]{2,1,0:T(8,128)(2,1)}, u32[]{:S(2)}, u32[]{:S(2)}) async-start(bf16[16,224,512]{2,1,0:T(8,128)(2,1)} %shard_map.97), calls=%async_computation.1 | async-start | bytes 7340032 | tf_op jit(solution)/shard_map/all_to_all | solution.py:457
  128.4 2.9 %copy-done.1 = bf16[16,208,1024]{2,1,0:T(8,128)(2,1)S(1)} copy-done((bf16[16,208,1024]{2,1,0:T(8,128)(2,1)S(1)}, bf16[16,208,1024]{2,1,0:T(8,128)(2,1)}, u32[]{:S(2)}) %copy-start.1) | copy-done | bytes 6815768
  131.3 1.6 shard_map.98
  132.9 76.7 %all-to-all-done.1.part_ref = bf16[16,224,512]{2,1,0:T(8,128)(2,1)} async-done(((bf16[16,224,512]{2,1,0:T(8,128)(2,1)}), bf16[16,224,512]{2,1,0:T(8,128)(2,1)}, u32[]{:S(2)}, u32[]{:S(2)}) %all-to-all-start.1) | async-done | bytes 3670048 | tf_op jit(solution)/shard_map/all_to_all | solution.py:457
  209.6 3.9 %shard_map.99 = (bf16[128,8192]{1,0:T(8,128)(2,1)}, f32[64,8192]{1,0:T(8,128)}, f32[64,1024]{1,0:T(8,128)}) custom-call(bf16[16,224,512]{2,1,0:T(8,128)(2,1)} %all-to-all-done.1.part_ref, bf16[256,1024]{1,0:T(8,128)(2,1)S(1)} %get-tuple-element.30.cot_ref, f32[1,128]{1,0:T(1,128)S(1)} %get-tuple-element.31.scale_ref), custom_call_target="tpu_custom_call" | custom-call | flops 134217728 | bytes 8388608 | tf_op jit(solution)/shard_map/pallas_call | solution.py:413
  (23 shorter events, 0.5 us)
Async XLA Ops:
  2.7 39.7 %copy-start.2 = (bf16[208,1024]{1,0:T(8,128)(2,1)S(1)}, bf16[208,1024]{1,0:T(8,128)(2,1)}, u32[]{:S(2)}) copy-start(bf16[208,1024]{1,0:T(8,128)(2,1)} %shard_map.94) | copy-start | bytes 1277956
  2.7 20.1 %collective-permute-start = (bf16[208,1024]{1,0:T(8,128)(2,1)}, bf16[208,1024]{1,0:T(8,128)(2,1)S(1)}, u32[]{:S(2)}, u32[]{:S(2)}) collective-permute-start(bf16[208,1024]{1,0:T(8,128)(2,1)} %shard_map.94), channel_id=1, source_target_pairs={{0,12},{1,13},{2,14},{3,15},{4,8},{5,9},{6,10},{7,11},{8,4},{9,5},... | collective-permute-start | bytes 1277960 | tf_op jit(solution)/shard_map/ppermute | solution.py:439
  4.0 20.8 %collective-permute-start.3 = (bf16[208,1024]{1,0:T(8,128)(2,1)}, bf16[208,1024]{1,0:T(8,128)(2,1)S(1)}, u32[]{:S(2)}, u32[]{:S(2)}) collective-permute-start(bf16[208,1024]{1,0:T(8,128)(2,1)} %shard_map.94), channel_id=1, source_target_pairs={{0,4},{1,5},{2,6},{3,7},{4,0},{5,1},{6,2},{7,3},{8,12},{9,13},{10,... | collective-permute-start | bytes 1277960 | tf_op jit(solution)/shard_map/ppermute | solution.py:439
  6.2 18.9 %collective-permute-start.1 = (bf16[208,1024]{1,0:T(8,128)(2,1)}, bf16[208,1024]{1,0:T(8,128)(2,1)S(1)}, u32[]{:S(2)}, u32[]{:S(2)}) collective-permute-start(bf16[208,1024]{1,0:T(8,128)(2,1)} %shard_map.94), channel_id=1, source_target_pairs={{0,2},{1,3},{2,0},{3,1},{4,6},{5,7},{6,4},{7,5},{8,10},{9,11},{10,... | collective-permute-start | bytes 1277960 | tf_op jit(solution)/shard_map/ppermute | solution.py:439
  22.8 2.3 %copy-start.3 = (bf16[208,1024]{1,0:T(8,128)(2,1)}, bf16[208,1024]{1,0:T(8,128)(2,1)S(1)}, u32[]{:S(2)}) copy-start(bf16[208,1024]{1,0:T(8,128)(2,1)S(1)} %collective-permute-done) | copy-start | bytes 1277956
  22.8 10.8 %collective-permute-start.2 = (bf16[208,1024]{1,0:T(8,128)(2,1)S(1)}, bf16[208,1024]{1,0:T(8,128)(2,1)}, u32[]{:S(2)}, u32[]{:S(2)}) collective-permute-start(bf16[208,1024]{1,0:T(8,128)(2,1)S(1)} %collective-permute-done), channel_id=1, source_target_pairs={{0,4},{1,5},{2,6},{3,7},{4,0},{5,1},{6,2},{7,3},{8,12},{9,13},{10,... | collective-permute-start | bytes 1277960 | tf_op jit(solution)/shard_map/ppermute | solution.py:439
  24.8 8.8 %copy-start.5 = (bf16[208,1024]{1,0:T(8,128)(2,1)}, bf16[208,1024]{1,0:T(8,128)(2,1)S(1)}, u32[]{:S(2)}) copy-start(bf16[208,1024]{1,0:T(8,128)(2,1)S(1)} %collective-permute-done.3) | copy-start | bytes 1277956
  24.8 9.6 %collective-permute-start.4 = (bf16[208,1024]{1,0:T(8,128)(2,1)S(1)}, bf16[208,1024]{1,0:T(8,128)(2,1)S(1)}, u32[]{:S(2)}, u32[]{:S(2)}) collective-permute-start(bf16[208,1024]{1,0:T(8,128)(2,1)S(1)} %collective-permute-done.3), channel_id=1, source_target_pairs={{0,2},{1,3},{2,0},{3,1},{4,6},{5,7},{6,4},{7,5},{8,10},{9,11},{10,... | collective-permute-start | bytes 1277960 | tf_op jit(solution)/shard_map/ppermute | solution.py:439
  34.4 78.1 %all-to-all-start = ((bf16[16,192,512]{2,1,0:T(8,128)(2,1)}), bf16[16,192,512]{2,1,0:T(8,128)(2,1)}, u32[]{:S(2)}, u32[]{:S(2)}) async-start(bf16[16,192,512]{2,1,0:T(8,128)(2,1)} %shard_map.95), calls=%async_computation | async-start | bytes 6291456 | tf_op jit(solution)/shard_map/all_to_all | solution.py:457
  42.3 3.7 %collective-permute-start.5 = (bf16[208,1024]{1,0:T(8,128)(2,1)S(1)}, bf16[208,1024]{1,0:T(8,128)(2,1)}, u32[]{:S(2)}, u32[]{:S(2)}) collective-permute-start(bf16[208,1024]{1,0:T(8,128)(2,1)S(1)} %copy-done.2), channel_id=1, source_target_pairs={{0,1},{1,0},{2,3},{3,2},{4,5},{5,4},{6,7},{7,6},{8,9},{9,8},{10,11... | collective-permute-start | bytes 1277960 | tf_op jit(solution)/shard_map/ppermute | solution.py:439
  42.8 1.0 copy-start.4
  42.8 1.4 copy-start.6
  43.8 3.9 %collective-permute-start.6 = (bf16[208,1024]{1,0:T(8,128)(2,1)S(1)}, bf16[208,1024]{1,0:T(8,128)(2,1)S(1)}, u32[]{:S(2)}, u32[]{:S(2)}) collective-permute-start(bf16[208,1024]{1,0:T(8,128)(2,1)S(1)} %copy-done.4), channel_id=1, source_target_pairs={{0,1},{1,0},{2,3},{3,2},{4,5},{5,4},{6,7},{7,6},{8,9},{9,8},{10,11... | collective-permute-start | bytes 1277960 | tf_op jit(solution)/shard_map/ppermute | solution.py:439
  43.9 25.6 %collective-permute-start.11 = (bf16[208,1024]{1,0:T(8,128)(2,1)S(1)}, bf16[208,1024]{1,0:T(8,128)(2,1)S(1)}, u32[]{:S(2)}, u32[]{:S(2)}) collective-permute-start(bf16[208,1024]{1,0:T(8,128)(2,1)S(1)} %copy-done.4), channel_id=1, source_target_pairs={{0,2},{1,3},{2,0},{3,1},{4,6},{5,7},{6,4},{7,5},{8,10},{9,11},{10,... | collective-permute-start | bytes 1277960 | tf_op jit(solution)/shard_map/ppermute | solution.py:439
  44.2 4.8 %collective-permute-start.7 = (bf16[208,1024]{1,0:T(8,128)(2,1)S(1)}, bf16[208,1024]{1,0:T(8,128)(2,1)S(1)}, u32[]{:S(2)}, u32[]{:S(2)}) collective-permute-start(bf16[208,1024]{1,0:T(8,128)(2,1)S(1)} %copy-done.6), channel_id=1, source_target_pairs={{0,1},{1,0},{2,3},{3,2},{4,5},{5,4},{6,7},{7,6},{8,9},{9,8},{10,11... | collective-permute-start | bytes 1277960 | tf_op jit(solution)/shard_map/ppermute | solution.py:439
  44.8 39.6 %collective-permute-start.9 = (bf16[208,1024]{1,0:T(8,128)(2,1)S(1)}, bf16[208,1024]{1,0:T(8,128)(2,1)S(1)}, u32[]{:S(2)}, u32[]{:S(2)}) collective-permute-start(bf16[208,1024]{1,0:T(8,128)(2,1)S(1)} %collective-permute-done.1), channel_id=1, source_target_pairs={{0,1},{1,0},{2,3},{3,2},{4,5},{5,4},{6,7},{7,6},{8,9},{9,8},{10,11... | collective-permute-start | bytes 1277960 | tf_op jit(solution)/shard_map/ppermute | solution.py:439
  46.1 38.3 %collective-permute-start.8 = (bf16[208,1024]{1,0:T(8,128)(2,1)}, bf16[208,1024]{1,0:T(8,128)(2,1)S(1)}, u32[]{:S(2)}, u32[]{:S(2)}) collective-permute-start(bf16[208,1024]{1,0:T(8,128)(2,1)} %collective-permute-done.2), channel_id=1, source_target_pairs={{0,1},{1,0},{2,3},{3,2},{4,5},{5,4},{6,7},{7,6},{8,9},{9,8},{10,11... | collective-permute-start | bytes 1277960 | tf_op jit(solution)/shard_map/ppermute | solution.py:439
  47.7 35.4 %collective-permute-start.12 = (bf16[208,1024]{1,0:T(8,128)(2,1)}, bf16[208,1024]{1,0:T(8,128)(2,1)S(1)}, u32[]{:S(2)}, u32[]{:S(2)}) collective-permute-start(bf16[208,1024]{1,0:T(8,128)(2,1)} %collective-permute-done.2), channel_id=1, source_target_pairs={{0,2},{1,3},{2,0},{3,1},{4,6},{5,7},{6,4},{7,5},{8,10},{9,11},{10,... | collective-permute-start | bytes 1277960 | tf_op jit(solution)/shard_map/ppermute | solution.py:439
  49.0 35.5 %collective-permute-start.10 = (bf16[208,1024]{1,0:T(8,128)(2,1)S(1)}, bf16[208,1024]{1,0:T(8,128)(2,1)S(1)}, u32[]{:S(2)}, u32[]{:S(2)}) collective-permute-start(bf16[208,1024]{1,0:T(8,128)(2,1)S(1)} %collective-permute-done.4), channel_id=1, source_target_pairs={{0,1},{1,0},{2,3},{3,2},{4,5},{5,4},{6,7},{7,6},{8,9},{9,8},{10,11... | collective-permute-start | bytes 1277960 | tf_op jit(solution)/shard_map/ppermute | solution.py:439
  69.6 15.1 %collective-permute-start.13 = (bf16[208,1024]{1,0:T(8,128)(2,1)S(1)}, bf16[208,1024]{1,0:T(8,128)(2,1)S(1)}, u32[]{:S(2)}, u32[]{:S(2)}) collective-permute-start(bf16[208,1024]{1,0:T(8,128)(2,1)S(1)} %collective-permute-done.11), channel_id=1, source_target_pairs={{0,1},{1,0},{2,3},{3,2},{4,5},{5,4},{6,7},{7,6},{8,9},{9,8},{10,11... | collective-permute-start | bytes 1277960 | tf_op jit(solution)/shard_map/ppermute | solution.py:439
  83.1 2.7 %collective-permute-start.14 = (bf16[208,1024]{1,0:T(8,128)(2,1)S(1)}, bf16[208,1024]{1,0:T(8,128)(2,1)S(1)}, u32[]{:S(2)}, u32[]{:S(2)}) collective-permute-start(bf16[208,1024]{1,0:T(8,128)(2,1)S(1)} %collective-permute-done.12), channel_id=1, source_target_pairs={{0,1},{1,0},{2,3},{3,2},{4,5},{5,4},{6,7},{7,6},{8,9},{9,8},{10,11... | collective-permute-start | bytes 1277960 | tf_op jit(solution)/shard_map/ppermute | solution.py:439
  85.8 2.8 %copy-start = (bf16[16,208,1024]{2,1,0:T(8,128)(2,1)}, bf16[16,208,1024]{2,1,0:T(8,128)(2,1)S(1)}, u32[]{:S(2)}) copy-start(bf16[16,208,1024]{2,1,0:T(8,128)(2,1)S(1)} %bitcast_dynamic-update-slice_fusion.cot_ref.up_ref.place_ref) | copy-start | bytes 20447236
  123.5 86.1 %all-to-all-start.1 = ((bf16[16,224,512]{2,1,0:T(8,128)(2,1)}), bf16[16,224,512]{2,1,0:T(8,128)(2,1)}, u32[]{:S(2)}, u32[]{:S(2)}) async-start(bf16[16,224,512]{2,1,0:T(8,128)(2,1)} %shard_map.97), calls=%async_computation.1 | async-start | bytes 7340032 | tf_op jit(solution)/shard_map/all_to_all | solution.py:457
  128.4 2.9 %copy-start.1 = (bf16[16,208,1024]{2,1,0:T(8,128)(2,1)S(1)}, bf16[16,208,1024]{2,1,0:T(8,128)(2,1)}, u32[]{:S(2)}) copy-start(bf16[16,208,1024]{2,1,0:T(8,128)(2,1)} %copy-done) | copy-start | bytes 20447236
